TPU v7x, 32 devices: a whole 2x2x4 slice. The times are simulated.
32 devices in a mesh: freq: 2 (over x), gz: 16 (over z, y, core).
Axes of the slice: x: 2, y: 2, z: 4, core: 2. Of those that a mesh axis runs over, the one named last changes fastest.
Arguments:
- initial_guess: float32 [128, 2, 8, 32, 128], P(('freq', 'gz')), parts along dimension 0
- velocity_class: int32 [64, 32, 128], P('gz'), may hold values from 0 to 15
- layer_code: int32 [64, 32, 128], P('gz'), may hold values from 0 to 7
- wavenumber: float32 [32], P('freq'), parts along dimension 0, may hold values from 0.5 to 3
- damping: float32 [8], replicated, may hold values from 0.05 to 1
- shot_cells: int32 [8, 3], replicated, may hold values from 0 to 127, as said below
- wavelet: float32 [4, 8], P('freq'), parts along dimension 0, may hold values from -12 to 12
Outputs:
- basis_two: float32 [128, 2, 8, 32, 128], P(('freq', 'gz')), parts along dimension 0
- hessenberg: float32 [4, 24, 16], P('freq'), parts along dimension 0
There are 2 independent parts, one for each index of `freq`. A program takes and returns all parts, laid end to end along the dimension named above; an argument that names none is the same for every part. Nothing has to cross between parts.
Inputs may be any that keep to these rules, and one draw needn't show every extreme that they name: `shot_cells`: row s holds shot s's depth cell below 64, first lateral cell below 32 and second lateral cell below 128; over all shots some depth cell is 63, some first lateral cell 32 - 1, some second lateral cell 128 - 1, and some depth cell 0.
All inputs are finite; a program needn't handle non-finite values.
Results may differ from a plain program's by a relative error of at most 0.0003.
Values sent between devices are 32-bit elements; how exact they have to be, the bound alone decides.
No kernel may reach another device: no remote copies, remote signals or barrier semaphores. Data moves between devices by JAX's collectives and lax.ppermute only.
A program may use at most 64 MiB of HBM per device.

v0:
```python
import functools

import jax
import jax.numpy as jnp
from jax import lax
from jax.experimental import pallas as pl
from jax.experimental.pallas import tpu as pltpu
from jax.sharding import PartitionSpec as P

SHIFT_BASE = 2.9
BLOCKS = 3
REACH = 3
VMEM_BYTES = 24 * 1024 * 1024
PAIRS = ((0, 0), (0, 1), (0, 2), (1, 1), (1, 2), (2, 2))


def shift_of(wave_ref, damp_ref):
    classes, levels = wave_ref.shape[0], damp_ref.shape[0]
    wave_mean = sum(wave_ref[i] for i in range(classes)) * (1.0 / classes)
    damp_mean = sum(damp_ref[i] for i in range(levels)) * (1.0 / levels)
    return SHIFT_BASE - wave_mean, -wave_mean * damp_mean


def edge_masks(shots, lanes):
    lane = lax.broadcasted_iota(jnp.int32, (shots, lanes), 1)
    return (
        jnp.where(lane == 0, 0.0, 1.0).astype(jnp.float32),
        jnp.where(lane == lanes - 1, 0.0, 1.0).astype(jnp.float32),
    )


def stencil_plane(sources, target, table, scale, keep):
    (low, low_plane), (mid, mid_plane), (high, high_plane) = sources
    out, out_plane = target
    table_ref, table_plane, kind = table
    width = table_ref.shape[2]
    left, right = keep

    def load(column):
        center, away = [], []
        for part in range(2):
            v = mid[mid_plane, column, part]
            d = low[low_plane, column, part] + high[high_plane, column, part]
            center.append(v)
            away.append(d + 3.0 * v)
        return center, away

    here_v, here_u = load(0)
    before_v = [jnp.zeros_like(v) for v in here_v]
    before_u = before_v
    for column in range(width):
        if column + 1 < width:
            after_v, after_u = load(column + 1)
        else:
            after_v = [jnp.zeros_like(v) for v in here_v]
            after_u = after_v
        real_row, imag_row = [
            jnp.broadcast_to(table_ref[table_plane, 2 * kind + part, column : column + 1, :], here_v[0].shape)
            for part in range(2)
        ]
        for part in range(2):
            near = here_u[part] + (before_v[part] + after_v[part])
            wide = (before_u[part] + after_u[part]) + (3.0 * here_u[part] + 5.0 * here_v[part])
            sides = pltpu.roll(wide, 1, 1) * left + pltpu.roll(wide, 127, 1) * right
            total = 3.0 * wide + 5.0 * near + sides
            if part == 0:
                own = real_row * here_v[0] + imag_row * here_v[1]
            else:
                own = real_row * here_v[1] - imag_row * here_v[0]
            out[out_plane, column, part] = own - scale * total
        before_v, before_u, here_v, here_u = here_v, here_u, after_v, after_u


def bring(rows, first_row, field, plane):
    width, parts, shots = field.shape[1:4]
    for column in range(width):
        for part in range(parts):
            field[plane, column, part] = rows[
                pl.ds(first_row + part * shots * width + column, shots, stride=width), :
            ]


def fill_tables(tables, plane, labels, codes, inside_flag, wave_ref, damp_ref):
    shift_real, shift_imag = shift_of(wave_ref, damp_ref)
    wave = jnp.zeros(labels.shape, jnp.float32)
    for i in range(wave_ref.shape[0]):
        wave = jnp.where(labels == float(i), wave_ref[i], wave)
    loss = jnp.zeros(labels.shape, jnp.float32)
    for i in range(damp_ref.shape[0]):
        loss = jnp.where(codes == float(i), damp_ref[i], loss)
    real = 185.0 / 30.0 - wave
    imag = wave * loss
    tables[plane, 0] = -inside_flag * real
    tables[plane, 1] = -inside_flag * imag
    tables[plane, 2] = inside_flag * (real - shift_real)
    tables[plane, 3] = inside_flag * (imag + shift_imag)


def add_sources(start, first_start, place_of, cells_ref, wavelet_ref):
    count, _, _, shots, lanes = start.shape
    lane_row = lax.broadcasted_iota(jnp.int32, (1, lanes), 1)
    for s in range(shots):
        place = place_of(cells_ref[0, s]) - first_start

        @pl.when((place >= 0) & (place < count))
        def _():
            column = cells_ref[1, s]
            hit = lane_row == cells_ref[2, s]
            for part in range(2):
                start[place, column, part, s : s + 1, :] += jnp.where(hit, wavelet_ref[part, s], 0.0)


def split_plane(sources, split_ref, spot_plane):
    width, _, shots, lanes = sources[0][0].shape[1:]
    rows = BLOCKS * 2 * shots
    for column in range(width):
        pieces = [ref[plane, column, part] for part in range(2) for ref, plane in sources]
        begin = (spot_plane * width + column) * lanes
        for pair in range(BLOCKS):
            value = jnp.concatenate(pieces[2 * pair : 2 * pair + 2], axis=0)
            for part in range(3):
                short = value.astype(jnp.bfloat16)
                row = part * rows + 2 * shots * pair
                split_ref[row : row + 2 * shots, begin : begin + lanes] = short
                if part < 2:
                    value = value - short.astype(jnp.float32)


def products_of(split_ref, spot_plane, span):
    chunk = split_ref[:, spot_plane * span : (spot_plane + 1) * span]
    return lax.dot_general(
        chunk, chunk, (((1,), (1,)), ((), ())), preferred_element_type=jnp.float32
    )


def pack_kernel(index_ref, guess_ref, codes_ref, far_ref, near_ref, sems):
    layers, parts, shots, width, lanes = guess_ref.shape
    fields = parts * shots
    odd = lax.rem(index_ref[0], 2) == 1
    planes = guess_ref.reshape(layers * fields, width, lanes)
    codes = codes_ref.reshape(2 * layers, width, lanes)
    far_begin = jnp.where(odd, layers - 2, 0) * fields
    far_code = jnp.where(odd, layers - 1, 0)
    near_begin = jnp.where(odd, 0, layers - REACH) * fields
    near_code = jnp.where(odd, 0, layers - 2)
    copies = []
    for number, (source, target) in enumerate(
        (
            (planes.at[pl.ds(far_begin, 2 * fields)], far_ref.at[pl.ds(0, 2 * fields)]),
            (codes.at[pl.ds(far_code, 1)], far_ref.at[pl.ds(2 * fields, 1)]),
            (codes.at[pl.ds(far_code + layers, 1)], far_ref.at[pl.ds(2 * fields + 1, 1)]),
            (planes.at[pl.ds(near_begin, REACH * fields)], near_ref.at[pl.ds(0, REACH * fields)]),
            (codes.at[pl.ds(near_code, 2)], near_ref.at[pl.ds(REACH * fields, 2)]),
            (codes.at[pl.ds(near_code + layers, 2)], near_ref.at[pl.ds(REACH * fields + 2, 2)]),
        )
    ):
        copies.append(pltpu.make_async_copy(source, target, sems.at[number]))
        copies[-1].start()
    for copy in copies:
        copy.wait()


def orientation(index_ref, layers, depth_total):
    index = index_ref[0]
    odd = lax.rem(index, 2) == 1
    first_plane = index * layers

    def place_of(plane):
        local = plane - first_plane
        return jnp.where(odd, local, layers - 1 - local)

    def inside(place):
        plane = first_plane + jnp.where(odd, place, layers - 1 - place)
        return jnp.where((plane >= 0) & (plane < depth_total), 1.0, 0.0).astype(jnp.float32)

    return odd, place_of, inside


def early_kernel(
    depth_total,
    index_ref,
    wave_ref,
    damp_ref,
    cells_ref,
    wavelet_ref,
    guess_ref,
    near_ref,
    codes_ref,
    field,
    start,
    first,
    second,
    tables,
    split_ref,
    products_ref,
    send_ref,
):
    layers, parts, shots, width, lanes = guess_ref.shape
    fields = parts * shots
    odd, place_of, inside = orientation(index_ref, layers, depth_total)
    guess_rows = guess_ref.reshape(layers * fields * width, lanes)
    near_rows = near_ref.reshape(near_ref.shape[0] * width, lanes)
    span = fields * width
    keep = edge_masks(shots, lanes)

    far_plane = jnp.where(odd, layers - REACH, REACH - 1)
    far_code = jnp.where(odd, layers - 2, 1)
    for part in range(parts):
        send_ref[part * shots : (part + 1) * shots] = guess_ref[far_plane, part]
    send_ref[fields] = codes_ref[0, far_code]
    send_ref[fields + 1] = codes_ref[1, far_code]

    extra = REACH * fields
    for k in range(2):
        pick = jnp.where(odd, k, 1 - k)
        fill_tables(
            tables, k, near_ref[extra + pick], near_ref[extra + 2 + pick], inside(k - 2), wave_ref, damp_ref
        )
    for q in range(layers):
        pick = jnp.where(odd, q, layers - 1 - q)
        fill_tables(
            tables, q + 2, codes_ref[0, pick], codes_ref[1, pick], jnp.float32(1.0), wave_ref, damp_ref
        )

    def bring_near(k, carry):
        bring(near_rows, jnp.where(odd, k, REACH - 1 - k) * span, field, k)
        return carry

    def bring_own(q, carry):
        bring(guess_rows, jnp.where(odd, q, layers - 1 - q) * span, field, q + REACH)
        return carry

    lax.fori_loop(0, REACH, bring_near, 0)
    lax.fori_loop(0, layers, bring_own, 0)

    def start_plane(i, carry):
        stencil_plane(
            ((field, i), (field, i + 1), (field, i + 2)),
            (start, i),
            (tables, i, 0),
            inside(i - 2) * (-1.0 / 30.0),
            keep,
        )
        return carry

    lax.fori_loop(0, layers + 1, start_plane, 0)
    add_sources(start, -2, place_of, cells_ref, wavelet_ref)

    def first_plane(j, carry):
        stencil_plane(
            ((start, j), (start, j + 1), (start, j + 2)),
            (first, j),
            (tables, j + 1, 1),
            inside(j - 1) * (1.0 / 30.0),
            keep,
        )
        return carry

    lax.fori_loop(0, layers - 1, first_plane, 0)
    products = jnp.zeros(products_ref.shape, jnp.float32)
    for k in range(layers - 3):
        stencil_plane(
            ((first, k), (first, k + 1), (first, k + 2)),
            (second, k),
            (tables, k + 2, 1),
            1.0 / 30.0,
            keep,
        )
        split_plane(((start, k + 2), (first, k + 1), (second, k)), split_ref, k)
        products += products_of(split_ref, k, width * lanes)
    products_ref[...] = products


def middle_kernel(
    depth_total,
    index_ref,
    wave_ref,
    damp_ref,
    cells_ref,
    wavelet_ref,
    far_ref,
    old_field,
    old_start,
    old_first,
    old_tables,
    old_products,
    field,
    start,
    first,
    second,
    tables,
    split_ref,
    products_ref,
):
    layers = old_field.shape[0] - REACH
    _, width, parts, shots, lanes = field.shape
    fields = parts * shots
    odd, place_of, inside = orientation(index_ref, layers, depth_total)
    far_rows = far_ref.reshape(far_ref.shape[0] * width, lanes)
    span = fields * width
    keep = edge_masks(shots, lanes)
    fill_tables(
        tables, 0, far_ref[2 * fields], far_ref[2 * fields + 1], inside(jnp.int32(layers)), wave_ref, damp_ref
    )
    for k in range(2):
        bring(far_rows, jnp.where(odd, k, 1 - k) * span, field, k)

    def at_field(place):
        return (old_field, place + REACH) if place < layers else (field, place - layers)

    def at_start(place):
        return (old_start, place + 2) if place < layers - 1 else (start, place - (layers - 1))

    def at_first(place):
        return (old_first, place + 1) if place < layers - 2 else (first, place - (layers - 2))

    def at_table(place, kind):
        return (old_tables, place + 2, kind) if place < layers else (tables, place - layers, kind)

    for place in range(layers - 1, layers + 1):
        stencil_plane(
            (at_field(place - 1), at_field(place), at_field(place + 1)),
            at_start(place),
            at_table(place, 0),
            inside(jnp.int32(place)) * (-1.0 / 30.0),
            keep,
        )
    add_sources(start, layers - 1, place_of, cells_ref, wavelet_ref)
    for place in range(layers - 2, layers):
        stencil_plane(
            (at_start(place - 1), at_start(place), at_start(place + 1)),
            at_first(place),
            at_table(place, 1),
            1.0 / 30.0,
            keep,
        )
    products = old_products[...]
    for k in range(2):
        place = layers - 3 + k
        stencil_plane(
            (at_first(place - 1), at_first(place), at_first(place + 1)),
            (second, k),
            at_table(place, 1),
            1.0 / 30.0,
            keep,
        )
        split_plane((at_start(place), at_first(place), (second, k)), split_ref, k)
        products += products_of(split_ref, k, width * lanes)
    products_ref[...] = products


def late_kernel(
    depth_total,
    layers,
    index_ref,
    wave_ref,
    damp_ref,
    cells_ref,
    wavelet_ref,
    last_ref,
    old_field,
    old_start,
    old_first,
    own_tables,
    far_tables,
    old_products,
    split_ref,
    gram_ref,
    field,
    start,
    first,
    second,
    tables,
):
    _, width, parts, shots, lanes = field.shape
    fields = parts * shots
    odd, place_of, inside = orientation(index_ref, layers, depth_total)
    last_rows = last_ref.reshape(last_ref.shape[0] * width, lanes)
    keep = edge_masks(shots, lanes)
    fill_tables(
        tables, 0, last_ref[fields], last_ref[fields + 1], inside(jnp.int32(layers + 1)), wave_ref, damp_ref
    )
    bring(last_rows, 0, field, 0)
    stencil_plane(
        ((old_field, 0), (old_field, 1), (field, 0)),
        (start, 0),
        (tables, 0, 0),
        inside(jnp.int32(layers + 1)) * (-1.0 / 30.0),
        keep,
    )
    add_sources(start, layers + 1, place_of, cells_ref, wavelet_ref)
    stencil_plane(
        ((old_start, 0), (old_start, 1), (start, 0)),
        (first, 0),
        (far_tables, 0, 1),
        inside(jnp.int32(layers)) * (1.0 / 30.0),
        keep,
    )
    stencil_plane(
        ((old_first, 0), (old_first, 1), (first, 0)),
        (second, 0),
        (own_tables, layers + 1, 1),
        1.0 / 30.0,
        keep,
    )
    split_plane(((old_start, 0), (old_first, 1), (second, 0)), split_ref, 0)
    products = old_products[...] + products_of(split_ref, 0, width * lanes)

    rows = BLOCKS * fields
    half = rows // 2
    cells = float(depth_total * width * lanes)
    summed = products[0:rows] + products[rows : 2 * rows] + products[2 * rows : 3 * rows]
    summed = summed[:, 0:rows] + summed[:, rows : 2 * rows] + summed[:, 2 * rows : 3 * rows]
    summed = summed * (1.0 / cells)
    real = summed[0:half, 0:half] + summed[half:rows, half:rows]
    imag = summed[0:half, half:rows] - summed[half:rows, 0:half]
    blocks = []
    for i, j in PAIRS:
        for values in (real, imag):
            blocks.append(values[i * shots : (i + 1) * shots, j * shots : (j + 1) * shots])
    blocks.append(jnp.zeros((shots, 128 - 2 * len(PAIRS) * shots), jnp.float32))
    packed = jnp.concatenate(blocks, axis=1)
    for copy in range(gram_ref.shape[0]):
        gram_ref[copy] = packed


def back_kernel(
    index_ref, wave_ref, damp_ref, grams_ref, early_ref, middle_ref, late_ref, basis_ref, hessenberg_ref
):
    layers, parts, shots, width, y = basis_ref.shape
    fields = parts * shots
    rows = BLOCKS * fields
    half = rows // 2
    tile = shots
    tiles = BLOCKS
    spread = BLOCKS * rows
    lanes = 128
    lead = spread - lanes

    grams = [grams_ref[i] for i in range(grams_ref.shape[0])]
    while len(grams) > 1:
        grams = [sum(grams[i : i + 2]) for i in range(0, len(grams), 2)]
    packed = grams[0]
    turned = packed.T
    lane = lax.broadcasted_iota(jnp.int32, (tile, lanes), 1)
    sub = lax.broadcasted_iota(jnp.int32, (tile, lanes), 0)
    wide_lane = lax.broadcasted_iota(jnp.int32, (tile, 2 * lanes), 1)
    wide_sub = lax.broadcasted_iota(jnp.int32, (tile, 2 * lanes), 0)
    real, imag = [], []
    for t in range(tiles):
        match = (wide_lane < spread) & (lax.rem(wide_lane, half) == wide_sub + t * tile)
        unit = jnp.where(match, 1.0, 0.0).astype(jnp.float32)
        blank = jnp.zeros((tile, lanes), jnp.float32)
        parts_of = []
        for part in range(2):
            blocks = [jnp.zeros((tile, lead), jnp.float32)]
            for j in range(tiles):
                if j >= t:
                    begin = (2 * PAIRS.index((t, j)) + part) * tile
                    blocks.append(packed[:, begin : begin + tile])
                else:
                    begin = (2 * PAIRS.index((j, t)) + part) * tile
                    block = turned[begin : begin + tile, 0:tile]
                    blocks.append(block if part == 0 else -block)
            blocks.append(jnp.zeros((tile, lanes - lead - half), jnp.float32))
            parts_of.append(jnp.concatenate(blocks, axis=1))
        real.append(unit + jnp.concatenate([blank, parts_of[0]], axis=1))
        imag.append(jnp.concatenate([blank, parts_of[1]], axis=1))
    pivots = []
    for k in range(half):
        owner, row = divmod(k, tile)
        row_real = real[owner][row : row + 1]
        row_imag = imag[owner][row : row + 1]
        spot = spread + k
        pivot = row_real[:, spot : spot + 1]
        pivots.append(pivot)
        inverse = 1.0 / pivot
        for t in range(owner, tiles):
            column_real = real[t][:, spot : spot + 1] * inverse
            column_imag = imag[t][:, spot : spot + 1] * inverse
            if t == owner:
                below = sub[:, 0:1] > row
                column_real = jnp.where(below, column_real, 0.0)
                column_imag = jnp.where(below, column_imag, 0.0)
            new_real = real[t] - (column_real * row_real - column_imag * row_imag)
            new_imag = imag[t] - (column_real * row_imag + column_imag * row_real)
            real[t], imag[t] = new_real, new_imag
    for t in range(tiles):
        scales = lax.rsqrt(jnp.concatenate(pivots[t * tile : (t + 1) * tile], axis=0))
        real[t] = real[t] * scales
        imag[t] = imag[t] * scales

    last_real, last_imag = real[tiles - 1], imag[tiles - 1]
    first_half = lax.rem(wide_lane, rows) < half
    mix = jnp.concatenate(
        [
            jnp.where(first_half, last_real, last_imag),
            jnp.where(first_half, -last_imag, last_real),
        ],
        axis=0,
    )
    pieces = []
    for part in range(3):
        short = mix.astype(jnp.bfloat16)
        pieces.append(short)
        mix = mix - short.astype(jnp.float32)
    left = jnp.concatenate(pieces, axis=0)[:, 0:spread]

    odd = lax.rem(index_ref[0], 2) == 1
    out_rows = basis_ref.reshape(layers * fields * width, y)
    spots = [
        (ref, spot)
        for ref in (early_ref, middle_ref, late_ref)
        for spot in range(ref.shape[1] // (width * y))
    ]
    group = 16
    for q in range(layers):
        source, spot = spots[q]
        plane = jnp.where(odd, q, layers - 1 - q)
        for begin in range(0, width, group):
            offset = (spot * width + begin) * y
            mixed = jnp.dot(
                left, source[:, offset : offset + group * y], preferred_element_type=jnp.float32
            )
            mixed = mixed[0:fields] + mixed[fields : 2 * fields] + mixed[2 * fields : 3 * fields]
            for column in range(group):
                out_rows[pl.ds(plane * (fields * width) + begin + column, fields, stride=width), :] = mixed[
                    :, column * y : (column + 1) * y
                ]

    wide = 2 * tile
    full_real = jnp.concatenate(real, axis=0)
    full_imag = jnp.concatenate(imag, axis=0)
    row_index = lax.broadcasted_iota(jnp.int32, (half, wide), 0)
    column_index = lax.broadcasted_iota(jnp.int32, (half, wide), 1)
    upper = row_index <= column_index + tile
    factor_real = jnp.where(upper, full_real[:, spread + tile : spread + half], 0.0)
    factor_imag = jnp.where(upper, full_imag[:, spread + tile : spread + half], 0.0)
    lower_real = full_real[0:wide, 0:wide]
    lower_imag = full_imag[0:wide, 0:wide]

    def times(left, right):
        return lax.dot_general(
            left,
            right,
            (((1,), (1,)), ((), ())),
            precision=lax.Precision.HIGHEST,
            preferred_element_type=jnp.float32,
        )

    shift_real, shift_imag = shift_of(wave_ref, damp_ref)
    diagonal = lax.broadcasted_iota(jnp.int32, (wide, half), 0) == lax.broadcasted_iota(
        jnp.int32, (wide, half), 1
    )
    hessenberg_ref[0] = (
        times(lower_real, factor_real)
        + times(lower_imag, factor_imag)
        + jnp.where(diagonal, shift_real, 0.0)
    )
    hessenberg_ref[1] = (
        times(lower_real, factor_imag)
        - times(lower_imag, factor_real)
        + jnp.where(diagonal, shift_imag, 0.0)
    )


def shards(initial_guess, velocity_class, layer_code, wavenumber, damping, shot_cells, wavelet):
    layers, parts, shots, width, lanes = initial_guess.shape
    devices = lax.axis_size("gz")
    fields = parts * shots
    rows = BLOCKS * fields
    span = width * lanes
    depth_total = devices * layers
    index = lax.axis_index("gz").astype(jnp.int32).reshape(1)
    shot_cells = shot_cells.T

    smem = pl.BlockSpec(memory_space=pltpu.SMEM)
    vmem = pl.BlockSpec(memory_space=pltpu.VMEM)
    hbm = pl.BlockSpec(memory_space=pl.ANY)
    params = pltpu.CompilerParams(vmem_limit_bytes=VMEM_BYTES)

    codes = jnp.stack([velocity_class, layer_code]).astype(jnp.float32)

    def float_shape(*dims):
        return jax.ShapeDtypeStruct(dims, jnp.float32)

    far, near = pl.pallas_call(
        pack_kernel,
        out_shape=(
            float_shape(2 * fields + 2, width, lanes),
            float_shape(REACH * fields + 4, width, lanes),
        ),
        in_specs=[smem, hbm, hbm],
        out_specs=(vmem, vmem),
        scratch_shapes=[pltpu.SemaphoreType.DMA((6,))],
        compiler_params=params,
        name="pack",
    )(index, initial_guess, codes)
    odd_to_even = [(i, i + 1) for i in range(1, devices - 1, 2)]
    even_to_odd = [(i, i + 1) for i in range(0, devices, 2)]
    far_pairs = odd_to_even + [(b, a) for a, b in odd_to_even]
    near_pairs = even_to_odd + [(b, a) for a, b in even_to_odd]
    far = lax.ppermute(far, "gz", far_pairs)
    near = lax.ppermute(near, "gz", near_pairs)

    def planes(count):
        return float_shape(count, width, parts, shots, lanes)

    def tables(count):
        return float_shape(count, 4, width, lanes)

    def split(count):
        return jax.ShapeDtypeStruct((BLOCKS * rows, count * span), jnp.bfloat16)

    def scratch(shape):
        return pltpu.VMEM(shape.shape, shape.dtype)

    products = float_shape(BLOCKS * rows, BLOCKS * rows)
    common = (index, wavenumber, damping, shot_cells, wavelet)
    field, start, first, _, own_tables, early_split, products_one, last = pl.pallas_call(
        functools.partial(early_kernel, depth_total),
        out_shape=(
            planes(layers + REACH),
            planes(layers + 1),
            planes(layers - 1),
            planes(layers - 3),
            tables(layers + 2),
            split(layers - 3),
            products,
            float_shape(fields + 2, width, lanes),
        ),
        in_specs=[smem] * 5 + [vmem] * 3,
        out_specs=(vmem,) * 8,
        compiler_params=params,
        cost_estimate=pl.CostEstimate(flops=10_000_000, bytes_accessed=16_000_000, transcendentals=0),
        name="early",
    )(*common, initial_guess, near, codes)
    last = lax.ppermute(last, "gz", far_pairs)
    field, start, first, _, far_tables, middle_split, products_two = pl.pallas_call(
        functools.partial(middle_kernel, depth_total),
        out_shape=(planes(2), planes(2), planes(2), planes(2), tables(1), split(2), products),
        in_specs=[smem] * 5 + [vmem] * 6,
        out_specs=(vmem,) * 7,
        compiler_params=params,
        cost_estimate=pl.CostEstimate(flops=8_000_000, bytes_accessed=12_000_000, transcendentals=0),
        name="middle",
    )(*common, far, field, start, first, own_tables, products_one)
    late_split, grams = pl.pallas_call(
        functools.partial(late_kernel, depth_total, layers),
        out_shape=(split(1), float_shape(devices, shots, 128)),
        in_specs=[smem] * 5 + [vmem] * 7,
        out_specs=(vmem, vmem),
        scratch_shapes=[scratch(planes(1))] * 4 + [scratch(tables(1))],
        compiler_params=params,
        name="late",
    )(*common, last, field, start, first, own_tables, far_tables, products_two)
    grams = lax.all_to_all(grams, "gz", 0, 0)
    basis_two, turned = pl.pallas_call(
        back_kernel,
        out_shape=(
            jax.ShapeDtypeStruct(initial_guess.shape, jnp.float32),
            jax.ShapeDtypeStruct((2, 2 * shots, BLOCKS * shots), jnp.float32),
        ),
        in_specs=[smem] * 3 + [vmem] * 4,
        out_specs=(vmem, vmem),
        compiler_params=params,
        name="back",
    )(index, wavenumber, damping, grams, early_split, middle_split, late_split)
    return basis_two, jnp.swapaxes(turned, 1, 2)


def solution(mesh):
    return jax.shard_map(
        shards,
        mesh=mesh,
        in_specs=(
            P(("freq", "gz"), None, None, None, None),
            P("gz", None, None),
            P("gz", None, None),
            P("freq"),
            P(),
            P(),
            P("freq", None),
        ),
        out_specs=(P(("freq", "gz"), None, None, None, None), P("freq", None, None)),
        check_vma=False,
    )
```

profile of v0, /device:TPU:0, one launch (start us, length us, event | category | flops | bytes accessed | tf_op | source)
XLA Modules:
  0.0 47.2 jit_solution(11612447997699550146)
XLA Ops:
  0.6 0.0 copy-start.4
  0.6 0.0 copy-start.3
  0.7 0.0 copy-start.2
  0.7 0.0 copy-start.1
  0.7 0.9 %add_convert_fusion.codes_ref = f32[2,4,32,128]{3,2,1,0:T(8,128)S(1)} fusion(s32[1,4,32,128]{3,2,1,0:T(8,128)} %bitcast.8, s32[1,4,32,128]{3,2,1,0:T(8,128)} %bitcast.9), kind=kLoop, calls=%fused_computation | loop fusion | flops 65536 | bytes 262144 | tf_op jit(solution)/shard_map/convert_element_type | solution.py:582
  1.6 0.0 copy-start
  1.6 1.2 %copy-done = f32[4,2,8,32,128]{4,3,2,1,0:T(8,128)S(1)} copy-done((f32[4,2,8,32,128]{4,3,2,1,0:T(8,128)S(1)}, f32[4,2,8,32,128]{4,3,2,1,0:T(8,128)}, u32[]{:S(2)}) %copy-start) | copy-done | bytes 1048600
  2.8 0.3 pack.1
  3.1 0.5 %collective-permute-start = (f32[52,32,128]{2,1,0:T(8,128)S(1)}, f32[52,32,128]{2,1,0:T(8,128)S(1)}, u32[]{:S(2)}, u32[]{:S(2)}) collective-permute-start(f32[52,32,128]{2,1,0:T(8,128)S(1)} %get-tuple-element.21), channel_id=1, source_target_pairs={{0,1},{2,3},{4,5},{6,7},{8,9},{10,11},{12,13},{14,15},{1,0},{3,2},... | collective-permute-start | bytes 2555912 | tf_op jit(solution)/shard_map/ppermute | solution.py:604
  3.6 0.7 %collective-permute-start.2 = (f32[34,32,128]{2,1,0:T(8,128)S(1)}, f32[34,32,128]{2,1,0:T(8,128)S(1)}, u32[]{:S(2)}, u32[]{:S(2)}) collective-permute-start(f32[34,32,128]{2,1,0:T(8,128)S(1)} %get-tuple-element.23), channel_id=1, source_target_pairs={{1,2},{3,4},{5,6},{7,8},{9,10},{11,12},{13,14},{2,1},{4,3},{6,5},{... | collective-permute-start | bytes 1671176 | tf_op jit(solution)/shard_map/ppermute | solution.py:603
  4.3 1.3 %collective-permute-done.near_ref = f32[52,32,128]{2,1,0:T(8,128)S(1)} collective-permute-done((f32[52,32,128]{2,1,0:T(8,128)S(1)}, f32[52,32,128]{2,1,0:T(8,128)S(1)}, u32[]{:S(2)}, u32[]{:S(2)}) %collective-permute-start) | collective-permute-done | bytes 852000 | tf_op jit(solution)/shard_map/ppermute | solution.py:604
  5.6 0.0 copy-done.4
  5.6 0.0 copy-done.3
  5.6 0.0 copy-done.2
  5.6 0.0 copy-done.1
  5.6 5.2 %early.1 = (f32[7,32,2,8,128]{4,3,2,1,0:T(8,128)S(1)}, f32[5,32,2,8,128]{4,3,2,1,0:T(8,128)S(1)}, f32[3,32,2,8,128]{4,3,2,1,0:T(8,128)S(1)}, f32[1,32,2,8,128]{4...) custom-call(s32[1]{0:T(128)} %bitcast.index_ref, ...), custom_call_target="tpu_custom_call" | custom-call | flops 10000000 | bytes 16000000 | tf_op jit(solution)/shard_map/early/pallas_call | solution.py:620
  10.9 0.7 %collective-permute-start.1 = (f32[18,32,128]{2,1,0:T(8,128)S(1)}, f32[18,32,128]{2,1,0:T(8,128)S(1)}, u32[]{:S(2)}, u32[]{:S(2)}) collective-permute-start(f32[18,32,128]{2,1,0:T(8,128)S(1)} %get-tuple-element.22), channel_id=1, source_target_pairs={{1,2},{3,4},{5,6},{7,8},{9,10},{11,12},{13,14},{2,1},{4,3},{6,5},{... | collective-permute-start | bytes 884744 | tf_op jit(solution)/shard_map/ppermute | solution.py:638
  11.5 0.0 collective-permute-done.2.far_ref
  11.5 4.0 %middle.1 = (f32[2,32,2,8,128]{4,3,2,1,0:T(8,128)S(1)}, f32[2,32,2,8,128]{4,3,2,1,0:T(8,128)S(1)}, f32[2,32,2,8,128]{4,3,2,1,0:T(8,128)S(1)}, f32[2,32,2,8,128]{...) custom-call(s32[1]{0:T(128)} %bitcast.index_ref, ...), custom_call_target="tpu_custom_call" | custom-call | flops 8000000 | bytes 12000000 | tf_op jit(solution)/shard_map/middle/pallas_call | solution.py:639
  15.6 0.0 collective-permute-done.1.last_ref
  15.6 2.3 %late.1 = (bf16[144,4096]{1,0:T(8,128)(2,1)S(1)}, f32[16,8,128]{2,1,0:T(8,128)S(1)}) custom-call(s32[1]{0:T(128)} %bitcast.index_ref, f32[16]{0:T(128)S(1)} %copy-done.3, f32[8]{0:T(128)S(1)} %copy-done.4, s32[3,8]{1,0:T(4,128)S(1)} %bitcast.7, f32[2,8]{1,0:T(2,128)S(1)} %copy-done.2, f32[18,32,128]{2,1,0:T(8,128)S(1)} %collective-permute-done.1.last_ref, ...), custom_call_target="tpu_custom_call" | custom-call | tf_op jit(solution)/shard_map/late/pallas_call | solution.py:648
  17.8 24.8 %all_to_all.5.grams_ref = f32[16,8,128]{2,1,0:T(8,128)S(1)} all-to-all(f32[16,8,128]{2,1,0:T(8,128)S(1)} %get-tuple-element.34), channel_id=1, replica_groups=mesh['freq'=2,'gz'=16] {'gz'}, dimensions={0} | all-to-all | bytes 131072 | tf_op jit(solution)/shard_map/all_to_all | solution.py:657
  42.6 4.5 %back.1 = (f32[4,2,8,32,128]{4,3,2,1,0:T(8,128)}, f32[2,16,24]{2,1,0:T(8,128)}) custom-call(s32[1]{0:T(128)} %bitcast.index_ref, f32[16]{0:T(128)S(1)} %copy-done.3, f32[8]{0:T(128)S(1)} %copy-done.4, f32[16,8,128]{2,1,0:T(8,128)S(1)} %all_to_all.5.grams_ref, bf16[144,4096]{1,0:T(8,128)(2,1)S(1)} %get-tuple-element.35.early_ref, ...), custom_call_target="tpu_custom_call" | custom-call | tf_op jit(solution)/shard_map/back/pallas_call | solution.py:658
Async XLA Ops:
  0.6 5.0 %copy-start.4 = (f32[8]{0:T(128)S(1)}, f32[8]{0:T(128)}, u32[]{:S(2)}) copy-start(f32[8]{0:T(128)} %damp_ref.7) | copy-start | bytes 100
  0.6 5.0 %copy-start.3 = (f32[16]{0:T(128)S(1)}, f32[16]{0:T(128)}, u32[]{:S(2)}) copy-start(f32[16]{0:T(128)} %wave_ref.7) | copy-start | bytes 196
  0.7 5.0 %copy-start.2 = (f32[2,8]{1,0:T(2,128)S(1)}, f32[2,8]{1,0:T(2,128)}, u32[]{:S(2)}) copy-start(f32[2,8]{1,0:T(2,128)} %wavelet_ref.5) | copy-start | bytes 196
  0.7 5.0 %copy-start.1 = (s32[8,3]{0,1:T(4,128)S(1)}, s32[8,3]{0,1:T(4,128)}, u32[]{:S(2)}) copy-start(s32[8,3]{0,1:T(4,128)} %param.12) | copy-start | bytes 292
  1.6 1.2 %copy-start = (f32[4,2,8,32,128]{4,3,2,1,0:T(8,128)S(1)}, f32[4,2,8,32,128]{4,3,2,1,0:T(8,128)}, u32[]{:S(2)}) copy-start(f32[4,2,8,32,128]{4,3,2,1,0:T(8,128)} %guess_ref.3) | copy-start | bytes 3145732
  3.1 2.5 %collective-permute-start = (f32[52,32,128]{2,1,0:T(8,128)S(1)}, f32[52,32,128]{2,1,0:T(8,128)S(1)}, u32[]{:S(2)}, u32[]{:S(2)}) collective-permute-start(f32[52,32,128]{2,1,0:T(8,128)S(1)} %get-tuple-element.21), channel_id=1, source_target_pairs={{0,1},{2,3},{4,5},{6,7},{8,9},{10,11},{12,13},{14,15},{1,0},{3,2},... | collective-permute-start | bytes 2555912 | tf_op jit(solution)/shard_map/ppermute | solution.py:604
  3.6 7.9 %collective-permute-start.2 = (f32[34,32,128]{2,1,0:T(8,128)S(1)}, f32[34,32,128]{2,1,0:T(8,128)S(1)}, u32[]{:S(2)}, u32[]{:S(2)}) collective-permute-start(f32[34,32,128]{2,1,0:T(8,128)S(1)} %get-tuple-element.23), channel_id=1, source_target_pairs={{1,2},{3,4},{5,6},{7,8},{9,10},{11,12},{13,14},{2,1},{4,3},{6,5},{... | collective-permute-start | bytes 1671176 | tf_op jit(solution)/shard_map/ppermute | solution.py:603
  10.9 4.7 %collective-permute-start.1 = (f32[18,32,128]{2,1,0:T(8,128)S(1)}, f32[18,32,128]{2,1,0:T(8,128)S(1)}, u32[]{:S(2)}, u32[]{:S(2)}) collective-permute-start(f32[18,32,128]{2,1,0:T(8,128)S(1)} %get-tuple-element.22), channel_id=1, source_target_pairs={{1,2},{3,4},{5,6},{7,8},{9,10},{11,12},{13,14},{2,1},{4,3},{6,5},{... | collective-permute-start | bytes 884744 | tf_op jit(solution)/shard_map/ppermute | solution.py:638
where the time goes:
time: 47.4 us; the launch traced here: 47.2 us
  blocking collectives  24.8 us (52%)
  Pallas kernels  16.3 us (34%)
  starting transfers between devices  1.87 us (4%)
  waiting for transfers between devices  1.32 us (3%)
  local copies, waits for them, and re-layouts  1.24 us (3%)
  other arithmetic  0.9 us (2%)
  between operations  0.73 us (2%)
    all_to_all x1, blocking collectives, shards(): grams = lax.all_to_all(grams, 'gz', 0, 0)  24.8 us
    pallas_call x1, Pallas kernels, shards(): pl.pallas_call(functools.partial(early_kernel, depth_total), out_shape=(p...  5.22 us
    pallas_call x1, Pallas kernels, shards(): pl.pallas_call(back_kernel, out_shape=(jax.ShapeDtypeStruct(initial_guess...  4.55 us
    pallas_call x1, Pallas kernels, shards(): pl.pallas_call(functools.partial(middle_kernel, depth_total), out_shape=(...  4.01 us
    pallas_call x1, Pallas kernels, shards(): pl.pallas_call(functools.partial(late_kernel, depth_total, layers), out_s...  2.26 us
    ppermute x1, waiting for transfers between devices, shards(): near = lax.ppermute(near, 'gz', near_pairs)  1.31 us
    unnamed x10, local copies, waits for them, and re-layouts  1.24 us
  transfers between devices with their start and end apart: 3, of which 1 were waited for; matrix products, arithmetic and copies ran while one was open for 0% of the time, Pallas kernels for 20%

commit v1 on v0

--- a/solution.py
+++ b/solution.py
@@ -133,31 +133,43 @@
     )
 
 
-def pack_kernel(index_ref, guess_ref, codes_ref, far_ref, near_ref, sems):
+def pack_kernel(index_ref, guess_ref, class_ref, layer_ref, edge_ref, near_ref, codes_ref, held, sems):
     layers, parts, shots, width, lanes = guess_ref.shape
     fields = parts * shots
     odd = lax.rem(index_ref[0], 2) == 1
     planes = guess_ref.reshape(layers * fields, width, lanes)
-    codes = codes_ref.reshape(2 * layers, width, lanes)
-    far_begin = jnp.where(odd, layers - 2, 0) * fields
-    far_code = jnp.where(odd, layers - 1, 0)
-    near_begin = jnp.where(odd, 0, layers - REACH) * fields
-    near_code = jnp.where(odd, 0, layers - 2)
+    edge = jnp.where(odd, layers - 1, 0) * fields
+    begin = jnp.where(odd, 0, layers - REACH) * fields
+    code = jnp.where(odd, 0, layers - 2)
+    moves = [(class_ref, held.at[0]), (layer_ref, held.at[1])]
+    moves.append((planes.at[pl.ds(edge, fields)], edge_ref))
+    for k in range(REACH):
+        moves.append(
+            (planes.at[pl.ds(begin + k * fields, fields)], near_ref.at[pl.ds(k * fields, fields)])
+        )
     copies = []
-    for number, (source, target) in enumerate(
-        (
-            (planes.at[pl.ds(far_begin, 2 * fields)], far_ref.at[pl.ds(0, 2 * fields)]),
-            (codes.at[pl.ds(far_code, 1)], far_ref.at[pl.ds(2 * fields, 1)]),
-            (codes.at[pl.ds(far_code + layers, 1)], far_ref.at[pl.ds(2 * fields + 1, 1)]),
-            (planes.at[pl.ds(near_begin, REACH * fields)], near_ref.at[pl.ds(0, REACH * fields)]),
-            (codes.at[pl.ds(near_code, 2)], near_ref.at[pl.ds(REACH * fields, 2)]),
-            (codes.at[pl.ds(near_code + layers, 2)], near_ref.at[pl.ds(REACH * fields + 2, 2)]),
-        )
-    ):
+    for number, (source, target) in enumerate(moves):
         copies.append(pltpu.make_async_copy(source, target, sems.at[number]))
         copies[-1].start()
-    for copy in copies:
+    copies[0].wait()
+    copies[1].wait()
+    for kind in range(2):
+        for q in range(layers):
+            codes_ref[kind, q] = held[kind, q].astype(jnp.float32)
+        for k in range(2):
+            near_ref[REACH * fields + 2 * kind + k] = held[kind, code + k].astype(jnp.float32)
+    for copy in copies[2:]:
         copy.wait()
+
+
+def fill_send(send_ref, guess_ref, codes_ref, odd, step):
+    layers, parts, shots = guess_ref.shape[:3]
+    plane = jnp.where(odd, layers - 1 - step, step)
+    code = jnp.where(odd, layers - step, step - 1)
+    for part in range(parts):
+        send_ref[part * shots : (part + 1) * shots] = guess_ref[plane, part]
+    send_ref[parts * shots] = codes_ref[0, code]
+    send_ref[parts * shots + 1] = codes_ref[1, code]
 
 
 def orientation(index_ref, layers, depth_total):
@@ -188,11 +200,7 @@
     codes_ref,
     field,
     start,
-    first,
-    second,
     tables,
-    split_ref,
-    products_ref,
     send_ref,
 ):
     layers, parts, shots, width, lanes = guess_ref.shape
@@ -202,14 +210,7 @@
     near_rows = near_ref.reshape(near_ref.shape[0] * width, lanes)
     span = fields * width
     keep = edge_masks(shots, lanes)
-
-    far_plane = jnp.where(odd, layers - REACH, REACH - 1)
-    far_code = jnp.where(odd, layers - 2, 1)
-    for part in range(parts):
-        send_ref[part * shots : (part + 1) * shots] = guess_ref[far_plane, part]
-    send_ref[fields] = codes_ref[0, far_code]
-    send_ref[fields + 1] = codes_ref[1, far_code]
-
+    fill_send(send_ref, guess_ref, codes_ref, odd, 1)
     extra = REACH * fields
     for k in range(2):
         pick = jnp.where(odd, k, 1 - k)
@@ -245,6 +246,25 @@
 
     lax.fori_loop(0, layers + 1, start_plane, 0)
     add_sources(start, -2, place_of, cells_ref, wavelet_ref)
+
+
+def image_kernel(
+    depth_total,
+    index_ref,
+    start,
+    tables,
+    nearest_ref,
+    first,
+    split_ref,
+    products_ref,
+    send_ref,
+    second,
+):
+    _, width, _, shots, lanes = start.shape
+    layers = start.shape[0] - 1
+    _, _, inside = orientation(index_ref, layers, depth_total)
+    keep = edge_masks(shots, lanes)
+    send_ref[0] = start[layers]
 
     def first_plane(j, carry):
         stencil_plane(
@@ -271,144 +291,9 @@
     products_ref[...] = products
 
 
-def middle_kernel(
-    depth_total,
-    index_ref,
-    wave_ref,
-    damp_ref,
-    cells_ref,
-    wavelet_ref,
-    far_ref,
-    old_field,
-    old_start,
-    old_first,
-    old_tables,
-    old_products,
-    field,
-    start,
-    first,
-    second,
-    tables,
-    split_ref,
-    products_ref,
-):
-    layers = old_field.shape[0] - REACH
-    _, width, parts, shots, lanes = field.shape
-    fields = parts * shots
-    odd, place_of, inside = orientation(index_ref, layers, depth_total)
-    far_rows = far_ref.reshape(far_ref.shape[0] * width, lanes)
-    span = fields * width
-    keep = edge_masks(shots, lanes)
-    fill_tables(
-        tables, 0, far_ref[2 * fields], far_ref[2 * fields + 1], inside(jnp.int32(layers)), wave_ref, damp_ref
-    )
-    for k in range(2):
-        bring(far_rows, jnp.where(odd, k, 1 - k) * span, field, k)
-
-    def at_field(place):
-        return (old_field, place + REACH) if place < layers else (field, place - layers)
-
-    def at_start(place):
-        return (old_start, place + 2) if place < layers - 1 else (start, place - (layers - 1))
-
-    def at_first(place):
-        return (old_first, place + 1) if place < layers - 2 else (first, place - (layers - 2))
-
-    def at_table(place, kind):
-        return (old_tables, place + 2, kind) if place < layers else (tables, place - layers, kind)
-
-    for place in range(layers - 1, layers + 1):
-        stencil_plane(
-            (at_field(place - 1), at_field(place), at_field(place + 1)),
-            at_start(place),
-            at_table(place, 0),
-            inside(jnp.int32(place)) * (-1.0 / 30.0),
-            keep,
-        )
-    add_sources(start, layers - 1, place_of, cells_ref, wavelet_ref)
-    for place in range(layers - 2, layers):
-        stencil_plane(
-            (at_start(place - 1), at_start(place), at_start(place + 1)),
-            at_first(place),
-            at_table(place, 1),
-            1.0 / 30.0,
-            keep,
-        )
-    products = old_products[...]
-    for k in range(2):
-        place = layers - 3 + k
-        stencil_plane(
-            (at_first(place - 1), at_first(place), at_first(place + 1)),
-            (second, k),
-            at_table(place, 1),
-            1.0 / 30.0,
-            keep,
-        )
-        split_plane((at_start(place), at_first(place), (second, k)), split_ref, k)
-        products += products_of(split_ref, k, width * lanes)
-    products_ref[...] = products
-
-
-def late_kernel(
-    depth_total,
-    layers,
-    index_ref,
-    wave_ref,
-    damp_ref,
-    cells_ref,
-    wavelet_ref,
-    last_ref,
-    old_field,
-    old_start,
-    old_first,
-    own_tables,
-    far_tables,
-    old_products,
-    split_ref,
-    gram_ref,
-    field,
-    start,
-    first,
-    second,
-    tables,
-):
-    _, width, parts, shots, lanes = field.shape
-    fields = parts * shots
-    odd, place_of, inside = orientation(index_ref, layers, depth_total)
-    last_rows = last_ref.reshape(last_ref.shape[0] * width, lanes)
-    keep = edge_masks(shots, lanes)
-    fill_tables(
-        tables, 0, last_ref[fields], last_ref[fields + 1], inside(jnp.int32(layers + 1)), wave_ref, damp_ref
-    )
-    bring(last_rows, 0, field, 0)
-    stencil_plane(
-        ((old_field, 0), (old_field, 1), (field, 0)),
-        (start, 0),
-        (tables, 0, 0),
-        inside(jnp.int32(layers + 1)) * (-1.0 / 30.0),
-        keep,
-    )
-    add_sources(start, layers + 1, place_of, cells_ref, wavelet_ref)
-    stencil_plane(
-        ((old_start, 0), (old_start, 1), (start, 0)),
-        (first, 0),
-        (far_tables, 0, 1),
-        inside(jnp.int32(layers)) * (1.0 / 30.0),
-        keep,
-    )
-    stencil_plane(
-        ((old_first, 0), (old_first, 1), (first, 0)),
-        (second, 0),
-        (own_tables, layers + 1, 1),
-        1.0 / 30.0,
-        keep,
-    )
-    split_plane(((old_start, 0), (old_first, 1), (second, 0)), split_ref, 0)
-    products = old_products[...] + products_of(split_ref, 0, width * lanes)
-
-    rows = BLOCKS * fields
+def pack_gram(products, shots, cells):
+    rows = 2 * BLOCKS * shots
     half = rows // 2
-    cells = float(depth_total * width * lanes)
     summed = products[0:rows] + products[rows : 2 * rows] + products[2 * rows : 3 * rows]
     summed = summed[:, 0:rows] + summed[:, rows : 2 * rows] + summed[:, 2 * rows : 3 * rows]
     summed = summed * (1.0 / cells)
@@ -419,14 +304,77 @@
         for values in (real, imag):
             blocks.append(values[i * shots : (i + 1) * shots, j * shots : (j + 1) * shots])
     blocks.append(jnp.zeros((shots, 128 - 2 * len(PAIRS) * shots), jnp.float32))
-    packed = jnp.concatenate(blocks, axis=1)
-    for copy in range(gram_ref.shape[0]):
-        gram_ref[copy] = packed
+    return jnp.concatenate(blocks, axis=1)
+
+
+def stage_kernel(stage, depth_total, layers, names, places, *refs):
+    refs = dict(zip(names, refs))
+    first, second, far_ref = refs["first"], refs["second"], refs["far"]
+    _, width, parts, shots, lanes = first.shape
+    odd, place_of, inside = orientation(refs["index"], layers, depth_total)
+    keep = edge_masks(shots, lanes)
+    top = layers - 1 + stage
+
+    def old(name):
+        return (refs[name], places[name])
+
+    if stage == 2:
+        start = far_ref
+        first_table = (refs["far_tables"], 0, 1)
+    else:
+        field, start = refs["field"], refs["start"]
+        first_table = (refs["own_tables"], top + 1, 1)
+        if stage == 0:
+            start_table = (refs["own_tables"], top + 2, 0)
+        else:
+            fill_tables(
+                refs["tables"],
+                0,
+                far_ref[parts * shots],
+                far_ref[parts * shots + 1],
+                inside(jnp.int32(top)),
+                refs["wave"],
+                refs["damp"],
+            )
+            start_table = (refs["tables"], 0, 0)
+        bring(far_ref.reshape(far_ref.shape[0] * width, lanes), 0, field, 0)
+        stencil_plane(
+            (old("field_a"), old("field_b"), (field, 0)),
+            (start, 0),
+            start_table,
+            inside(jnp.int32(top)) * (-1.0 / 30.0),
+            keep,
+        )
+        add_sources(start, top, place_of, refs["cells"], refs["wavelet"])
+    stencil_plane(
+        (old("start_a"), old("start_b"), (start, 0)),
+        (first, 0),
+        first_table,
+        inside(jnp.int32(top - 1)) * (1.0 / 30.0),
+        keep,
+    )
+    stencil_plane(
+        (old("first_a"), old("first_b"), (first, 0)),
+        (second, 0),
+        (refs["own_tables"], top, 1),
+        1.0 / 30.0,
+        keep,
+    )
+    split_ref = refs["split"]
+    split_plane((old("start_a"), old("first_b"), (second, 0)), split_ref, 0)
+    products = refs["products_in"][...] + products_of(split_ref, 0, width * lanes)
+    if stage < 2:
+        refs["products"][...] = products
+    else:
+        packed = pack_gram(products, shots, float(depth_total * width * lanes))
+        for copy in range(refs["grams"].shape[0]):
+            refs["grams"][copy] = packed
 
 
 def back_kernel(
-    index_ref, wave_ref, damp_ref, grams_ref, early_ref, middle_ref, late_ref, basis_ref, hessenberg_ref
+    index_ref, wave_ref, damp_ref, grams_ref, *rest
 ):
+    basis_ref, hessenberg_ref = rest[-2:]
     layers, parts, shots, width, y = basis_ref.shape
     fields = parts * shots
     rows = BLOCKS * fields
@@ -510,7 +458,7 @@
     out_rows = basis_ref.reshape(layers * fields * width, y)
     spots = [
         (ref, spot)
-        for ref in (early_ref, middle_ref, late_ref)
+        for ref in rest[:-2]
         for spot in range(ref.shape[1] // (width * y))
     ]
     group = 16
@@ -579,28 +527,38 @@
     hbm = pl.BlockSpec(memory_space=pl.ANY)
     params = pltpu.CompilerParams(vmem_limit_bytes=VMEM_BYTES)
 
-    codes = jnp.stack([velocity_class, layer_code]).astype(jnp.float32)
 
     def float_shape(*dims):
         return jax.ShapeDtypeStruct(dims, jnp.float32)
 
-    far, near = pl.pallas_call(
-        pack_kernel,
-        out_shape=(
-            float_shape(2 * fields + 2, width, lanes),
-            float_shape(REACH * fields + 4, width, lanes),
-        ),
-        in_specs=[smem, hbm, hbm],
-        out_specs=(vmem, vmem),
-        scratch_shapes=[pltpu.SemaphoreType.DMA((6,))],
-        compiler_params=params,
-        name="pack",
-    )(index, initial_guess, codes)
     odd_to_even = [(i, i + 1) for i in range(1, devices - 1, 2)]
     even_to_odd = [(i, i + 1) for i in range(0, devices, 2)]
     far_pairs = odd_to_even + [(b, a) for a, b in odd_to_even]
     near_pairs = even_to_odd + [(b, a) for a, b in even_to_odd]
-    far = lax.ppermute(far, "gz", far_pairs)
+
+    edge, near, codes = pl.pallas_call(
+        pack_kernel,
+        out_shape=(
+            float_shape(fields, width, lanes),
+            float_shape(REACH * fields + 4, width, lanes),
+            float_shape(2, layers, width, lanes),
+        ),
+        in_specs=[smem, hbm, hbm, hbm],
+        out_specs=(vmem, vmem, vmem),
+        scratch_shapes=[
+            pltpu.VMEM((2, layers, width, lanes), jnp.int32),
+            pltpu.SemaphoreType.DMA((3 + REACH,)),
+        ],
+        compiler_params=params,
+        name="pack",
+    )(
+        index,
+        *(
+            pltpu.with_memory_space_constraint(array, pltpu.HBM)
+            for array in (initial_guess, velocity_class, layer_code)
+        ),
+    )
+    nearest = lax.ppermute(edge, "gz", far_pairs)
     near = lax.ppermute(near, "gz", near_pairs)
 
     def planes(count):
@@ -616,44 +574,112 @@
         return pltpu.VMEM(shape.shape, shape.dtype)
 
     products = float_shape(BLOCKS * rows, BLOCKS * rows)
+    cost = pl.CostEstimate(flops=10_000_000, bytes_accessed=16_000_000, transcendentals=0)
     common = (index, wavenumber, damping, shot_cells, wavelet)
-    field, start, first, _, own_tables, early_split, products_one, last = pl.pallas_call(
+    send_shape = float_shape(fields + 2, width, lanes)
+    field, start, own_tables, send = pl.pallas_call(
         functools.partial(early_kernel, depth_total),
-        out_shape=(
-            planes(layers + REACH),
-            planes(layers + 1),
-            planes(layers - 1),
-            planes(layers - 3),
-            tables(layers + 2),
-            split(layers - 3),
-            products,
-            float_shape(fields + 2, width, lanes),
-        ),
+        out_shape=(planes(layers + REACH), planes(layers + 1), tables(layers + 2), send_shape),
         in_specs=[smem] * 5 + [vmem] * 3,
-        out_specs=(vmem,) * 8,
+        out_specs=(vmem,) * 4,
         compiler_params=params,
-        cost_estimate=pl.CostEstimate(flops=10_000_000, bytes_accessed=16_000_000, transcendentals=0),
+        cost_estimate=cost,
         name="early",
     )(*common, initial_guess, near, codes)
-    last = lax.ppermute(last, "gz", far_pairs)
-    field, start, first, _, far_tables, middle_split, products_two = pl.pallas_call(
-        functools.partial(middle_kernel, depth_total),
-        out_shape=(planes(2), planes(2), planes(2), planes(2), tables(1), split(2), products),
-        in_specs=[smem] * 5 + [vmem] * 6,
-        out_specs=(vmem,) * 7,
+    second_far = lax.ppermute(send, "gz", far_pairs)
+    first, early_split, early_products, send = pl.pallas_call(
+        functools.partial(image_kernel, depth_total),
+        out_shape=(planes(layers - 1), split(layers - 3), products, planes(1)),
+        in_specs=[smem] + [vmem] * 3,
+        out_specs=(vmem,) * 4,
+        scratch_shapes=[scratch(planes(layers - 3))],
         compiler_params=params,
-        cost_estimate=pl.CostEstimate(flops=8_000_000, bytes_accessed=12_000_000, transcendentals=0),
-        name="middle",
-    )(*common, far, field, start, first, own_tables, products_one)
-    late_split, grams = pl.pallas_call(
-        functools.partial(late_kernel, depth_total, layers),
-        out_shape=(split(1), float_shape(devices, shots, 128)),
-        in_specs=[smem] * 5 + [vmem] * 7,
-        out_specs=(vmem, vmem),
-        scratch_shapes=[scratch(planes(1))] * 4 + [scratch(tables(1))],
-        compiler_params=params,
-        name="late",
-    )(*common, last, field, start, first, own_tables, far_tables, products_two)
+        cost_estimate=cost,
+        name="images",
+    )(index, start, own_tables, nearest)
+    third_far = lax.ppermute(send, "gz", far_pairs)
+    shapes = {
+        "field": planes(1),
+        "start": planes(1),
+        "first": planes(1),
+        "second": planes(1),
+        "tables": tables(1),
+        "split": split(1),
+        "products": products,
+        "grams": float_shape(devices, shots, 128),
+    }
+
+    def run_stage(stage, far, old, extra, outs, temporaries):
+        inputs = {"index": index}
+        if stage < 2:
+            inputs = dict(zip(("index", "wave", "damp", "cells", "wavelet"), common))
+        scalars = len(inputs)
+        inputs["far"] = far
+        inputs.update({name: array for name, (array, _) in old.items()})
+        inputs.update(extra)
+        results = pl.pallas_call(
+            functools.partial(
+                stage_kernel,
+                stage,
+                depth_total,
+                layers,
+                list(inputs) + outs + temporaries,
+                {name: place for name, (_, place) in old.items()},
+            ),
+            out_shape=tuple(shapes[name] for name in outs),
+            in_specs=[smem] * scalars + [vmem] * (len(inputs) - scalars),
+            out_specs=(vmem,) * len(outs),
+            scratch_shapes=[scratch(shapes[name]) for name in temporaries],
+            compiler_params=params,
+            cost_estimate=cost,
+            name="stage_%d" % stage,
+        )(*inputs.values())
+        return dict(zip(outs, results))
+
+    zero = run_stage(
+        0,
+        nearest,
+        {
+            "field_a": (field, layers + 1),
+            "field_b": (field, layers + 2),
+            "start_a": (start, layers - 1),
+            "start_b": (start, layers),
+            "first_a": (first, layers - 3),
+            "first_b": (first, layers - 2),
+        },
+        {"own_tables": own_tables, "products_in": early_products},
+        ["field", "start", "first", "split", "products"],
+        ["second"],
+    )
+    one = run_stage(
+        1,
+        second_far,
+        {
+            "field_a": (field, layers + 2),
+            "field_b": (zero["field"], 0),
+            "start_a": (start, layers),
+            "start_b": (zero["start"], 0),
+            "first_a": (first, layers - 2),
+            "first_b": (zero["first"], 0),
+        },
+        {"own_tables": own_tables, "products_in": zero["products"]},
+        ["start", "first", "tables", "split", "products"],
+        ["field", "second"],
+    )
+    two = run_stage(
+        2,
+        third_far,
+        {
+            "start_a": (zero["start"], 0),
+            "start_b": (one["start"], 0),
+            "first_a": (zero["first"], 0),
+            "first_b": (one["first"], 0),
+        },
+        {"own_tables": own_tables, "far_tables": one["tables"], "products_in": one["products"]},
+        ["split", "grams"],
+        ["first", "second"],
+    )
+    grams = two["grams"]
     grams = lax.all_to_all(grams, "gz", 0, 0)
     basis_two, turned = pl.pallas_call(
         back_kernel,
@@ -661,11 +687,11 @@
             jax.ShapeDtypeStruct(initial_guess.shape, jnp.float32),
             jax.ShapeDtypeStruct((2, 2 * shots, BLOCKS * shots), jnp.float32),
         ),
-        in_specs=[smem] * 3 + [vmem] * 4,
+        in_specs=[smem] * 3 + [vmem] * 5,
         out_specs=(vmem, vmem),
         compiler_params=params,
         name="back",
-    )(index, wavenumber, damping, grams, early_split, middle_split, late_split)
+    )(index, wavenumber, damping, grams, early_split, zero["split"], one["split"], two["split"])
     return basis_two, jnp.swapaxes(turned, 1, 2)
 
 

time: 47.4 us -> 44.5 us (0.939)
  local copies, waits for them, and re-layouts: 1.24 us -> 0.02 us
  blocking collectives: 24.8 us -> 23.6 us
  other arithmetic: 0.9 us -> 0 us
  starting transfers between devices: 1.87 us -> 2.54 us
    pallas_call x1, Pallas kernels: 5.22 us -> 3.13 us  [shards(): pl.pallas_call(functools.partial(early_kernel, depth_total), out_shape=(p...]
    pallas_call x3 -> x5, Pallas kernels: 6.55 us -> 8.3 us  [the longest x3 5.43 us: run_stage(): pl.pallas_call(functools.partial(stage_kernel, stage, depth_total, layers...]
    unnamed x10, local copies, waits for them, and re-layouts: 1.24 us -> 0.02 us
    all_to_all x1, blocking collectives: 24.8 us -> 23.6 us  [shards(): grams = lax.all_to_all(grams, 'gz', 0, 0)]
    convert_element_type x1 -> x0, other arithmetic: 0.9 us -> none  [shards(): codes = jnp.stack([velocity_class, layer_code]).astype(jnp.float32)]
    ppermute x2 -> x3, starting transfers between devices: 1.35 us -> 2.02 us  [the longest x1 0.68 us: shards(): second_far = lax.ppermute(send, 'gz', far_pairs)]
  transfers between devices with their start and end apart: 3 -> 4, of which waited for: 1 -> 1; matrix products, arithmetic and copies ran while one was open for 0% -> 0% of each run, Pallas kernels for 20% -> 20%
where the time goes in v1:
time: 44.5 us; the launch traced here: 44.3 us
  blocking collectives  23.6 us (53%)
  Pallas kernels  16 us (36%)
  starting transfers between devices  2.54 us (6%)
  waiting for transfers between devices  1.34 us (3%)
  between operations  0.78 us (2%)
    all_to_all x1, blocking collectives, shards(): grams = lax.all_to_all(grams, 'gz', 0, 0)  23.6 us
    pallas_call x3, Pallas kernels, run_stage(): pl.pallas_call(functools.partial(stage_kernel, stage, depth_total, layers...  5.43 us
    pallas_call x1, Pallas kernels, shards(): pl.pallas_call(back_kernel, out_shape=(jax.ShapeDtypeStruct(initial_guess...  4.55 us
    pallas_call x1, Pallas kernels, shards(): pl.pallas_call(functools.partial(early_kernel, depth_total), out_shape=(p...  3.13 us
    pallas_call x1, Pallas kernels, shards(): pl.pallas_call(functools.partial(image_kernel, depth_total), out_shape=(p...  1.48 us
    pallas_call x1, Pallas kernels, shards(): pl.pallas_call(pack_kernel, out_shape=(float_shape(fields, width, lanes),...  1.38 us
    ppermute x1, waiting for transfers between devices, shards(): near = lax.ppermute(near, 'gz', near_pairs)  1.33 us
  transfers between devices with their start and end apart: 4, of which 1 were waited for; matrix products, arithmetic and copies ran while one was open for 0% of the time, Pallas kernels for 20%

profile of v1, /device:TPU:0, one launch (start us, length us, event | category | flops | bytes accessed | tf_op | source)
XLA Modules:
  0.0 44.3 jit_solution(13453597441219881940)
XLA Ops:
  0.6 0.0 copy-start
  0.6 0.0 copy-start.4
  0.7 0.0 copy-start.3
  0.7 0.0 copy-start.2
  0.7 0.0 copy-start.1
  0.7 1.4 %pack.1 = (f32[16,32,128]{2,1,0:T(8,128)S(1)}, f32[52,32,128]{2,1,0:T(8,128)S(1)}, f32[2,4,32,128]{3,2,1,0:T(8,128)S(1)}) custom-call(s32[1]{0:T(128)} %bitcast.index_ref.refs_0_, f32[4,2,8,32,128]{4,3,2,1,0:T(8,128)} %guess_ref.3, s32[4,32,128]{2,1,0:T(8,128)} %class_ref.1, s32[4,32,128]{2,1,0:T(8,128)} %layer_ref.1), custom_call_target="tpu_custom_call" | custom-call | tf_op jit(solution)/shard_map/pack/pallas_call | solution.py:539
  2.1 0.5 %collective-permute-start = (f32[52,32,128]{2,1,0:T(8,128)S(1)}, f32[52,32,128]{2,1,0:T(8,128)S(1)}, u32[]{:S(2)}, u32[]{:S(2)}) collective-permute-start(f32[52,32,128]{2,1,0:T(8,128)S(1)} %get-tuple-element.27), channel_id=1, source_target_pairs={{0,1},{2,3},{4,5},{6,7},{8,9},{10,11},{12,13},{14,15},{1,0},{3,2},... | collective-permute-start | bytes 2555912 | tf_op jit(solution)/shard_map/ppermute | solution.py:562
  2.6 0.7 %collective-permute-start.1 = (f32[16,32,128]{2,1,0:T(8,128)S(1)}, f32[16,32,128]{2,1,0:T(8,128)S(1)}, u32[]{:S(2)}, u32[]{:S(2)}) collective-permute-start(f32[16,32,128]{2,1,0:T(8,128)S(1)} %get-tuple-element.31), channel_id=1, source_target_pairs={{1,2},{3,4},{5,6},{7,8},{9,10},{11,12},{13,14},{2,1},{4,3},{6,5},{... | collective-permute-start | bytes 786440 | tf_op jit(solution)/shard_map/ppermute | solution.py:561
  3.3 1.3 %collective-permute-done.near_ref = f32[52,32,128]{2,1,0:T(8,128)S(1)} collective-permute-done((f32[52,32,128]{2,1,0:T(8,128)S(1)}, f32[52,32,128]{2,1,0:T(8,128)S(1)}, u32[]{:S(2)}, u32[]{:S(2)}) %collective-permute-start) | collective-permute-done | bytes 852000 | tf_op jit(solution)/shard_map/ppermute | solution.py:562
  4.6 0.0 copy-done
  4.6 0.0 copy-done.4
  4.6 0.0 copy-done.3
  4.6 0.0 copy-done.2
  4.6 0.0 copy-done.1
  4.6 3.1 %early.1 = (f32[7,32,2,8,128]{4,3,2,1,0:T(8,128)S(1)}, f32[5,32,2,8,128]{4,3,2,1,0:T(8,128)S(1)}, f32[6,4,32,128]{3,2,1,0:T(8,128)S(1)}, f32[18,32,128]{2,1,0:T(8,128)S(1)}) custom-call(s32[1]{0:T(128)} %bitcast.index_ref.refs_0_, f32[16]{0:T(128)S(1)} %copy-done.3, f32[8]{0:T(128)S(1)} %copy-done.4, s32[3,8]{1,0:T(4,128)S(1)} %bitcast.3, ...), custom_call_target="tpu_custom_call" | custom-call | flops 10000000 | bytes 16000000 | tf_op jit(solution)/shard_map/early/pallas_call | solution.py:580
  7.8 0.7 %collective-permute-start.3 = (f32[18,32,128]{2,1,0:T(8,128)S(1)}, f32[18,32,128]{2,1,0:T(8,128)S(1)}, u32[]{:S(2)}, u32[]{:S(2)}) collective-permute-start(f32[18,32,128]{2,1,0:T(8,128)S(1)} %get-tuple-element.37), channel_id=1, source_target_pairs={{1,2},{3,4},{5,6},{7,8},{9,10},{11,12},{13,14},{2,1},{4,3},{6,5},{... | collective-permute-start | bytes 884744 | tf_op jit(solution)/shard_map/ppermute | solution.py:589
  8.4 0.0 collective-permute-done.1.nearest_ref.refs_5_
  8.5 1.5 %images.1 = (f32[3,32,2,8,128]{4,3,2,1,0:T(8,128)S(1)}, bf16[144,4096]{1,0:T(8,128)(2,1)S(1)}, f32[144,144]{1,0:T(8,128)S(1)}, f32[1,32,2,8,128]{4,3,2,1,0:T(8,128)S(1)}) custom-call(s32[1]{0:T(128)} %bitcast.index_ref.refs_0_, f32[5,32,2,8,128]{4,3,2,1,0:T(8,128)S(1)} %get-tuple-element.29.start.refs_8_.refs_9_, ...), custom_call_target="tpu_custom_call" | custom-call | flops 10000000 | bytes 16000000 | tf_op jit(solution)/shard_map/images/pallas_call | solution.py:590
  9.9 0.7 %collective-permute-start.2 = (f32[1,32,2,8,128]{4,3,2,1,0:T(8,128)S(1)}, f32[1,32,2,8,128]{4,3,2,1,0:T(8,128)S(1)}, u32[]{:S(2)}, u32[]{:S(2)}) collective-permute-start(f32[1,32,2,8,128]{4,3,2,1,0:T(8,128)S(1)} %get-tuple-element.32), channel_id=1, source_target_pairs={{1,2},{3,4},{5,6},{7,8},{9,10},{11,12},{13,14},{2,1},{4,3},{6,5},{... | collective-permute-start | bytes 786440 | tf_op jit(solution)/shard_map/ppermute | solution.py:600
  10.6 2.1 %stage_0.1 = (f32[1,32,2,8,128]{4,3,2,1,0:T(8,128)S(1)}, f32[1,32,2,8,128]{4,3,2,1,0:T(8,128)S(1)}, f32[1,32,2,8,128]{4,3,2,1,0:T(8,128)S(1)}, bf16[144,4096]{1,0:T(8,128)(2,1)S(1)}, f32[144,144]{1,0:T(8,128)S(1)}) custom-call(s32[1]{0:T(128)} %bitcast.index_ref.refs_0_, f32[16]{0:T(128)S(1)} %copy-done.3, f32[8]{0:T(128)S(1)} %copy-done.4, ...), custom_call_target="tpu_custom_call" | custom-call | flops 10000000 | bytes 16000000 | tf_op jit(solution)/shard_map/stage_0/pallas_call | solution.py:620
  12.7 0.0 collective-permute-done.3.refs_5_
  12.7 2.1 %stage_1.1 = (f32[1,32,2,8,128]{4,3,2,1,0:T(8,128)S(1)}, f32[1,32,2,8,128]{4,3,2,1,0:T(8,128)S(1)}, f32[1,4,32,128]{3,2,1,0:T(8,128)S(1)}, bf16[144,4096]{1,0:T(8,128)(2,1)S(1)}, f32[144,144]{1,0:T(8,128)S(1)}) custom-call(s32[1]{0:T(128)} %bitcast.index_ref.refs_0_, f32[16]{0:T(128)S(1)} %copy-done.3, f32[8]{0:T(128)S(1)} %copy-done.4, s32[3,8]{1,0:T(4,128)S(1)} %bitcast.5, ...), custom_call_target="tpu_custom_call" | custom-call | flops 10000000 | bytes 16000000 | tf_op jit(solution)/shard_map/stage_1/pallas_call | solution.py:620
  14.8 0.0 collective-permute-done.2.refs_1_
  14.8 1.3 %stage_2.1 = (bf16[144,4096]{1,0:T(8,128)(2,1)S(1)}, f32[16,8,128]{2,1,0:T(8,128)S(1)}) custom-call(s32[1]{0:T(128)} %bitcast.index_ref.refs_0_, f32[1,32,2,8,128]{4,3,2,1,0:T(8,128)S(1)} %collective-permute-done.2.refs_1_, f32[1,32,2,8,128]{4,3,2,1,0:T(8,128)S(1)} %get-tuple-element.36.refs_9_.refs_2_, f32[1,32,2,8,128]{4,3,2,1,0:T(8,128)S(1)} %get-tuple-element.41.refs_3_, ...), custom_call_target="tpu_custom_call" | custom-call | flops 10000000 | bytes 16000000 | tf_op jit(solution)/shard_map/stage_2/pallas_call | solution.py:620
  16.1 23.6 %all_to_all.5.grams_ref = f32[16,8,128]{2,1,0:T(8,128)S(1)} all-to-all(f32[16,8,128]{2,1,0:T(8,128)S(1)} %get-tuple-element.45), channel_id=1, replica_groups=mesh['freq'=2,'gz'=16] {'gz'}, dimensions={0} | all-to-all | bytes 131072 | tf_op jit(solution)/shard_map/all_to_all | solution.py:683
  39.7 4.6 %back.1 = (f32[4,2,8,32,128]{4,3,2,1,0:T(8,128)}, f32[2,16,24]{2,1,0:T(8,128)}) custom-call(s32[1]{0:T(128)} %bitcast.index_ref.refs_0_, f32[16]{0:T(128)S(1)} %copy-done.3, f32[8]{0:T(128)S(1)} %copy-done.4, f32[16,8,128]{2,1,0:T(8,128)S(1)} %all_to_all.5.grams_ref, bf16[144,4096]{1,0:T(8,128)(2,1)S(1)} %get-tuple-element.46.rest_0_, ...), custom_call_target="tpu_custom_call" | custom-call | tf_op jit(solution)/shard_map/back/pallas_call | solution.py:684
Async XLA Ops:
  0.6 4.0 %copy-start = (f32[4,2,8,32,128]{4,3,2,1,0:T(8,128)S(1)}, f32[4,2,8,32,128]{4,3,2,1,0:T(8,128)}, u32[]{:S(2)}) copy-start(f32[4,2,8,32,128]{4,3,2,1,0:T(8,128)} %guess_ref.3) | copy-start | bytes 3145732
  0.6 4.0 %copy-start.4 = (f32[8]{0:T(128)S(1)}, f32[8]{0:T(128)}, u32[]{:S(2)}) copy-start(f32[8]{0:T(128)} %damp_ref.3) | copy-start | bytes 100
  0.7 4.0 %copy-start.3 = (f32[16]{0:T(128)S(1)}, f32[16]{0:T(128)}, u32[]{:S(2)}) copy-start(f32[16]{0:T(128)} %wave_ref.3) | copy-start | bytes 196
  0.7 3.9 %copy-start.2 = (f32[2,8]{1,0:T(2,128)S(1)}, f32[2,8]{1,0:T(2,128)}, u32[]{:S(2)}) copy-start(f32[2,8]{1,0:T(2,128)} %refs_4_.3) | copy-start | bytes 196
  0.7 3.9 %copy-start.1 = (s32[8,3]{0,1:T(4,128)S(1)}, s32[8,3]{0,1:T(4,128)}, u32[]{:S(2)}) copy-start(s32[8,3]{0,1:T(4,128)} %param.12) | copy-start | bytes 292
  2.1 2.5 %collective-permute-start = (f32[52,32,128]{2,1,0:T(8,128)S(1)}, f32[52,32,128]{2,1,0:T(8,128)S(1)}, u32[]{:S(2)}, u32[]{:S(2)}) collective-permute-start(f32[52,32,128]{2,1,0:T(8,128)S(1)} %get-tuple-element.27), channel_id=1, source_target_pairs={{0,1},{2,3},{4,5},{6,7},{8,9},{10,11},{12,13},{14,15},{1,0},{3,2},... | collective-permute-start | bytes 2555912 | tf_op jit(solution)/shard_map/ppermute | solution.py:562
  2.6 5.9 %collective-permute-start.1 = (f32[16,32,128]{2,1,0:T(8,128)S(1)}, f32[16,32,128]{2,1,0:T(8,128)S(1)}, u32[]{:S(2)}, u32[]{:S(2)}) collective-permute-start(f32[16,32,128]{2,1,0:T(8,128)S(1)} %get-tuple-element.31), channel_id=1, source_target_pairs={{1,2},{3,4},{5,6},{7,8},{9,10},{11,12},{13,14},{2,1},{4,3},{6,5},{... | collective-permute-start | bytes 786440 | tf_op jit(solution)/shard_map/ppermute | solution.py:561
  7.8 5.0 %collective-permute-start.3 = (f32[18,32,128]{2,1,0:T(8,128)S(1)}, f32[18,32,128]{2,1,0:T(8,128)S(1)}, u32[]{:S(2)}, u32[]{:S(2)}) collective-permute-start(f32[18,32,128]{2,1,0:T(8,128)S(1)} %get-tuple-element.37), channel_id=1, source_target_pairs={{1,2},{3,4},{5,6},{7,8},{9,10},{11,12},{13,14},{2,1},{4,3},{6,5},{... | collective-permute-start | bytes 884744 | tf_op jit(solution)/shard_map/ppermute | solution.py:589
  9.9 4.9 %collective-permute-start.2 = (f32[1,32,2,8,128]{4,3,2,1,0:T(8,128)S(1)}, f32[1,32,2,8,128]{4,3,2,1,0:T(8,128)S(1)}, u32[]{:S(2)}, u32[]{:S(2)}) collective-permute-start(f32[1,32,2,8,128]{4,3,2,1,0:T(8,128)S(1)} %get-tuple-element.32), channel_id=1, source_target_pairs={{1,2},{3,4},{5,6},{7,8},{9,10},{11,12},{13,14},{2,1},{4,3},{6,5},{... | collective-permute-start | bytes 786440 | tf_op jit(solution)/shard_map/ppermute | solution.py:600

commit v2 on v1

--- a/solution.py
+++ b/solution.py
@@ -133,7 +133,7 @@
     )
 
 
-def pack_kernel(index_ref, guess_ref, class_ref, layer_ref, edge_ref, near_ref, codes_ref, held, sems):
+def pack_kernel(index_ref, guess_ref, class_ref, layer_ref, edge_ref, next_ref, near_ref, codes_ref, held, sems):
     layers, parts, shots, width, lanes = guess_ref.shape
     fields = parts * shots
     odd = lax.rem(index_ref[0], 2) == 1
@@ -141,8 +141,9 @@
     edge = jnp.where(odd, layers - 1, 0) * fields
     begin = jnp.where(odd, 0, layers - REACH) * fields
     code = jnp.where(odd, 0, layers - 2)
+    edge_code = jnp.where(odd, layers - 1, 0)
     moves = [(class_ref, held.at[0]), (layer_ref, held.at[1])]
-    moves.append((planes.at[pl.ds(edge, fields)], edge_ref))
+    moves.append((planes.at[pl.ds(edge, fields)], edge_ref.at[pl.ds(0, fields)]))
     for k in range(REACH):
         moves.append(
             (planes.at[pl.ds(begin + k * fields, fields)], near_ref.at[pl.ds(k * fields, fields)])
@@ -158,18 +159,11 @@
             codes_ref[kind, q] = held[kind, q].astype(jnp.float32)
         for k in range(2):
             near_ref[REACH * fields + 2 * kind + k] = held[kind, code + k].astype(jnp.float32)
+        edge_ref[fields + kind] = held[kind, edge_code].astype(jnp.float32)
     for copy in copies[2:]:
         copy.wait()
-
-
-def fill_send(send_ref, guess_ref, codes_ref, odd, step):
-    layers, parts, shots = guess_ref.shape[:3]
-    plane = jnp.where(odd, layers - 1 - step, step)
-    code = jnp.where(odd, layers - step, step - 1)
-    for part in range(parts):
-        send_ref[part * shots : (part + 1) * shots] = guess_ref[plane, part]
-    send_ref[parts * shots] = codes_ref[0, code]
-    send_ref[parts * shots + 1] = codes_ref[1, code]
+    following = jnp.where(odd, REACH - 1, 0) * fields
+    next_ref[...] = near_ref[pl.ds(following, fields)]
 
 
 def orientation(index_ref, layers, depth_total):
@@ -195,22 +189,23 @@
     damp_ref,
     cells_ref,
     wavelet_ref,
-    guess_ref,
+    edge_ref,
+    own_ref,
     near_ref,
     codes_ref,
     field,
     start,
     tables,
-    send_ref,
 ):
-    layers, parts, shots, width, lanes = guess_ref.shape
+    _, layers, width, lanes = codes_ref.shape
+    parts, shots = start.shape[2:4]
     fields = parts * shots
     odd, place_of, inside = orientation(index_ref, layers, depth_total)
-    guess_rows = guess_ref.reshape(layers * fields * width, lanes)
+    own_rows = own_ref.reshape(own_ref.shape[0] * width, lanes)
+    edge_rows = edge_ref.reshape(edge_ref.shape[0] * width, lanes)
     near_rows = near_ref.reshape(near_ref.shape[0] * width, lanes)
     span = fields * width
     keep = edge_masks(shots, lanes)
-    fill_send(send_ref, guess_ref, codes_ref, odd, 1)
     extra = REACH * fields
     for k in range(2):
         pick = jnp.where(odd, k, 1 - k)
@@ -228,11 +223,12 @@
         return carry
 
     def bring_own(q, carry):
-        bring(guess_rows, jnp.where(odd, q, layers - 1 - q) * span, field, q + REACH)
+        bring(own_rows, jnp.where(odd, q, REACH - 1 - q) * span, field, q + REACH)
         return carry
 
     lax.fori_loop(0, REACH, bring_near, 0)
-    lax.fori_loop(0, layers, bring_own, 0)
+    lax.fori_loop(0, REACH, bring_own, 0)
+    bring(edge_rows, 0, field, REACH + layers - 1)
 
     def start_plane(i, carry):
         stencil_plane(
@@ -253,7 +249,6 @@
     index_ref,
     start,
     tables,
-    nearest_ref,
     first,
     split_ref,
     products_ref,
@@ -330,8 +325,8 @@
             fill_tables(
                 refs["tables"],
                 0,
-                far_ref[parts * shots],
-                far_ref[parts * shots + 1],
+                refs["nearest"][parts * shots],
+                refs["nearest"][parts * shots + 1],
                 inside(jnp.int32(top)),
                 refs["wave"],
                 refs["damp"],
@@ -415,26 +410,55 @@
         real.append(unit + jnp.concatenate([blank, parts_of[0]], axis=1))
         imag.append(jnp.concatenate([blank, parts_of[1]], axis=1))
     pivots = []
-    for k in range(half):
-        owner, row = divmod(k, tile)
-        row_real = real[owner][row : row + 1]
-        row_imag = imag[owner][row : row + 1]
-        spot = spread + k
-        pivot = row_real[:, spot : spot + 1]
-        pivots.append(pivot)
-        inverse = 1.0 / pivot
-        for t in range(owner, tiles):
-            column_real = real[t][:, spot : spot + 1] * inverse
-            column_imag = imag[t][:, spot : spot + 1] * inverse
-            if t == owner:
-                below = sub[:, 0:1] > row
-                column_real = jnp.where(below, column_real, 0.0)
-                column_imag = jnp.where(below, column_imag, 0.0)
-            new_real = real[t] - (column_real * row_real - column_imag * row_imag)
-            new_imag = imag[t] - (column_real * row_imag + column_imag * row_real)
-            real[t], imag[t] = new_real, new_imag
+    for owner in range(tiles):
+        spots = [spread + owner * tile + r for r in range(tile)]
+        shape = (tile, lanes)
+        ahead = {
+            (t, r): [
+                jnp.broadcast_to(values[t][:, spots[r] : spots[r] + 1], shape) for values in (real, imag)
+            ]
+            for t in range(owner, tiles)
+            for r in range(tile)
+        }
+        for r in range(tile):
+            own_real, own_imag = ahead[owner, r]
+            pivot = jnp.broadcast_to(own_real[r : r + 1], shape)
+            pivots.append(pivot)
+            inverse = pl.reciprocal(pivot, approx=True)
+            for _ in range(2):
+                inverse = inverse * (2.0 - pivot * inverse)
+            scaled = {}
+            for t in range(owner, tiles):
+                column_real, column_imag = [value * inverse for value in ahead[t, r]]
+                if t == owner:
+                    column_real = jnp.where(sub > r, column_real, 0.0)
+                    column_imag = jnp.where(sub > r, column_imag, 0.0)
+                scaled[t] = column_real, column_imag
+            for later in range(r + 1, tile):
+                entry_real = jnp.broadcast_to(own_real[later : later + 1], shape)
+                entry_imag = jnp.broadcast_to(own_imag[later : later + 1], shape)
+                for t in range(owner, tiles):
+                    column_real, column_imag = scaled[t]
+                    old_real, old_imag = ahead[t, later]
+                    ahead[t, later] = [
+                        old_real - (column_real * entry_real + column_imag * entry_imag),
+                        old_imag - (column_imag * entry_real - column_real * entry_imag),
+                    ]
+            row_real = real[owner][r : r + 1]
+            row_imag = imag[owner][r : r + 1]
+            for t in range(owner, tiles):
+                column_real, column_imag = [
+                    jnp.concatenate([value, value], axis=1) for value in scaled[t]
+                ]
+                new_real = real[t] - (column_real * row_real - column_imag * row_imag)
+                new_imag = imag[t] - (column_real * row_imag + column_imag * row_real)
+                real[t], imag[t] = new_real, new_imag
     for t in range(tiles):
-        scales = lax.rsqrt(jnp.concatenate(pivots[t * tile : (t + 1) * tile], axis=0))
+        scales = pivots[t * tile]
+        for r in range(1, tile):
+            scales = jnp.where(sub == r, pivots[t * tile + r], scales)
+        scales = lax.rsqrt(scales)
+        scales = jnp.concatenate([scales, scales], axis=1)
         real[t] = real[t] * scales
         imag[t] = imag[t] * scales
 
@@ -515,6 +539,7 @@
 def shards(initial_guess, velocity_class, layer_code, wavenumber, damping, shot_cells, wavelet):
     layers, parts, shots, width, lanes = initial_guess.shape
     devices = lax.axis_size("gz")
+    assert layers == REACH + 1 and devices % 2 == 0
     fields = parts * shots
     rows = BLOCKS * fields
     span = width * lanes
@@ -536,15 +561,16 @@
     far_pairs = odd_to_even + [(b, a) for a, b in odd_to_even]
     near_pairs = even_to_odd + [(b, a) for a, b in even_to_odd]
 
-    edge, near, codes = pl.pallas_call(
+    edge, following, near, codes = pl.pallas_call(
         pack_kernel,
         out_shape=(
+            float_shape(fields + 2, width, lanes),
             float_shape(fields, width, lanes),
             float_shape(REACH * fields + 4, width, lanes),
             float_shape(2, layers, width, lanes),
         ),
         in_specs=[smem, hbm, hbm, hbm],
-        out_specs=(vmem, vmem, vmem),
+        out_specs=(vmem, vmem, vmem, vmem),
         scratch_shapes=[
             pltpu.VMEM((2, layers, width, lanes), jnp.int32),
             pltpu.SemaphoreType.DMA((3 + REACH,)),
@@ -559,7 +585,9 @@
         ),
     )
     nearest = lax.ppermute(edge, "gz", far_pairs)
-    near = lax.ppermute(near, "gz", near_pairs)
+    second_far = lax.ppermute(following, "gz", far_pairs)
+    own = near
+    near = lax.ppermute(own, "gz", near_pairs)
 
     def planes(count):
         return float_shape(count, width, parts, shots, lanes)
@@ -576,27 +604,25 @@
     products = float_shape(BLOCKS * rows, BLOCKS * rows)
     cost = pl.CostEstimate(flops=10_000_000, bytes_accessed=16_000_000, transcendentals=0)
     common = (index, wavenumber, damping, shot_cells, wavelet)
-    send_shape = float_shape(fields + 2, width, lanes)
-    field, start, own_tables, send = pl.pallas_call(
+    field, start, own_tables = pl.pallas_call(
         functools.partial(early_kernel, depth_total),
-        out_shape=(planes(layers + REACH), planes(layers + 1), tables(layers + 2), send_shape),
-        in_specs=[smem] * 5 + [vmem] * 3,
-        out_specs=(vmem,) * 4,
+        out_shape=(planes(layers + REACH), planes(layers + 1), tables(layers + 2)),
+        in_specs=[smem] * 5 + [vmem] * 4,
+        out_specs=(vmem,) * 3,
         compiler_params=params,
         cost_estimate=cost,
         name="early",
-    )(*common, initial_guess, near, codes)
-    second_far = lax.ppermute(send, "gz", far_pairs)
+    )(*common, edge, own, near, codes)
     first, early_split, early_products, send = pl.pallas_call(
         functools.partial(image_kernel, depth_total),
         out_shape=(planes(layers - 1), split(layers - 3), products, planes(1)),
-        in_specs=[smem] + [vmem] * 3,
+        in_specs=[smem] + [vmem] * 2,
         out_specs=(vmem,) * 4,
         scratch_shapes=[scratch(planes(layers - 3))],
         compiler_params=params,
         cost_estimate=cost,
         name="images",
-    )(index, start, own_tables, nearest)
+    )(index, start, own_tables)
     third_far = lax.ppermute(send, "gz", far_pairs)
     shapes = {
         "field": planes(1),
@@ -662,7 +688,7 @@
             "first_a": (first, layers - 2),
             "first_b": (zero["first"], 0),
         },
-        {"own_tables": own_tables, "products_in": zero["products"]},
+        {"own_tables": own_tables, "products_in": zero["products"], "nearest": nearest},
         ["start", "first", "tables", "split", "products"],
         ["field", "second"],
     )

time: 44.5 us -> 42.6 us (0.957)
  Pallas kernels: 16 us -> 14.8 us
  waiting for transfers between devices: 1.34 us -> 0.65 us
    pallas_call x1, Pallas kernels: 4.55 us -> 3.39 us  [shards(): pl.pallas_call(back_kernel, out_shape=(jax.ShapeDtypeStruct(initial_guess...]
    ppermute x2, waiting for transfers between devices: 1.34 us -> 0.65 us  [the longest x1 0.65 us: shards(): near = lax.ppermute(own, 'gz', near_pairs)]
  transfers between devices with their start and end apart: 4 -> 4, of which waited for: 1 -> 1; matrix products, arithmetic and copies ran while one was open for 0% -> 0% of each run, Pallas kernels for 20% -> 21%
where the time goes in v2:
time: 42.6 us; the launch traced here: 42.4 us
  blocking collectives  23.7 us (56%)
  Pallas kernels  14.8 us (35%)
  starting transfers between devices  2.54 us (6%)
  between operations  0.77 us (2%)
  waiting for transfers between devices  0.65 us (2%)
    all_to_all x1, blocking collectives, shards(): grams = lax.all_to_all(grams, 'gz', 0, 0)  23.7 us
    pallas_call x3, Pallas kernels, run_stage(): pl.pallas_call(functools.partial(stage_kernel, stage, depth_total, layers...  5.44 us
    pallas_call x1, Pallas kernels, shards(): pl.pallas_call(back_kernel, out_shape=(jax.ShapeDtypeStruct(initial_guess...  3.39 us
    pallas_call x1, Pallas kernels, shards(): pl.pallas_call(functools.partial(early_kernel, depth_total), out_shape=(p...  3.09 us
    pallas_call x1, Pallas kernels, shards(): pl.pallas_call(functools.partial(image_kernel, depth_total), out_shape=(p...  1.48 us
    pallas_call x1, Pallas kernels, shards(): pl.pallas_call(pack_kernel, out_shape=(float_shape(fields + 2, width, lan...  1.35 us
  transfers between devices with their start and end apart: 4, of which 1 were waited for; matrix products, arithmetic and copies ran while one was open for 0% of the time, Pallas kernels for 21%

profile of v2, /device:TPU:0, one launch (start us, length us, event | category | flops | bytes accessed | tf_op | source)
XLA Modules:
  0.0 42.4 jit_solution(16582853558629276935)
XLA Ops:
  0.6 0.0 copy-start.3
  0.6 0.0 copy-start.2
  0.7 0.0 copy-start.1
  0.7 0.0 copy-start
  0.7 1.4 %pack.1 = (f32[18,32,128]{2,1,0:T(8,128)S(1)}, f32[16,32,128]{2,1,0:T(8,128)S(1)}, f32[52,32,128]{2,1,0:T(8,128)S(1)}, f32[2,4,32,128]{3,2,1,0:T(8,128)S(1)}) custom-call(s32[1]{0:T(128)} %bitcast.index_ref.refs_0_, f32[4,2,8,32,128]{4,3,2,1,0:T(8,128)} %guess_ref.1, s32[4,32,128]{2,1,0:T(8,128)} %class_ref.1, s32[4,32,128]{2,1,0:T(8,128)} %layer_ref.1), custom_call_target="tpu_custom_call" | custom-call | tf_op jit(solution)/shard_map/pack/pallas_call | solution.py:564
  2.0 0.5 %collective-permute-start = (f32[52,32,128]{2,1,0:T(8,128)S(1)}, f32[52,32,128]{2,1,0:T(8,128)S(1)}, u32[]{:S(2)}, u32[]{:S(2)}) collective-permute-start(f32[52,32,128]{2,1,0:T(8,128)S(1)} %get-tuple-element.28.own_ref), channel_id=1, source_target_pairs={{0,1},{2,3},{4,5},{6,7},{8,9},{10,11},{12,13},{14,15},{1,0},{3,2},... | collective-permute-start | bytes 2555912 | tf_op jit(solution)/shard_map/ppermute | solution.py:590
  2.6 0.7 %collective-permute-start.2 = (f32[18,32,128]{2,1,0:T(8,128)S(1)}, f32[18,32,128]{2,1,0:T(8,128)S(1)}, u32[]{:S(2)}, u32[]{:S(2)}) collective-permute-start(f32[18,32,128]{2,1,0:T(8,128)S(1)} %get-tuple-element.27.edge_ref), channel_id=1, source_target_pairs={{1,2},{3,4},{5,6},{7,8},{9,10},{11,12},{13,14},{2,1},{4,3},{6,5},{... | collective-permute-start | bytes 884744 | tf_op jit(solution)/shard_map/ppermute | solution.py:587
  3.2 0.7 %collective-permute-start.3 = (f32[16,32,128]{2,1,0:T(8,128)S(1)}, f32[16,32,128]{2,1,0:T(8,128)S(1)}, u32[]{:S(2)}, u32[]{:S(2)}) collective-permute-start(f32[16,32,128]{2,1,0:T(8,128)S(1)} %get-tuple-element.37), channel_id=1, source_target_pairs={{1,2},{3,4},{5,6},{7,8},{9,10},{11,12},{13,14},{2,1},{4,3},{6,5},{... | collective-permute-start | bytes 786440 | tf_op jit(solution)/shard_map/ppermute | solution.py:588
  3.9 0.6 %collective-permute-done.near_ref = f32[52,32,128]{2,1,0:T(8,128)S(1)} collective-permute-done((f32[52,32,128]{2,1,0:T(8,128)S(1)}, f32[52,32,128]{2,1,0:T(8,128)S(1)}, u32[]{:S(2)}, u32[]{:S(2)}) %collective-permute-start) | collective-permute-done | bytes 852000 | tf_op jit(solution)/shard_map/ppermute | solution.py:590
  4.6 0.0 copy-done.3
  4.6 0.0 copy-done.2
  4.6 0.0 copy-done.1
  4.6 0.0 copy-done
  4.6 3.1 %early.1 = (f32[7,32,2,8,128]{4,3,2,1,0:T(8,128)S(1)}, f32[5,32,2,8,128]{4,3,2,1,0:T(8,128)S(1)}, f32[6,4,32,128]{3,2,1,0:T(8,128)S(1)}) custom-call(s32[1]{0:T(128)} %bitcast.index_ref.refs_0_, f32[16]{0:T(128)S(1)} %copy-done.2, f32[8]{0:T(128)S(1)} %copy-done.3, s32[3,8]{1,0:T(4,128)S(1)} %bitcast.3, f32[2,8]{1,0:T(2,128)S(1)} %copy-done.1, ...), custom_call_target="tpu_custom_call" | custom-call | flops 10000000 | bytes 16000000 | tf_op jit(solution)/shard_map/early/pallas_call | solution.py:607
  7.7 1.5 %images.1 = (f32[3,32,2,8,128]{4,3,2,1,0:T(8,128)S(1)}, bf16[144,4096]{1,0:T(8,128)(2,1)S(1)}, f32[144,144]{1,0:T(8,128)S(1)}, f32[1,32,2,8,128]{4,3,2,1,0:T(8,128)S(1)}) custom-call(s32[1]{0:T(128)} %bitcast.index_ref.refs_0_, f32[5,32,2,8,128]{4,3,2,1,0:T(8,128)S(1)} %get-tuple-element.30.start.refs_8_.refs_9_, ...), custom_call_target="tpu_custom_call" | custom-call | flops 10000000 | bytes 16000000 | tf_op jit(solution)/shard_map/images/pallas_call | solution.py:616
  9.2 0.7 %collective-permute-start.1 = (f32[1,32,2,8,128]{4,3,2,1,0:T(8,128)S(1)}, f32[1,32,2,8,128]{4,3,2,1,0:T(8,128)S(1)}, u32[]{:S(2)}, u32[]{:S(2)}) collective-permute-start(f32[1,32,2,8,128]{4,3,2,1,0:T(8,128)S(1)} %get-tuple-element.32), channel_id=1, source_target_pairs={{1,2},{3,4},{5,6},{7,8},{9,10},{11,12},{13,14},{2,1},{4,3},{6,5},{... | collective-permute-start | bytes 786440 | tf_op jit(solution)/shard_map/ppermute | solution.py:626
  9.9 0.0 collective-permute-done.2.refs_5_.refs_14_
  9.9 2.1 %stage_0.1 = (f32[1,32,2,8,128]{4,3,2,1,0:T(8,128)S(1)}, f32[1,32,2,8,128]{4,3,2,1,0:T(8,128)S(1)}, f32[1,32,2,8,128]{4,3,2,1,0:T(8,128)S(1)}, bf16[144,4096]{1,0:T(8,128)(2,1)S(1)}, f32[144,144]{1,0:T(8,128)S(1)}) custom-call(s32[1]{0:T(128)} %bitcast.index_ref.refs_0_, f32[16]{0:T(128)S(1)} %copy-done.2, f32[8]{0:T(128)S(1)} %copy-done.3, ...), custom_call_target="tpu_custom_call" | custom-call | flops 10000000 | bytes 16000000 | tf_op jit(solution)/shard_map/stage_0/pallas_call | solution.py:646
  11.9 0.0 collective-permute-done.3.refs_5_
  12.0 2.1 %stage_1.1 = (f32[1,32,2,8,128]{4,3,2,1,0:T(8,128)S(1)}, f32[1,32,2,8,128]{4,3,2,1,0:T(8,128)S(1)}, f32[1,4,32,128]{3,2,1,0:T(8,128)S(1)}, bf16[144,4096]{1,0:T(8,128)(2,1)S(1)}, f32[144,144]{1,0:T(8,128)S(1)}) custom-call(s32[1]{0:T(128)} %bitcast.index_ref.refs_0_, f32[16]{0:T(128)S(1)} %copy-done.2, f32[8]{0:T(128)S(1)} %copy-done.3, s32[3,8]{1,0:T(4,128)S(1)} %bitcast.5, ...), custom_call_target="tpu_custom_call" | custom-call | flops 10000000 | bytes 16000000 | tf_op jit(solution)/shard_map/stage_1/pallas_call | solution.py:646
  14.1 0.0 collective-permute-done.1.refs_1_
  14.1 1.3 %stage_2.1 = (bf16[144,4096]{1,0:T(8,128)(2,1)S(1)}, f32[16,8,128]{2,1,0:T(8,128)S(1)}) custom-call(s32[1]{0:T(128)} %bitcast.index_ref.refs_0_, f32[1,32,2,8,128]{4,3,2,1,0:T(8,128)S(1)} %collective-permute-done.1.refs_1_, f32[1,32,2,8,128]{4,3,2,1,0:T(8,128)S(1)} %get-tuple-element.36.refs_9_.refs_2_, f32[1,32,2,8,128]{4,3,2,1,0:T(8,128)S(1)} %get-tuple-element.41.refs_3_, ...), custom_call_target="tpu_custom_call" | custom-call | flops 10000000 | bytes 16000000 | tf_op jit(solution)/shard_map/stage_2/pallas_call | solution.py:646
  15.3 23.7 %all_to_all.5.grams_ref = f32[16,8,128]{2,1,0:T(8,128)S(1)} all-to-all(f32[16,8,128]{2,1,0:T(8,128)S(1)} %get-tuple-element.45), channel_id=1, replica_groups=mesh['freq'=2,'gz'=16] {'gz'}, dimensions={0} | all-to-all | bytes 131072 | tf_op jit(solution)/shard_map/all_to_all | solution.py:709
  39.0 3.4 %back.1 = (f32[4,2,8,32,128]{4,3,2,1,0:T(8,128)}, f32[2,16,24]{2,1,0:T(8,128)}) custom-call(s32[1]{0:T(128)} %bitcast.index_ref.refs_0_, f32[16]{0:T(128)S(1)} %copy-done.2, f32[8]{0:T(128)S(1)} %copy-done.3, f32[16,8,128]{2,1,0:T(8,128)S(1)} %all_to_all.5.grams_ref, bf16[144,4096]{1,0:T(8,128)(2,1)S(1)} %get-tuple-element.46.rest_0_, ...), custom_call_target="tpu_custom_call" | custom-call | tf_op jit(solution)/shard_map/back/pallas_call | solution.py:710
Async XLA Ops:
  0.6 3.9 %copy-start.3 = (f32[8]{0:T(128)S(1)}, f32[8]{0:T(128)}, u32[]{:S(2)}) copy-start(f32[8]{0:T(128)} %damp_ref.3) | copy-start | bytes 100
  0.6 3.9 %copy-start.2 = (f32[16]{0:T(128)S(1)}, f32[16]{0:T(128)}, u32[]{:S(2)}) copy-start(f32[16]{0:T(128)} %wave_ref.3) | copy-start | bytes 196
  0.7 3.9 %copy-start.1 = (f32[2,8]{1,0:T(2,128)S(1)}, f32[2,8]{1,0:T(2,128)}, u32[]{:S(2)}) copy-start(f32[2,8]{1,0:T(2,128)} %refs_4_.3) | copy-start | bytes 196
  0.7 3.9 %copy-start = (s32[8,3]{0,1:T(4,128)S(1)}, s32[8,3]{0,1:T(4,128)}, u32[]{:S(2)}) copy-start(s32[8,3]{0,1:T(4,128)} %param.12) | copy-start | bytes 292
  2.0 2.5 %collective-permute-start = (f32[52,32,128]{2,1,0:T(8,128)S(1)}, f32[52,32,128]{2,1,0:T(8,128)S(1)}, u32[]{:S(2)}, u32[]{:S(2)}) collective-permute-start(f32[52,32,128]{2,1,0:T(8,128)S(1)} %get-tuple-element.28.own_ref), channel_id=1, source_target_pairs={{0,1},{2,3},{4,5},{6,7},{8,9},{10,11},{12,13},{14,15},{1,0},{3,2},... | collective-permute-start | bytes 2555912 | tf_op jit(solution)/shard_map/ppermute | solution.py:590
  2.6 7.3 %collective-permute-start.2 = (f32[18,32,128]{2,1,0:T(8,128)S(1)}, f32[18,32,128]{2,1,0:T(8,128)S(1)}, u32[]{:S(2)}, u32[]{:S(2)}) collective-permute-start(f32[18,32,128]{2,1,0:T(8,128)S(1)} %get-tuple-element.27.edge_ref), channel_id=1, source_target_pairs={{1,2},{3,4},{5,6},{7,8},{9,10},{11,12},{13,14},{2,1},{4,3},{6,5},{... | collective-permute-start | bytes 884744 | tf_op jit(solution)/shard_map/ppermute | solution.py:587
  3.2 8.7 %collective-permute-start.3 = (f32[16,32,128]{2,1,0:T(8,128)S(1)}, f32[16,32,128]{2,1,0:T(8,128)S(1)}, u32[]{:S(2)}, u32[]{:S(2)}) collective-permute-start(f32[16,32,128]{2,1,0:T(8,128)S(1)} %get-tuple-element.37), channel_id=1, source_target_pairs={{1,2},{3,4},{5,6},{7,8},{9,10},{11,12},{13,14},{2,1},{4,3},{6,5},{... | collective-permute-start | bytes 786440 | tf_op jit(solution)/shard_map/ppermute | solution.py:588
  9.2 4.9 %collective-permute-start.1 = (f32[1,32,2,8,128]{4,3,2,1,0:T(8,128)S(1)}, f32[1,32,2,8,128]{4,3,2,1,0:T(8,128)S(1)}, u32[]{:S(2)}, u32[]{:S(2)}) collective-permute-start(f32[1,32,2,8,128]{4,3,2,1,0:T(8,128)S(1)} %get-tuple-element.32), channel_id=1, source_target_pairs={{1,2},{3,4},{5,6},{7,8},{9,10},{11,12},{13,14},{2,1},{4,3},{6,5},{... | collective-permute-start | bytes 786440 | tf_op jit(solution)/shard_map/ppermute | solution.py:626

commit v3 on v2

--- a/solution.py
+++ b/solution.py
@@ -133,10 +133,10 @@
     )
 
 
-def pack_kernel(index_ref, guess_ref, class_ref, layer_ref, edge_ref, next_ref, near_ref, codes_ref, held, sems):
+def pack_kernel(guess_ref, class_ref, layer_ref, edge_ref, next_ref, near_ref, codes_ref, held, sems):
     layers, parts, shots, width, lanes = guess_ref.shape
     fields = parts * shots
-    odd = lax.rem(index_ref[0], 2) == 1
+    odd = lax.rem(lax.axis_index("gz"), 2) == 1
     planes = guess_ref.reshape(layers * fields, width, lanes)
     edge = jnp.where(odd, layers - 1, 0) * fields
     begin = jnp.where(odd, 0, layers - REACH) * fields
@@ -166,8 +166,8 @@
     next_ref[...] = near_ref[pl.ds(following, fields)]
 
 
-def orientation(index_ref, layers, depth_total):
-    index = index_ref[0]
+def orientation(layers, depth_total):
+    index = lax.axis_index("gz")
     odd = lax.rem(index, 2) == 1
     first_plane = index * layers
 
@@ -184,7 +184,6 @@
 
 def early_kernel(
     depth_total,
-    index_ref,
     wave_ref,
     damp_ref,
     cells_ref,
@@ -196,16 +195,23 @@
     field,
     start,
     tables,
+    shift_ref,
 ):
     _, layers, width, lanes = codes_ref.shape
     parts, shots = start.shape[2:4]
     fields = parts * shots
-    odd, place_of, inside = orientation(index_ref, layers, depth_total)
+    odd, place_of, inside = orientation(layers, depth_total)
     own_rows = own_ref.reshape(own_ref.shape[0] * width, lanes)
     edge_rows = edge_ref.reshape(edge_ref.shape[0] * width, lanes)
     near_rows = near_ref.reshape(near_ref.shape[0] * width, lanes)
     span = fields * width
     keep = edge_masks(shots, lanes)
+    diagonal = lax.broadcasted_iota(jnp.int32, shift_ref.shape[1:], 0) == lax.broadcasted_iota(
+        jnp.int32, shift_ref.shape[1:], 1
+    )
+    for part, value in enumerate(shift_of(wave_ref, damp_ref)):
+        shift_ref[part] = jnp.where(diagonal, value, 0.0)
+
     extra = REACH * fields
     for k in range(2):
         pick = jnp.where(odd, k, 1 - k)
@@ -246,7 +252,6 @@
 
 def image_kernel(
     depth_total,
-    index_ref,
     start,
     tables,
     first,
@@ -257,7 +262,7 @@
 ):
     _, width, _, shots, lanes = start.shape
     layers = start.shape[0] - 1
-    _, _, inside = orientation(index_ref, layers, depth_total)
+    _, _, inside = orientation(layers, depth_total)
     keep = edge_masks(shots, lanes)
     send_ref[0] = start[layers]
 
@@ -306,7 +311,7 @@
     refs = dict(zip(names, refs))
     first, second, far_ref = refs["first"], refs["second"], refs["far"]
     _, width, parts, shots, lanes = first.shape
-    odd, place_of, inside = orientation(refs["index"], layers, depth_total)
+    odd, place_of, inside = orientation(layers, depth_total)
     keep = edge_masks(shots, lanes)
     top = layers - 1 + stage
 
@@ -367,7 +372,7 @@
 
 
 def back_kernel(
-    index_ref, wave_ref, damp_ref, grams_ref, *rest
+    shift_ref, grams_ref, *rest
 ):
     basis_ref, hessenberg_ref = rest[-2:]
     layers, parts, shots, width, y = basis_ref.shape
@@ -478,7 +483,7 @@
         mix = mix - short.astype(jnp.float32)
     left = jnp.concatenate(pieces, axis=0)[:, 0:spread]
 
-    odd = lax.rem(index_ref[0], 2) == 1
+    odd = lax.rem(lax.axis_index("gz"), 2) == 1
     out_rows = basis_ref.reshape(layers * fields * width, y)
     spots = [
         (ref, spot)
@@ -520,19 +525,15 @@
             preferred_element_type=jnp.float32,
         )
 
-    shift_real, shift_imag = shift_of(wave_ref, damp_ref)
-    diagonal = lax.broadcasted_iota(jnp.int32, (wide, half), 0) == lax.broadcasted_iota(
-        jnp.int32, (wide, half), 1
-    )
     hessenberg_ref[0] = (
         times(lower_real, factor_real)
         + times(lower_imag, factor_imag)
-        + jnp.where(diagonal, shift_real, 0.0)
+        + shift_ref[0]
     )
     hessenberg_ref[1] = (
         times(lower_real, factor_imag)
         - times(lower_imag, factor_real)
-        + jnp.where(diagonal, shift_imag, 0.0)
+        + shift_ref[1]
     )
 
 
@@ -544,7 +545,6 @@
     rows = BLOCKS * fields
     span = width * lanes
     depth_total = devices * layers
-    index = lax.axis_index("gz").astype(jnp.int32).reshape(1)
     shot_cells = shot_cells.T
 
     smem = pl.BlockSpec(memory_space=pltpu.SMEM)
@@ -569,7 +569,7 @@
             float_shape(REACH * fields + 4, width, lanes),
             float_shape(2, layers, width, lanes),
         ),
-        in_specs=[smem, hbm, hbm, hbm],
+        in_specs=[hbm, hbm, hbm],
         out_specs=(vmem, vmem, vmem, vmem),
         scratch_shapes=[
             pltpu.VMEM((2, layers, width, lanes), jnp.int32),
@@ -578,11 +578,10 @@
         compiler_params=params,
         name="pack",
     )(
-        index,
         *(
             pltpu.with_memory_space_constraint(array, pltpu.HBM)
             for array in (initial_guess, velocity_class, layer_code)
-        ),
+        )
     )
     nearest = lax.ppermute(edge, "gz", far_pairs)
     second_far = lax.ppermute(following, "gz", far_pairs)
@@ -603,12 +602,13 @@
 
     products = float_shape(BLOCKS * rows, BLOCKS * rows)
     cost = pl.CostEstimate(flops=10_000_000, bytes_accessed=16_000_000, transcendentals=0)
-    common = (index, wavenumber, damping, shot_cells, wavelet)
-    field, start, own_tables = pl.pallas_call(
+    common = (wavenumber, damping, shot_cells, wavelet)
+    turned_shape = float_shape(2, 2 * shots, BLOCKS * shots)
+    field, start, own_tables, shift = pl.pallas_call(
         functools.partial(early_kernel, depth_total),
-        out_shape=(planes(layers + REACH), planes(layers + 1), tables(layers + 2)),
-        in_specs=[smem] * 5 + [vmem] * 4,
-        out_specs=(vmem,) * 3,
+        out_shape=(planes(layers + REACH), planes(layers + 1), tables(layers + 2), turned_shape),
+        in_specs=[smem] * 4 + [vmem] * 4,
+        out_specs=(vmem,) * 4,
         compiler_params=params,
         cost_estimate=cost,
         name="early",
@@ -616,13 +616,13 @@
     first, early_split, early_products, send = pl.pallas_call(
         functools.partial(image_kernel, depth_total),
         out_shape=(planes(layers - 1), split(layers - 3), products, planes(1)),
-        in_specs=[smem] + [vmem] * 2,
+        in_specs=[vmem] * 2,
         out_specs=(vmem,) * 4,
         scratch_shapes=[scratch(planes(layers - 3))],
         compiler_params=params,
         cost_estimate=cost,
         name="images",
-    )(index, start, own_tables)
+    )(start, own_tables)
     third_far = lax.ppermute(send, "gz", far_pairs)
     shapes = {
         "field": planes(1),
@@ -636,9 +636,9 @@
     }
 
     def run_stage(stage, far, old, extra, outs, temporaries):
-        inputs = {"index": index}
+        inputs = {}
         if stage < 2:
-            inputs = dict(zip(("index", "wave", "damp", "cells", "wavelet"), common))
+            inputs = dict(zip(("wave", "damp", "cells", "wavelet"), common))
         scalars = len(inputs)
         inputs["far"] = far
         inputs.update({name: array for name, (array, _) in old.items()})
@@ -711,13 +711,13 @@
         back_kernel,
         out_shape=(
             jax.ShapeDtypeStruct(initial_guess.shape, jnp.float32),
-            jax.ShapeDtypeStruct((2, 2 * shots, BLOCKS * shots), jnp.float32),
+            turned_shape,
         ),
-        in_specs=[smem] * 3 + [vmem] * 5,
+        in_specs=[vmem] * 6,
         out_specs=(vmem, vmem),
         compiler_params=params,
         name="back",
-    )(index, wavenumber, damping, grams, early_split, zero["split"], one["split"], two["split"])
+    )(shift, grams, early_split, zero["split"], one["split"], two["split"])
     return basis_two, jnp.swapaxes(turned, 1, 2)
 
 

time: 42.6 us -> 42.1 us (0.988)
  Pallas kernels: 14.8 us -> 14 us
    pallas_call x1, Pallas kernels: 3.39 us -> 2.86 us  [shards(): pl.pallas_call(back_kernel, out_shape=(jax.ShapeDtypeStruct(initial_guess...]
  transfers between devices with their start and end apart: 4 -> 4, of which waited for: 1 -> 1; matrix products, arithmetic and copies ran while one was open for 0% -> 0% of each run, Pallas kernels for 21% -> 20%
where the time goes in v3:
time: 42.1 us; the launch traced here: 41.9 us
  blocking collectives  23.9 us (57%)
  Pallas kernels  14 us (33%)
  starting transfers between devices  2.54 us (6%)
  between operations  0.76 us (2%)
  waiting for transfers between devices  0.65 us (2%)
    all_to_all x1, blocking collectives, shards(): grams = lax.all_to_all(grams, 'gz', 0, 0)  23.9 us
    pallas_call x3, Pallas kernels, run_stage(): pl.pallas_call(functools.partial(stage_kernel, stage, depth_total, layers...  5.31 us
    pallas_call x1, Pallas kernels, shards(): pl.pallas_call(functools.partial(early_kernel, depth_total), out_shape=(p...  3.08 us
    pallas_call x1, Pallas kernels, shards(): pl.pallas_call(back_kernel, out_shape=(jax.ShapeDtypeStruct(initial_guess...  2.86 us
    pallas_call x1, Pallas kernels, shards(): pl.pallas_call(functools.partial(image_kernel, depth_total), out_shape=(p...  1.43 us
    pallas_call x1, Pallas kernels, shards(): pl.pallas_call(pack_kernel, out_shape=(float_shape(fields + 2, width, lan...  1.36 us
  transfers between devices with their start and end apart: 4, of which 1 were waited for; matrix products, arithmetic and copies ran while one was open for 0% of the time, Pallas kernels for 20%

profile of v3, /device:TPU:0, one launch (start us, length us, event | category | flops | bytes accessed | tf_op | source)
XLA Modules:
  0.0 41.9 jit_solution(16415330861142623952)
XLA Ops:
  0.6 0.0 copy-start.1
  0.6 0.0 copy-start.3
  0.7 0.0 copy-start.2
  0.7 0.0 copy-start
  0.7 1.4 %pack.1 = (f32[18,32,128]{2,1,0:T(8,128)S(1)}, f32[16,32,128]{2,1,0:T(8,128)S(1)}, f32[52,32,128]{2,1,0:T(8,128)S(1)}, f32[2,4,32,128]{3,2,1,0:T(8,128)S(1)}) custom-call(f32[4,2,8,32,128]{4,3,2,1,0:T(8,128)} %guess_ref.1, s32[4,32,128]{2,1,0:T(8,128)} %class_ref.1, s32[4,32,128]{2,1,0:T(8,128)} %layer_ref.1), custom_call_target="tpu_custom_call" | custom-call | tf_op jit(solution)/shard_map/pack/pallas_call | solution.py:564
  2.0 0.5 %collective-permute-start = (f32[52,32,128]{2,1,0:T(8,128)S(1)}, f32[52,32,128]{2,1,0:T(8,128)S(1)}, u32[]{:S(2)}, u32[]{:S(2)}) collective-permute-start(f32[52,32,128]{2,1,0:T(8,128)S(1)} %get-tuple-element.29.own_ref), channel_id=1, source_target_pairs={{0,1},{2,3},{4,5},{6,7},{8,9},{10,11},{12,13},{14,15},{1,0},{3,2},... | collective-permute-start | bytes 2555912 | tf_op jit(solution)/shard_map/ppermute | solution.py:589
  2.6 0.7 %collective-permute-start.2 = (f32[18,32,128]{2,1,0:T(8,128)S(1)}, f32[18,32,128]{2,1,0:T(8,128)S(1)}, u32[]{:S(2)}, u32[]{:S(2)}) collective-permute-start(f32[18,32,128]{2,1,0:T(8,128)S(1)} %get-tuple-element.28.edge_ref), channel_id=1, source_target_pairs={{1,2},{3,4},{5,6},{7,8},{9,10},{11,12},{13,14},{2,1},{4,3},{6,5},{... | collective-permute-start | bytes 884744 | tf_op jit(solution)/shard_map/ppermute | solution.py:586
  3.2 0.7 %collective-permute-start.3 = (f32[16,32,128]{2,1,0:T(8,128)S(1)}, f32[16,32,128]{2,1,0:T(8,128)S(1)}, u32[]{:S(2)}, u32[]{:S(2)}) collective-permute-start(f32[16,32,128]{2,1,0:T(8,128)S(1)} %get-tuple-element.39), channel_id=1, source_target_pairs={{1,2},{3,4},{5,6},{7,8},{9,10},{11,12},{13,14},{2,1},{4,3},{6,5},{... | collective-permute-start | bytes 786440 | tf_op jit(solution)/shard_map/ppermute | solution.py:587
  3.9 0.6 %collective-permute-done.near_ref = f32[52,32,128]{2,1,0:T(8,128)S(1)} collective-permute-done((f32[52,32,128]{2,1,0:T(8,128)S(1)}, f32[52,32,128]{2,1,0:T(8,128)S(1)}, u32[]{:S(2)}, u32[]{:S(2)}) %collective-permute-start) | collective-permute-done | bytes 852000 | tf_op jit(solution)/shard_map/ppermute | solution.py:589
  4.6 0.0 copy-done.1
  4.6 0.0 copy-done.3
  4.6 0.0 copy-done.2
  4.6 0.0 copy-done
  4.6 3.1 %early.1 = (f32[7,32,2,8,128]{4,3,2,1,0:T(8,128)S(1)}, f32[5,32,2,8,128]{4,3,2,1,0:T(8,128)S(1)}, f32[6,4,32,128]{3,2,1,0:T(8,128)S(1)}, f32[2,16,24]{2,1,0:T(8,128)S(1)}) custom-call(f32[16]{0:T(128)S(1)} %copy-done.2, f32[8]{0:T(128)S(1)} %copy-done.3, s32[3,8]{1,0:T(4,128)S(1)} %bitcast.2, f32[2,8]{1,0:T(2,128)S(1)} %copy-done.1, ...), custom_call_target="tpu_custom_call" | custom-call | flops 10000000 | bytes 16000000 | tf_op jit(solution)/shard_map/early/pallas_call | solution.py:607
  7.7 1.4 %images.1 = (f32[3,32,2,8,128]{4,3,2,1,0:T(8,128)S(1)}, bf16[144,4096]{1,0:T(8,128)(2,1)S(1)}, f32[144,144]{1,0:T(8,128)S(1)}, f32[1,32,2,8,128]{4,3,2,1,0:T(8,128)S(1)}) custom-call(f32[5,32,2,8,128]{4,3,2,1,0:T(8,128)S(1)} %get-tuple-element.32.start.refs_7_.refs_8_, f32[6,4,32,128]{3,2,1,0:T(8,128)S(1)} %get-tuple-element.33.tables.refs_11_.refs_5_), custom_call_target="tpu_custom_call" | custom-call | flops 10000000 | bytes 16000000 | tf_op jit(solution)/shard_map/images/pallas_call | solution.py:616
  9.1 0.7 %collective-permute-start.1 = (f32[1,32,2,8,128]{4,3,2,1,0:T(8,128)S(1)}, f32[1,32,2,8,128]{4,3,2,1,0:T(8,128)S(1)}, u32[]{:S(2)}, u32[]{:S(2)}) collective-permute-start(f32[1,32,2,8,128]{4,3,2,1,0:T(8,128)S(1)} %get-tuple-element.34), channel_id=1, source_target_pairs={{1,2},{3,4},{5,6},{7,8},{9,10},{11,12},{13,14},{2,1},{4,3},{6,5},{... | collective-permute-start | bytes 786440 | tf_op jit(solution)/shard_map/ppermute | solution.py:626
  9.8 0.0 collective-permute-done.2.refs_4_.refs_13_
  9.8 2.0 %stage_0.1 = (f32[1,32,2,8,128]{4,3,2,1,0:T(8,128)S(1)}, f32[1,32,2,8,128]{4,3,2,1,0:T(8,128)S(1)}, f32[1,32,2,8,128]{4,3,2,1,0:T(8,128)S(1)}, bf16[144,4096]{1,0:T(8,128)(2,1)S(1)}, f32[144,144]{1,0:T(8,128)S(1)}) custom-call(f32[16]{0:T(128)S(1)} %copy-done.2, f32[8]{0:T(128)S(1)} %copy-done.3, s32[3,8]{1,0:T(4,128)S(1)} %bitcast.3, f32[2,8]{1,0:T(2,128)S(1)} %copy-done.1, ...), custom_call_target="tpu_custom_call" | custom-call | flops 10000000 | bytes 16000000 | tf_op jit(solution)/shard_map/stage_0/pallas_call | solution.py:646
  11.8 0.0 collective-permute-done.3.refs_4_
  11.8 2.0 %stage_1.1 = (f32[1,32,2,8,128]{4,3,2,1,0:T(8,128)S(1)}, f32[1,32,2,8,128]{4,3,2,1,0:T(8,128)S(1)}, f32[1,4,32,128]{3,2,1,0:T(8,128)S(1)}, bf16[144,4096]{1,0:T(8,128)(2,1)S(1)}, f32[144,144]{1,0:T(8,128)S(1)}) custom-call(f32[16]{0:T(128)S(1)} %copy-done.2, f32[8]{0:T(128)S(1)} %copy-done.3, s32[3,8]{1,0:T(4,128)S(1)} %bitcast.4, f32[2,8]{1,0:T(2,128)S(1)} %copy-done.1, ...), custom_call_target="tpu_custom_call" | custom-call | flops 10000000 | bytes 16000000 | tf_op jit(solution)/shard_map/stage_1/pallas_call | solution.py:646
  13.9 0.0 collective-permute-done.1.refs_0_
  13.9 1.2 %stage_2.1 = (bf16[144,4096]{1,0:T(8,128)(2,1)S(1)}, f32[16,8,128]{2,1,0:T(8,128)S(1)}) custom-call(f32[1,32,2,8,128]{4,3,2,1,0:T(8,128)S(1)} %collective-permute-done.1.refs_0_, f32[1,32,2,8,128]{4,3,2,1,0:T(8,128)S(1)} %get-tuple-element.38.refs_8_.refs_1_, f32[1,32,2,8,128]{4,3,2,1,0:T(8,128)S(1)} %get-tuple-element.43.refs_2_, ...), custom_call_target="tpu_custom_call" | custom-call | flops 10000000 | bytes 16000000 | tf_op jit(solution)/shard_map/stage_2/pallas_call | solution.py:646
  15.1 23.9 %all_to_all.5.grams_ref = f32[16,8,128]{2,1,0:T(8,128)S(1)} all-to-all(f32[16,8,128]{2,1,0:T(8,128)S(1)} %get-tuple-element.47), channel_id=1, replica_groups=mesh['freq'=2,'gz'=16] {'gz'}, dimensions={0} | all-to-all | bytes 131072 | tf_op jit(solution)/shard_map/all_to_all | solution.py:709
  39.0 2.9 %back.1 = (f32[4,2,8,32,128]{4,3,2,1,0:T(8,128)}, f32[2,16,24]{2,1,0:T(8,128)}) custom-call(f32[2,16,24]{2,1,0:T(8,128)S(1)} %get-tuple-element.31.shift_ref, f32[16,8,128]{2,1,0:T(8,128)S(1)} %all_to_all.5.grams_ref, bf16[144,4096]{1,0:T(8,128)(2,1)S(1)} %get-tuple-element.48.rest_0_, bf16[144,4096]{1,0:T(8,128)(2,1)S(1)} %get-tuple-element.49.rest_1_, ...), custom_call_target="tpu_custom_call" | custom-call | tf_op jit(solution)/shard_map/back/pallas_call | solution.py:710
Async XLA Ops:
  0.6 3.9 %copy-start.1 = (f32[2,8]{1,0:T(2,128)S(1)}, f32[2,8]{1,0:T(2,128)}, u32[]{:S(2)}) copy-start(f32[2,8]{1,0:T(2,128)} %refs_3_.3) | copy-start | bytes 196
  0.6 3.9 %copy-start.3 = (f32[8]{0:T(128)S(1)}, f32[8]{0:T(128)}, u32[]{:S(2)}) copy-start(f32[8]{0:T(128)} %refs_1_.3) | copy-start | bytes 100
  0.7 3.9 %copy-start.2 = (f32[16]{0:T(128)S(1)}, f32[16]{0:T(128)}, u32[]{:S(2)}) copy-start(f32[16]{0:T(128)} %refs_0_.3) | copy-start | bytes 196
  0.7 3.9 %copy-start = (s32[8,3]{0,1:T(4,128)S(1)}, s32[8,3]{0,1:T(4,128)}, u32[]{:S(2)}) copy-start(s32[8,3]{0,1:T(4,128)} %param.12) | copy-start | bytes 292
  2.0 2.5 %collective-permute-start = (f32[52,32,128]{2,1,0:T(8,128)S(1)}, f32[52,32,128]{2,1,0:T(8,128)S(1)}, u32[]{:S(2)}, u32[]{:S(2)}) collective-permute-start(f32[52,32,128]{2,1,0:T(8,128)S(1)} %get-tuple-element.29.own_ref), channel_id=1, source_target_pairs={{0,1},{2,3},{4,5},{6,7},{8,9},{10,11},{12,13},{14,15},{1,0},{3,2},... | collective-permute-start | bytes 2555912 | tf_op jit(solution)/shard_map/ppermute | solution.py:589
  2.6 7.2 %collective-permute-start.2 = (f32[18,32,128]{2,1,0:T(8,128)S(1)}, f32[18,32,128]{2,1,0:T(8,128)S(1)}, u32[]{:S(2)}, u32[]{:S(2)}) collective-permute-start(f32[18,32,128]{2,1,0:T(8,128)S(1)} %get-tuple-element.28.edge_ref), channel_id=1, source_target_pairs={{1,2},{3,4},{5,6},{7,8},{9,10},{11,12},{13,14},{2,1},{4,3},{6,5},{... | collective-permute-start | bytes 884744 | tf_op jit(solution)/shard_map/ppermute | solution.py:586
  3.2 8.6 %collective-permute-start.3 = (f32[16,32,128]{2,1,0:T(8,128)S(1)}, f32[16,32,128]{2,1,0:T(8,128)S(1)}, u32[]{:S(2)}, u32[]{:S(2)}) collective-permute-start(f32[16,32,128]{2,1,0:T(8,128)S(1)} %get-tuple-element.39), channel_id=1, source_target_pairs={{1,2},{3,4},{5,6},{7,8},{9,10},{11,12},{13,14},{2,1},{4,3},{6,5},{... | collective-permute-start | bytes 786440 | tf_op jit(solution)/shard_map/ppermute | solution.py:587
  9.1 4.8 %collective-permute-start.1 = (f32[1,32,2,8,128]{4,3,2,1,0:T(8,128)S(1)}, f32[1,32,2,8,128]{4,3,2,1,0:T(8,128)S(1)}, u32[]{:S(2)}, u32[]{:S(2)}) collective-permute-start(f32[1,32,2,8,128]{4,3,2,1,0:T(8,128)S(1)} %get-tuple-element.34), channel_id=1, source_target_pairs={{1,2},{3,4},{5,6},{7,8},{9,10},{11,12},{13,14},{2,1},{4,3},{6,5},{... | collective-permute-start | bytes 786440 | tf_op jit(solution)/shard_map/ppermute | solution.py:626

commit v4 on v3

--- a/solution.py
+++ b/solution.py
@@ -110,24 +110,22 @@
                 start[place, column, part, s : s + 1, :] += jnp.where(hit, wavelet_ref[part, s], 0.0)
 
 
-def split_plane(sources, split_ref, spot_plane):
-    width, _, shots, lanes = sources[0][0].shape[1:]
-    rows = BLOCKS * 2 * shots
+def split_level(source, level, split_ref):
+    ref, plane = source
+    width, parts, shots, lanes = ref.shape[1:]
+    fields = parts * shots
     for column in range(width):
-        pieces = [ref[plane, column, part] for part in range(2) for ref, plane in sources]
-        begin = (spot_plane * width + column) * lanes
-        for pair in range(BLOCKS):
-            value = jnp.concatenate(pieces[2 * pair : 2 * pair + 2], axis=0)
-            for part in range(3):
-                short = value.astype(jnp.bfloat16)
-                row = part * rows + 2 * shots * pair
-                split_ref[row : row + 2 * shots, begin : begin + lanes] = short
-                if part < 2:
-                    value = value - short.astype(jnp.float32)
-
-
-def products_of(split_ref, spot_plane, span):
-    chunk = split_ref[:, spot_plane * span : (spot_plane + 1) * span]
+        value = ref[plane, column].reshape(fields, lanes)
+        for part in range(3):
+            short = value.astype(jnp.bfloat16)
+            row = (part * BLOCKS + level) * fields
+            split_ref[row : row + fields, column * lanes : (column + 1) * lanes] = short
+            if part < 2:
+                value = value - short.astype(jnp.float32)
+
+
+def products_of(split_ref):
+    chunk = split_ref[...]
     return lax.dot_general(
         chunk, chunk, (((1,), (1,)), ((), ())), preferred_element_type=jnp.float32
     )
@@ -286,24 +284,31 @@
             1.0 / 30.0,
             keep,
         )
-        split_plane(((start, k + 2), (first, k + 1), (second, k)), split_ref, k)
-        products += products_of(split_ref, k, width * lanes)
+        for level, source in enumerate(((start, k + 2), (first, k + 1), (second, k))):
+            split_level(source, level, split_ref)
+        products += products_of(split_ref)
     products_ref[...] = products
 
 
 def pack_gram(products, shots, cells):
-    rows = 2 * BLOCKS * shots
-    half = rows // 2
+    fields = 2 * shots
+    rows = BLOCKS * fields
     summed = products[0:rows] + products[rows : 2 * rows] + products[2 * rows : 3 * rows]
     summed = summed[:, 0:rows] + summed[:, rows : 2 * rows] + summed[:, 2 * rows : 3 * rows]
     summed = summed * (1.0 / cells)
-    real = summed[0:half, 0:half] + summed[half:rows, half:rows]
-    imag = summed[0:half, half:rows] - summed[half:rows, 0:half]
+    summed = jnp.concatenate([summed, jnp.zeros((rows, 128 - rows), jnp.float32)], axis=1)
+    lane = lax.broadcasted_iota(jnp.int32, (shots, 128), 1)
     blocks = []
-    for i, j in PAIRS:
-        for values in (real, imag):
-            blocks.append(values[i * shots : (i + 1) * shots, j * shots : (j + 1) * shots])
-    blocks.append(jnp.zeros((shots, 128 - 2 * len(PAIRS) * shots), jnp.float32))
+    for level in range(BLOCKS):
+        real_rows = summed[level * fields : level * fields + shots]
+        imag_rows = summed[level * fields + shots : (level + 1) * fields]
+        both = jnp.where(
+            lax.rem(lane, fields) < shots,
+            real_rows + pltpu.roll(imag_rows, 128 - shots, 1),
+            real_rows - pltpu.roll(imag_rows, shots, 1),
+        )
+        blocks.append(both[:, level * fields : rows])
+    blocks.append(jnp.zeros((shots, 128 - len(PAIRS) * fields), jnp.float32))
     return jnp.concatenate(blocks, axis=1)
 
 
@@ -361,8 +366,14 @@
         keep,
     )
     split_ref = refs["split"]
-    split_plane((old("start_a"), old("first_b"), (second, 0)), split_ref, 0)
-    products = refs["products_in"][...] + products_of(split_ref, 0, width * lanes)
+    levels = (old("start_a"), old("first_b"), (second, 0))
+    for level, source in enumerate(levels):
+        if stage < 2 or level == 2:
+            split_level(source, level, split_ref)
+    if stage == 1:
+        for level, source in enumerate((old("start_b"), (first, 0))):
+            split_level(source, level, refs["next_split"])
+    products = refs["products_in"][...] + products_of(split_ref)
     if stage < 2:
         refs["products"][...] = products
     else:
@@ -394,9 +405,10 @@
     sub = lax.broadcasted_iota(jnp.int32, (tile, lanes), 0)
     wide_lane = lax.broadcasted_iota(jnp.int32, (tile, 2 * lanes), 1)
     wide_sub = lax.broadcasted_iota(jnp.int32, (tile, 2 * lanes), 0)
+    column = lax.rem(wide_lane, rows) // fields * tile + lax.rem(wide_lane, tile)
     real, imag = [], []
     for t in range(tiles):
-        match = (wide_lane < spread) & (lax.rem(wide_lane, half) == wide_sub + t * tile)
+        match = (wide_lane < spread) & (column == wide_sub + t * tile)
         unit = jnp.where(match, 1.0, 0.0).astype(jnp.float32)
         blank = jnp.zeros((tile, lanes), jnp.float32)
         parts_of = []
@@ -430,8 +442,7 @@
             pivot = jnp.broadcast_to(own_real[r : r + 1], shape)
             pivots.append(pivot)
             inverse = pl.reciprocal(pivot, approx=True)
-            for _ in range(2):
-                inverse = inverse * (2.0 - pivot * inverse)
+            inverse = inverse * (2.0 - pivot * inverse)
             scaled = {}
             for t in range(owner, tiles):
                 column_real, column_imag = [value * inverse for value in ahead[t, r]]
@@ -468,7 +479,7 @@
         imag[t] = imag[t] * scales
 
     last_real, last_imag = real[tiles - 1], imag[tiles - 1]
-    first_half = lax.rem(wide_lane, rows) < half
+    first_half = lax.rem(wide_lane, fields) < tile
     mix = jnp.concatenate(
         [
             jnp.where(first_half, last_real, last_imag),
@@ -513,8 +524,10 @@
     upper = row_index <= column_index + tile
     factor_real = jnp.where(upper, full_real[:, spread + tile : spread + half], 0.0)
     factor_imag = jnp.where(upper, full_imag[:, spread + tile : spread + half], 0.0)
-    lower_real = full_real[0:wide, 0:wide]
-    lower_imag = full_imag[0:wide, 0:wide]
+    lower_real, lower_imag = [
+        jnp.concatenate([value[0:wide, 0:tile], value[0:wide, fields : fields + tile]], axis=1)
+        for value in (full_real, full_imag)
+    ]
 
     def times(left, right):
         return lax.dot_general(
@@ -631,6 +644,7 @@
         "second": planes(1),
         "tables": tables(1),
         "split": split(1),
+        "next_split": split(1),
         "products": products,
         "grams": float_shape(devices, shots, 128),
     }
@@ -656,6 +670,7 @@
             in_specs=[smem] * scalars + [vmem] * (len(inputs) - scalars),
             out_specs=(vmem,) * len(outs),
             scratch_shapes=[scratch(shapes[name]) for name in temporaries],
+            input_output_aliases={len(inputs) - 1: 0} if stage == 2 else {},
             compiler_params=params,
             cost_estimate=cost,
             name="stage_%d" % stage,
@@ -689,7 +704,7 @@
             "first_b": (zero["first"], 0),
         },
         {"own_tables": own_tables, "products_in": zero["products"], "nearest": nearest},
-        ["start", "first", "tables", "split", "products"],
+        ["start", "first", "tables", "split", "products", "next_split"],
         ["field", "second"],
     )
     two = run_stage(
@@ -701,7 +716,7 @@
             "first_a": (zero["first"], 0),
             "first_b": (one["first"], 0),
         },
-        {"own_tables": own_tables, "far_tables": one["tables"], "products_in": one["products"]},
+        {"own_tables": own_tables, "far_tables": one["tables"], "products_in": one["products"], "begun": one["next_split"]},
         ["split", "grams"],
         ["first", "second"],
     )

time: 42.1 us -> 41.9 us (level)
  transfers between devices with their start and end apart: 4 -> 4, of which waited for: 1 -> 1; matrix products, arithmetic and copies ran while one was open for 0% -> 0% of each run, Pallas kernels for 20% -> 21%
where the time goes in v4:
time: 41.9 us; the launch traced here: 41.6 us
  blocking collectives  23.7 us (57%)
  Pallas kernels  14 us (33%)
  starting transfers between devices  2.54 us (6%)
  between operations  0.76 us (2%)
  waiting for transfers between devices  0.65 us (2%)
    all_to_all x1, blocking collectives, shards(): grams = lax.all_to_all(grams, 'gz', 0, 0)  23.7 us
    pallas_call x3, Pallas kernels, run_stage(): pl.pallas_call(functools.partial(stage_kernel, stage, depth_total, layers...  5.23 us
    pallas_call x1, Pallas kernels, shards(): pl.pallas_call(functools.partial(early_kernel, depth_total), out_shape=(p...  3.08 us
    pallas_call x1, Pallas kernels, shards(): pl.pallas_call(back_kernel, out_shape=(jax.ShapeDtypeStruct(initial_guess...  2.88 us
    pallas_call x1, Pallas kernels, shards(): pl.pallas_call(functools.partial(image_kernel, depth_total), out_shape=(p...  1.44 us
    pallas_call x1, Pallas kernels, shards(): pl.pallas_call(pack_kernel, out_shape=(float_shape(fields + 2, width, lan...  1.36 us
  transfers between devices with their start and end apart: 4, of which 1 were waited for; matrix products, arithmetic and copies ran while one was open for 0% of the time, Pallas kernels for 21%

profile of v4, /device:TPU:0, one launch (start us, length us, event | category | flops | bytes accessed | tf_op | source)
XLA Modules:
  0.0 41.6 jit_solution(1630387512112513035)
XLA Ops:
  0.6 0.0 copy-start.1
  0.6 0.0 copy-start.3
  0.7 0.0 copy-start.2
  0.7 0.0 copy-start
  0.7 1.4 %pack.1 = (f32[18,32,128]{2,1,0:T(8,128)S(1)}, f32[16,32,128]{2,1,0:T(8,128)S(1)}, f32[52,32,128]{2,1,0:T(8,128)S(1)}, f32[2,4,32,128]{3,2,1,0:T(8,128)S(1)}) custom-call(f32[4,2,8,32,128]{4,3,2,1,0:T(8,128)} %guess_ref.1, s32[4,32,128]{2,1,0:T(8,128)} %class_ref.1, s32[4,32,128]{2,1,0:T(8,128)} %layer_ref.1), custom_call_target="tpu_custom_call" | custom-call | tf_op jit(solution)/shard_map/pack/pallas_call | solution.py:577
  2.0 0.5 %collective-permute-start = (f32[52,32,128]{2,1,0:T(8,128)S(1)}, f32[52,32,128]{2,1,0:T(8,128)S(1)}, u32[]{:S(2)}, u32[]{:S(2)}) collective-permute-start(f32[52,32,128]{2,1,0:T(8,128)S(1)} %get-tuple-element.30.own_ref), channel_id=1, source_target_pairs={{0,1},{2,3},{4,5},{6,7},{8,9},{10,11},{12,13},{14,15},{1,0},{3,2},... | collective-permute-start | bytes 2555912 | tf_op jit(solution)/shard_map/ppermute | solution.py:602
  2.6 0.7 %collective-permute-start.2 = (f32[18,32,128]{2,1,0:T(8,128)S(1)}, f32[18,32,128]{2,1,0:T(8,128)S(1)}, u32[]{:S(2)}, u32[]{:S(2)}) collective-permute-start(f32[18,32,128]{2,1,0:T(8,128)S(1)} %get-tuple-element.29.edge_ref), channel_id=1, source_target_pairs={{1,2},{3,4},{5,6},{7,8},{9,10},{11,12},{13,14},{2,1},{4,3},{6,5},{... | collective-permute-start | bytes 884744 | tf_op jit(solution)/shard_map/ppermute | solution.py:599
  3.2 0.7 %collective-permute-start.3 = (f32[16,32,128]{2,1,0:T(8,128)S(1)}, f32[16,32,128]{2,1,0:T(8,128)S(1)}, u32[]{:S(2)}, u32[]{:S(2)}) collective-permute-start(f32[16,32,128]{2,1,0:T(8,128)S(1)} %get-tuple-element.40), channel_id=1, source_target_pairs={{1,2},{3,4},{5,6},{7,8},{9,10},{11,12},{13,14},{2,1},{4,3},{6,5},{... | collective-permute-start | bytes 786440 | tf_op jit(solution)/shard_map/ppermute | solution.py:600
  3.9 0.6 %collective-permute-done.near_ref = f32[52,32,128]{2,1,0:T(8,128)S(1)} collective-permute-done((f32[52,32,128]{2,1,0:T(8,128)S(1)}, f32[52,32,128]{2,1,0:T(8,128)S(1)}, u32[]{:S(2)}, u32[]{:S(2)}) %collective-permute-start) | collective-permute-done | bytes 852000 | tf_op jit(solution)/shard_map/ppermute | solution.py:602
  4.6 0.0 copy-done.1
  4.6 0.0 copy-done.3
  4.6 0.0 copy-done.2
  4.6 0.0 copy-done
  4.6 3.1 %early.1 = (f32[7,32,2,8,128]{4,3,2,1,0:T(8,128)S(1)}, f32[5,32,2,8,128]{4,3,2,1,0:T(8,128)S(1)}, f32[6,4,32,128]{3,2,1,0:T(8,128)S(1)}, f32[2,16,24]{2,1,0:T(8,128)S(1)}) custom-call(f32[16]{0:T(128)S(1)} %copy-done.2, f32[8]{0:T(128)S(1)} %copy-done.3, s32[3,8]{1,0:T(4,128)S(1)} %bitcast.2, f32[2,8]{1,0:T(2,128)S(1)} %copy-done.1, ...), custom_call_target="tpu_custom_call" | custom-call | flops 10000000 | bytes 16000000 | tf_op jit(solution)/shard_map/early/pallas_call | solution.py:620
  7.7 1.4 %images.1 = (f32[3,32,2,8,128]{4,3,2,1,0:T(8,128)S(1)}, bf16[144,4096]{1,0:T(8,128)(2,1)S(1)}, f32[144,144]{1,0:T(8,128)S(1)}, f32[1,32,2,8,128]{4,3,2,1,0:T(8,128)S(1)}) custom-call(f32[5,32,2,8,128]{4,3,2,1,0:T(8,128)S(1)} %get-tuple-element.33.start.refs_7_.refs_8_, f32[6,4,32,128]{3,2,1,0:T(8,128)S(1)} %get-tuple-element.34.tables.refs_11_.refs_5_), custom_call_target="tpu_custom_call" | custom-call | flops 10000000 | bytes 16000000 | tf_op jit(solution)/shard_map/images/pallas_call | solution.py:629
  9.1 0.7 %collective-permute-start.1 = (f32[1,32,2,8,128]{4,3,2,1,0:T(8,128)S(1)}, f32[1,32,2,8,128]{4,3,2,1,0:T(8,128)S(1)}, u32[]{:S(2)}, u32[]{:S(2)}) collective-permute-start(f32[1,32,2,8,128]{4,3,2,1,0:T(8,128)S(1)} %get-tuple-element.35), channel_id=1, source_target_pairs={{1,2},{3,4},{5,6},{7,8},{9,10},{11,12},{13,14},{2,1},{4,3},{6,5},{... | collective-permute-start | bytes 786440 | tf_op jit(solution)/shard_map/ppermute | solution.py:639
  9.8 0.0 collective-permute-done.2.refs_4_.refs_13_
  9.8 2.0 %stage_0.1 = (f32[1,32,2,8,128]{4,3,2,1,0:T(8,128)S(1)}, f32[1,32,2,8,128]{4,3,2,1,0:T(8,128)S(1)}, f32[1,32,2,8,128]{4,3,2,1,0:T(8,128)S(1)}, bf16[144,4096]{1,0:T(8,128)(2,1)S(1)}, f32[144,144]{1,0:T(8,128)S(1)}) custom-call(f32[16]{0:T(128)S(1)} %copy-done.2, f32[8]{0:T(128)S(1)} %copy-done.3, s32[3,8]{1,0:T(4,128)S(1)} %bitcast.3, f32[2,8]{1,0:T(2,128)S(1)} %copy-done.1, ...), custom_call_target="tpu_custom_call" | custom-call | flops 10000000 | bytes 16000000 | tf_op jit(solution)/shard_map/stage_0/pallas_call | solution.py:660
  11.8 0.0 collective-permute-done.3.refs_4_
  11.9 2.2 %stage_1.1 = (f32[1,32,2,8,128]{4,3,2,1,0:T(8,128)S(1)}, f32[1,32,2,8,128]{4,3,2,1,0:T(8,128)S(1)}, f32[1,4,32,128]{3,2,1,0:T(8,128)S(1)}, bf16[144,4096]{1,0:T(...) custom-call(f32[16]{0:T(128)S(1)} %copy-done.2, f32[8]{0:T(128)S(1)} %copy-done.3, ...), custom_call_target="tpu_custom_call" | custom-call | flops 10000000 | bytes 16000000 | tf_op jit(solution)/shard_map/stage_1/pallas_call | solution.py:660
  14.1 0.0 collective-permute-done.1.refs_0_
  14.1 1.0 %stage_2.1 = (bf16[144,4096]{1,0:T(8,128)(2,1)S(1)}, f32[16,8,128]{2,1,0:T(8,128)S(1)}) custom-call(f32[1,32,2,8,128]{4,3,2,1,0:T(8,128)S(1)} %collective-permute-done.1.refs_0_, f32[1,32,2,8,128]{4,3,2,1,0:T(8,128)S(1)} %get-tuple-element.39.refs_8_.refs_1_, f32[1,32,2,8,128]{4,3,2,1,0:T(8,128)S(1)} %get-tuple-element.44.refs_2_, ...), custom_call_target="tpu_custom_call", output_to_operand_aliasing={{0}: (8, {})} | custom-call | flops 10000000 | bytes 16000000 | tf_op jit(solution)/shard_map/stage_2/pallas_call | solution.py:660
  15.1 23.7 %all_to_all.5.grams_ref = f32[16,8,128]{2,1,0:T(8,128)S(1)} all-to-all(f32[16,8,128]{2,1,0:T(8,128)S(1)} %get-tuple-element.49), channel_id=1, replica_groups=mesh['freq'=2,'gz'=16] {'gz'}, dimensions={0} | all-to-all | bytes 131072 | tf_op jit(solution)/shard_map/all_to_all | solution.py:724
  38.8 2.9 %back.1 = (f32[4,2,8,32,128]{4,3,2,1,0:T(8,128)}, f32[2,16,24]{2,1,0:T(8,128)}) custom-call(f32[2,16,24]{2,1,0:T(8,128)S(1)} %get-tuple-element.32.shift_ref, f32[16,8,128]{2,1,0:T(8,128)S(1)} %all_to_all.5.grams_ref, bf16[144,4096]{1,0:T(8,128)(2,1)S(1)} %get-tuple-element.50.rest_0_, bf16[144,4096]{1,0:T(8,128)(2,1)S(1)} %get-tuple-element.51.rest_1_, ...), custom_call_target="tpu_custom_call" | custom-call | tf_op jit(solution)/shard_map/back/pallas_call | solution.py:725
Async XLA Ops:
  0.6 3.9 %copy-start.1 = (f32[2,8]{1,0:T(2,128)S(1)}, f32[2,8]{1,0:T(2,128)}, u32[]{:S(2)}) copy-start(f32[2,8]{1,0:T(2,128)} %refs_3_.3) | copy-start | bytes 196
  0.6 3.9 %copy-start.3 = (f32[8]{0:T(128)S(1)}, f32[8]{0:T(128)}, u32[]{:S(2)}) copy-start(f32[8]{0:T(128)} %refs_1_.3) | copy-start | bytes 100
  0.7 3.9 %copy-start.2 = (f32[16]{0:T(128)S(1)}, f32[16]{0:T(128)}, u32[]{:S(2)}) copy-start(f32[16]{0:T(128)} %refs_0_.3) | copy-start | bytes 196
  0.7 3.9 %copy-start = (s32[8,3]{0,1:T(4,128)S(1)}, s32[8,3]{0,1:T(4,128)}, u32[]{:S(2)}) copy-start(s32[8,3]{0,1:T(4,128)} %param.12) | copy-start | bytes 292
  2.0 2.5 %collective-permute-start = (f32[52,32,128]{2,1,0:T(8,128)S(1)}, f32[52,32,128]{2,1,0:T(8,128)S(1)}, u32[]{:S(2)}, u32[]{:S(2)}) collective-permute-start(f32[52,32,128]{2,1,0:T(8,128)S(1)} %get-tuple-element.30.own_ref), channel_id=1, source_target_pairs={{0,1},{2,3},{4,5},{6,7},{8,9},{10,11},{12,13},{14,15},{1,0},{3,2},... | collective-permute-start | bytes 2555912 | tf_op jit(solution)/shard_map/ppermute | solution.py:602
  2.6 7.2 %collective-permute-start.2 = (f32[18,32,128]{2,1,0:T(8,128)S(1)}, f32[18,32,128]{2,1,0:T(8,128)S(1)}, u32[]{:S(2)}, u32[]{:S(2)}) collective-permute-start(f32[18,32,128]{2,1,0:T(8,128)S(1)} %get-tuple-element.29.edge_ref), channel_id=1, source_target_pairs={{1,2},{3,4},{5,6},{7,8},{9,10},{11,12},{13,14},{2,1},{4,3},{6,5},{... | collective-permute-start | bytes 884744 | tf_op jit(solution)/shard_map/ppermute | solution.py:599
  3.2 8.6 %collective-permute-start.3 = (f32[16,32,128]{2,1,0:T(8,128)S(1)}, f32[16,32,128]{2,1,0:T(8,128)S(1)}, u32[]{:S(2)}, u32[]{:S(2)}) collective-permute-start(f32[16,32,128]{2,1,0:T(8,128)S(1)} %get-tuple-element.40), channel_id=1, source_target_pairs={{1,2},{3,4},{5,6},{7,8},{9,10},{11,12},{13,14},{2,1},{4,3},{6,5},{... | collective-permute-start | bytes 786440 | tf_op jit(solution)/shard_map/ppermute | solution.py:600
  9.1 4.9 %collective-permute-start.1 = (f32[1,32,2,8,128]{4,3,2,1,0:T(8,128)S(1)}, f32[1,32,2,8,128]{4,3,2,1,0:T(8,128)S(1)}, u32[]{:S(2)}, u32[]{:S(2)}) collective-permute-start(f32[1,32,2,8,128]{4,3,2,1,0:T(8,128)S(1)} %get-tuple-element.35), channel_id=1, source_target_pairs={{1,2},{3,4},{5,6},{7,8},{9,10},{11,12},{13,14},{2,1},{4,3},{6,5},{... | collective-permute-start | bytes 786440 | tf_op jit(solution)/shard_map/ppermute | solution.py:639

commit v5 on v4

--- a/solution.py
+++ b/solution.py
@@ -30,7 +30,7 @@
 
 
 def stencil_plane(sources, target, table, scale, keep):
-    (low, low_plane), (mid, mid_plane), (high, high_plane) = sources
+    (low, low_plane), (mid, mid_plane), high = sources
     out, out_plane = target
     table_ref, table_plane, kind = table
     width = table_ref.shape[2]
@@ -40,7 +40,9 @@
         center, away = [], []
         for part in range(2):
             v = mid[mid_plane, column, part]
-            d = low[low_plane, column, part] + high[high_plane, column, part]
+            d = low[low_plane, column, part]
+            if high is not None:
+                d = d + high[0][high[1], column, part]
             center.append(v)
             away.append(d + 3.0 * v)
         return center, away
@@ -71,6 +73,22 @@
         before_v, before_u, here_v, here_u = here_v, here_u, after_v, after_u
 
 
+def couple_plane(source, target, scale, keep):
+    ref, plane = source
+    out, out_plane = target
+    width = ref.shape[1]
+    left, right = keep
+    blank = jnp.zeros(ref.shape[3:], jnp.float32)
+    for part in range(2):
+        before, here = blank, ref[plane, 0, part]
+        for column in range(width):
+            after = ref[plane, column + 1, part] if column + 1 < width else blank
+            wide = (before + after) + 3.0 * here
+            sides = pltpu.roll(wide, 1, 1) * left + pltpu.roll(wide, 127, 1) * right
+            out[out_plane, column, part] = scale * (3.0 * wide + 5.0 * here + sides)
+            before, here = here, after
+
+
 def bring(rows, first_row, field, plane):
     width, parts, shots = field.shape[1:4]
     for column in range(width):
@@ -110,12 +128,15 @@
                 start[place, column, part, s : s + 1, :] += jnp.where(hit, wavelet_ref[part, s], 0.0)
 
 
-def split_level(source, level, split_ref):
+def split_level(source, level, split_ref, more=None):
     ref, plane = source
     width, parts, shots, lanes = ref.shape[1:]
     fields = parts * shots
     for column in range(width):
-        value = ref[plane, column].reshape(fields, lanes)
+        value = ref[plane, column]
+        if more is not None:
+            value = value + more[0][more[1], column]
+        value = value.reshape(fields, lanes)
         for part in range(3):
             short = value.astype(jnp.bfloat16)
             row = (part * BLOCKS + level) * fields
@@ -257,12 +278,14 @@
     products_ref,
     send_ref,
     second,
+    coupled,
 ):
     _, width, _, shots, lanes = start.shape
     layers = start.shape[0] - 1
     _, _, inside = orientation(layers, depth_total)
     keep = edge_masks(shots, lanes)
-    send_ref[0] = start[layers]
+    couple_plane((start, layers), (coupled, 0), -1.0 / 30.0, keep)
+    couple_plane((coupled, 0), (send_ref, 0), -1.0 / 30.0, keep)
 
     def first_plane(j, carry):
         stencil_plane(
@@ -315,6 +338,8 @@
 def stage_kernel(stage, depth_total, layers, names, places, *refs):
     refs = dict(zip(names, refs))
     first, second, far_ref = refs["first"], refs["second"], refs["far"]
+    field, start = refs["field"], refs["start"]
+    own_tables = refs["own_tables"]
     _, width, parts, shots, lanes = first.shape
     odd, place_of, inside = orientation(layers, depth_total)
     keep = edge_masks(shots, lanes)
@@ -323,63 +348,72 @@
     def old(name):
         return (refs[name], places[name])
 
-    if stage == 2:
-        start = far_ref
-        first_table = (refs["far_tables"], 0, 1)
+    if stage == 0:
+        start_table = (own_tables, top + 2, 0)
     else:
-        field, start = refs["field"], refs["start"]
-        first_table = (refs["own_tables"], top + 1, 1)
-        if stage == 0:
-            start_table = (refs["own_tables"], top + 2, 0)
-        else:
-            fill_tables(
-                refs["tables"],
-                0,
-                refs["nearest"][parts * shots],
-                refs["nearest"][parts * shots + 1],
-                inside(jnp.int32(top)),
-                refs["wave"],
-                refs["damp"],
-            )
-            start_table = (refs["tables"], 0, 0)
-        bring(far_ref.reshape(far_ref.shape[0] * width, lanes), 0, field, 0)
-        stencil_plane(
-            (old("field_a"), old("field_b"), (field, 0)),
-            (start, 0),
-            start_table,
-            inside(jnp.int32(top)) * (-1.0 / 30.0),
-            keep,
-        )
-        add_sources(start, top, place_of, refs["cells"], refs["wavelet"])
+        fill_tables(
+            refs["tables"],
+            0,
+            refs["nearest"][parts * shots],
+            refs["nearest"][parts * shots + 1],
+            inside(jnp.int32(top)),
+            refs["wave"],
+            refs["damp"],
+        )
+        start_table = (refs["tables"], 0, 0)
+    bring(far_ref.reshape(far_ref.shape[0] * width, lanes), 0, field, 0)
+    stencil_plane(
+        (old("field_a"), old("field_b"), (field, 0)),
+        (start, 0),
+        start_table,
+        inside(jnp.int32(top)) * (-1.0 / 30.0),
+        keep,
+    )
+    add_sources(start, top, place_of, refs["cells"], refs["wavelet"])
     stencil_plane(
         (old("start_a"), old("start_b"), (start, 0)),
         (first, 0),
-        first_table,
-        inside(jnp.int32(top - 1)) * (1.0 / 30.0),
+        (own_tables, top + 1, 1),
+        1.0 / 30.0,
         keep,
     )
     stencil_plane(
         (old("first_a"), old("first_b"), (first, 0)),
         (second, 0),
-        (refs["own_tables"], top, 1),
+        (own_tables, top, 1),
         1.0 / 30.0,
         keep,
     )
+    if stage == 1:
+        outer, base = refs["outer"], refs["base"]
+        stencil_plane(
+            (old("start_b"), (start, 0), None),
+            (outer, 0),
+            (refs["tables"], 0, 1),
+            inside(jnp.int32(top)) * (1.0 / 30.0),
+            keep,
+        )
+        stencil_plane(
+            (old("first_b"), (first, 0), (outer, 0)),
+            (base, 0),
+            (own_tables, top + 1, 1),
+            1.0 / 30.0,
+            keep,
+        )
     split_ref = refs["split"]
-    levels = (old("start_a"), old("first_b"), (second, 0))
-    for level, source in enumerate(levels):
-        if stage < 2 or level == 2:
-            split_level(source, level, split_ref)
+    for level, source in enumerate((old("start_a"), old("first_b"), (second, 0))):
+        split_level(source, level, split_ref)
     if stage == 1:
         for level, source in enumerate((old("start_b"), (first, 0))):
             split_level(source, level, refs["next_split"])
-    products = refs["products_in"][...] + products_of(split_ref)
-    if stage < 2:
-        refs["products"][...] = products
-    else:
-        packed = pack_gram(products, shots, float(depth_total * width * lanes))
-        for copy in range(refs["grams"].shape[0]):
-            refs["grams"][copy] = packed
+    refs["products"][...] = refs["products_in"][...] + products_of(split_ref)
+
+
+def last_kernel(cells, far_ref, base_ref, products_ref, begun_ref, split_ref, grams_ref):
+    split_level((base_ref, 0), 2, split_ref, (far_ref, 0))
+    packed = pack_gram(products_ref[...] + products_of(split_ref), far_ref.shape[3], cells)
+    for copy in range(grams_ref.shape[0]):
+        grams_ref[copy] = packed
 
 
 def back_kernel(
@@ -631,7 +665,7 @@
         out_shape=(planes(layers - 1), split(layers - 3), products, planes(1)),
         in_specs=[vmem] * 2,
         out_specs=(vmem,) * 4,
-        scratch_shapes=[scratch(planes(layers - 3))],
+        scratch_shapes=[scratch(planes(layers - 3)), scratch(planes(1))],
         compiler_params=params,
         cost_estimate=cost,
         name="images",
@@ -645,14 +679,13 @@
         "tables": tables(1),
         "split": split(1),
         "next_split": split(1),
+        "outer": planes(1),
+        "base": planes(1),
         "products": products,
-        "grams": float_shape(devices, shots, 128),
     }
 
     def run_stage(stage, far, old, extra, outs, temporaries):
-        inputs = {}
-        if stage < 2:
-            inputs = dict(zip(("wave", "damp", "cells", "wavelet"), common))
+        inputs = dict(zip(("wave", "damp", "cells", "wavelet"), common))
         scalars = len(inputs)
         inputs["far"] = far
         inputs.update({name: array for name, (array, _) in old.items()})
@@ -670,7 +703,6 @@
             in_specs=[smem] * scalars + [vmem] * (len(inputs) - scalars),
             out_specs=(vmem,) * len(outs),
             scratch_shapes=[scratch(shapes[name]) for name in temporaries],
-            input_output_aliases={len(inputs) - 1: 0} if stage == 2 else {},
             compiler_params=params,
             cost_estimate=cost,
             name="stage_%d" % stage,
@@ -704,23 +736,18 @@
             "first_b": (zero["first"], 0),
         },
         {"own_tables": own_tables, "products_in": zero["products"], "nearest": nearest},
-        ["start", "first", "tables", "split", "products", "next_split"],
-        ["field", "second"],
-    )
-    two = run_stage(
-        2,
-        third_far,
-        {
-            "start_a": (zero["start"], 0),
-            "start_b": (one["start"], 0),
-            "first_a": (zero["first"], 0),
-            "first_b": (one["first"], 0),
-        },
-        {"own_tables": own_tables, "far_tables": one["tables"], "products_in": one["products"], "begun": one["next_split"]},
-        ["split", "grams"],
-        ["first", "second"],
-    )
-    grams = two["grams"]
+        ["base", "split", "products", "next_split"],
+        ["field", "start", "first", "second", "tables", "outer"],
+    )
+    last_split, grams = pl.pallas_call(
+        functools.partial(last_kernel, float(depth_total * span)),
+        out_shape=(split(1), float_shape(devices, shots, 128)),
+        in_specs=[vmem] * 4,
+        out_specs=(vmem, vmem),
+        input_output_aliases={3: 0},
+        compiler_params=params,
+        name="last",
+    )(third_far, one["base"], one["products"], one["next_split"])
     grams = lax.all_to_all(grams, "gz", 0, 0)
     basis_two, turned = pl.pallas_call(
         back_kernel,
@@ -732,7 +759,7 @@
         out_specs=(vmem, vmem),
         compiler_params=params,
         name="back",
-    )(shift, grams, early_split, zero["split"], one["split"], two["split"])
+    )(shift, grams, early_split, zero["split"], one["split"], last_split)
     return basis_two, jnp.swapaxes(turned, 1, 2)
 
 

time: 41.9 us -> 41.6 us (level)
  blocking collectives: 23.7 us -> 23.2 us
    pallas_call x3 -> x2, Pallas kernels: 5.23 us -> 4.43 us  [run_stage(): pl.pallas_call(functools.partial(stage_kernel, stage, depth_total, layers...]
    pallas_call x0 -> x1, Pallas kernels: none -> 0.7 us  [shards(): pl.pallas_call(functools.partial(last_kernel, float(depth_total * span)),...]
    all_to_all x1, blocking collectives: 23.7 us -> 23.2 us  [shards(): grams = lax.all_to_all(grams, 'gz', 0, 0)]
  transfers between devices with their start and end apart: 4 -> 4, of which waited for: 1 -> 1; matrix products, arithmetic and copies ran while one was open for 0% -> 0% of each run, Pallas kernels for 21% -> 22%
where the time goes in v5:
time: 41.6 us; the launch traced here: 41.3 us
  blocking collectives  23.2 us (56%)
  Pallas kernels  14.2 us (34%)
  starting transfers between devices  2.54 us (6%)
  between operations  0.75 us (2%)
  waiting for transfers between devices  0.65 us (2%)
    all_to_all x1, blocking collectives, shards(): grams = lax.all_to_all(grams, 'gz', 0, 0)  23.2 us
    pallas_call x2, Pallas kernels, run_stage(): pl.pallas_call(functools.partial(stage_kernel, stage, depth_total, layers...  4.43 us
    pallas_call x1, Pallas kernels, shards(): pl.pallas_call(functools.partial(early_kernel, depth_total), out_shape=(p...  3.09 us
    pallas_call x1, Pallas kernels, shards(): pl.pallas_call(back_kernel, out_shape=(jax.ShapeDtypeStruct(initial_guess...  2.87 us
    pallas_call x1, Pallas kernels, shards(): pl.pallas_call(functools.partial(image_kernel, depth_total), out_shape=(p...  1.78 us
    pallas_call x1, Pallas kernels, shards(): pl.pallas_call(pack_kernel, out_shape=(float_shape(fields + 2, width, lan...  1.36 us
  transfers between devices with their start and end apart: 4, of which 1 were waited for; matrix products, arithmetic and copies ran while one was open for 0% of the time, Pallas kernels for 22%

profile of v5, /device:TPU:0, one launch (start us, length us, event | category | flops | bytes accessed | tf_op | source)
XLA Modules:
  0.0 41.3 jit_solution(5196245790823790800)
XLA Ops:
  0.6 0.0 copy-start.1
  0.6 0.0 copy-start.3
  0.7 0.0 copy-start.2
  0.7 0.0 copy-start
  0.7 1.4 %pack.1 = (f32[18,32,128]{2,1,0:T(8,128)S(1)}, f32[16,32,128]{2,1,0:T(8,128)S(1)}, f32[52,32,128]{2,1,0:T(8,128)S(1)}, f32[2,4,32,128]{3,2,1,0:T(8,128)S(1)}) custom-call(f32[4,2,8,32,128]{4,3,2,1,0:T(8,128)} %guess_ref.1, s32[4,32,128]{2,1,0:T(8,128)} %class_ref.1, s32[4,32,128]{2,1,0:T(8,128)} %layer_ref.1), custom_call_target="tpu_custom_call" | custom-call | tf_op jit(solution)/shard_map/pack/pallas_call | solution.py:611
  2.0 0.5 %collective-permute-start = (f32[52,32,128]{2,1,0:T(8,128)S(1)}, f32[52,32,128]{2,1,0:T(8,128)S(1)}, u32[]{:S(2)}, u32[]{:S(2)}) collective-permute-start(f32[52,32,128]{2,1,0:T(8,128)S(1)} %get-tuple-element.28.own_ref), channel_id=1, source_target_pairs={{0,1},{2,3},{4,5},{6,7},{8,9},{10,11},{12,13},{14,15},{1,0},{3,2},... | collective-permute-start | bytes 2555912 | tf_op jit(solution)/shard_map/ppermute | solution.py:636
  2.6 0.7 %collective-permute-start.3 = (f32[18,32,128]{2,1,0:T(8,128)S(1)}, f32[18,32,128]{2,1,0:T(8,128)S(1)}, u32[]{:S(2)}, u32[]{:S(2)}) collective-permute-start(f32[18,32,128]{2,1,0:T(8,128)S(1)} %get-tuple-element.27.edge_ref), channel_id=1, source_target_pairs={{1,2},{3,4},{5,6},{7,8},{9,10},{11,12},{13,14},{2,1},{4,3},{6,5},{... | collective-permute-start | bytes 884744 | tf_op jit(solution)/shard_map/ppermute | solution.py:633
  3.2 0.7 %collective-permute-start.2 = (f32[16,32,128]{2,1,0:T(8,128)S(1)}, f32[16,32,128]{2,1,0:T(8,128)S(1)}, u32[]{:S(2)}, u32[]{:S(2)}) collective-permute-start(f32[16,32,128]{2,1,0:T(8,128)S(1)} %get-tuple-element.34), channel_id=1, source_target_pairs={{1,2},{3,4},{5,6},{7,8},{9,10},{11,12},{13,14},{2,1},{4,3},{6,5},{... | collective-permute-start | bytes 786440 | tf_op jit(solution)/shard_map/ppermute | solution.py:634
  3.9 0.6 %collective-permute-done.near_ref = f32[52,32,128]{2,1,0:T(8,128)S(1)} collective-permute-done((f32[52,32,128]{2,1,0:T(8,128)S(1)}, f32[52,32,128]{2,1,0:T(8,128)S(1)}, u32[]{:S(2)}, u32[]{:S(2)}) %collective-permute-start) | collective-permute-done | bytes 852000 | tf_op jit(solution)/shard_map/ppermute | solution.py:636
  4.6 0.0 copy-done.1
  4.6 0.0 copy-done.3
  4.6 0.0 copy-done.2
  4.6 0.0 copy-done
  4.6 3.1 %early.1 = (f32[7,32,2,8,128]{4,3,2,1,0:T(8,128)S(1)}, f32[5,32,2,8,128]{4,3,2,1,0:T(8,128)S(1)}, f32[6,4,32,128]{3,2,1,0:T(8,128)S(1)}, f32[2,16,24]{2,1,0:T(8,128)S(1)}) custom-call(f32[16]{0:T(128)S(1)} %copy-done.2, f32[8]{0:T(128)S(1)} %copy-done.3, s32[3,8]{1,0:T(4,128)S(1)} %bitcast.2, f32[2,8]{1,0:T(2,128)S(1)} %copy-done.1, ...), custom_call_target="tpu_custom_call" | custom-call | flops 10000000 | bytes 16000000 | tf_op jit(solution)/shard_map/early/pallas_call | solution.py:654
  7.7 1.8 %images.1 = (f32[3,32,2,8,128]{4,3,2,1,0:T(8,128)S(1)}, bf16[144,4096]{1,0:T(8,128)(2,1)S(1)}, f32[144,144]{1,0:T(8,128)S(1)}, f32[1,32,2,8,128]{4,3,2,1,0:T(8,128)S(1)}) custom-call(f32[5,32,2,8,128]{4,3,2,1,0:T(8,128)S(1)} %get-tuple-element.31.start.refs_7_.refs_8_, f32[6,4,32,128]{3,2,1,0:T(8,128)S(1)} %get-tuple-element.32.tables.refs_11_), custom_call_target="tpu_custom_call" | custom-call | flops 10000000 | bytes 16000000 | tf_op jit(solution)/shard_map/images/pallas_call | solution.py:663
  9.5 0.7 %collective-permute-start.1 = (f32[1,32,2,8,128]{4,3,2,1,0:T(8,128)S(1)}, f32[1,32,2,8,128]{4,3,2,1,0:T(8,128)S(1)}, u32[]{:S(2)}, u32[]{:S(2)}) collective-permute-start(f32[1,32,2,8,128]{4,3,2,1,0:T(8,128)S(1)} %get-tuple-element.33), channel_id=1, source_target_pairs={{1,2},{3,4},{5,6},{7,8},{9,10},{11,12},{13,14},{2,1},{4,3},{6,5},{... | collective-permute-start | bytes 786440 | tf_op jit(solution)/shard_map/ppermute | solution.py:673
  10.1 0.0 collective-permute-done.3.refs_4_.refs_13_
  10.1 2.0 %stage_0.1 = (f32[1,32,2,8,128]{4,3,2,1,0:T(8,128)S(1)}, f32[1,32,2,8,128]{4,3,2,1,0:T(8,128)S(1)}, f32[1,32,2,8,128]{4,3,2,1,0:T(8,128)S(1)}, bf16[144,4096]{1,0:T(8,128)(2,1)S(1)}, f32[144,144]{1,0:T(8,128)S(1)}) custom-call(f32[16]{0:T(128)S(1)} %copy-done.2, f32[8]{0:T(128)S(1)} %copy-done.3, s32[3,8]{1,0:T(4,128)S(1)} %bitcast.3, f32[2,8]{1,0:T(2,128)S(1)} %copy-done.1, ...), custom_call_target="tpu_custom_call" | custom-call | flops 10000000 | bytes 16000000 | tf_op jit(solution)/shard_map/stage_0/pallas_call | solution.py:693
  12.2 0.0 collective-permute-done.2.refs_4_
  12.2 2.4 %stage_1.1 = (f32[1,32,2,8,128]{4,3,2,1,0:T(8,128)S(1)}, bf16[144,4096]{1,0:T(8,128)(2,1)S(1)}, f32[144,144]{1,0:T(8,128)S(1)}, bf16[144,4096]{1,0:T(8,128)(2,1)S(1)}) custom-call(f32[16]{0:T(128)S(1)} %copy-done.2, f32[8]{0:T(128)S(1)} %copy-done.3, s32[3,8]{1,0:T(4,128)S(1)} %bitcast.4, f32[2,8]{1,0:T(2,128)S(1)} %copy-done.1, ...), custom_call_target="tpu_custom_call" | custom-call | flops 10000000 | bytes 16000000 | tf_op jit(solution)/shard_map/stage_1/pallas_call | solution.py:693
  14.6 0.0 collective-permute-done.1.far_ref
  14.6 0.7 %last.1 = (bf16[144,4096]{1,0:T(8,128)(2,1)S(1)}, f32[16,8,128]{2,1,0:T(8,128)S(1)}) custom-call(f32[1,32,2,8,128]{4,3,2,1,0:T(8,128)S(1)} %collective-permute-done.1.far_ref, f32[1,32,2,8,128]{4,3,2,1,0:T(8,128)S(1)} %get-tuple-element.42.base_ref, f32[144,144]{1,0:T(8,128)S(1)} %get-tuple-element.43.products_ref, ...), custom_call_target="tpu_custom_call", output_to_operand_aliasing={{0}: (3, {})} | custom-call | tf_op jit(solution)/shard_map/last/pallas_call | solution.py:742
  15.3 23.2 %all_to_all.5.grams_ref = f32[16,8,128]{2,1,0:T(8,128)S(1)} all-to-all(f32[16,8,128]{2,1,0:T(8,128)S(1)} %get-tuple-element.45), channel_id=1, replica_groups=mesh['freq'=2,'gz'=16] {'gz'}, dimensions={0} | all-to-all | bytes 131072 | tf_op jit(solution)/shard_map/all_to_all | solution.py:751
  38.5 2.9 %back.1 = (f32[4,2,8,32,128]{4,3,2,1,0:T(8,128)}, f32[2,16,24]{2,1,0:T(8,128)}) custom-call(f32[2,16,24]{2,1,0:T(8,128)S(1)} %get-tuple-element.30.shift_ref, f32[16,8,128]{2,1,0:T(8,128)S(1)} %all_to_all.5.grams_ref, bf16[144,4096]{1,0:T(8,128)(2,1)S(1)} %get-tuple-element.46.rest_0_, bf16[144,4096]{1,0:T(8,128)(2,1)S(1)} %get-tuple-element.47.rest_1_, ...), custom_call_target="tpu_custom_call" | custom-call | tf_op jit(solution)/shard_map/back/pallas_call | solution.py:752
Async XLA Ops:
  0.6 3.9 %copy-start.1 = (f32[2,8]{1,0:T(2,128)S(1)}, f32[2,8]{1,0:T(2,128)}, u32[]{:S(2)}) copy-start(f32[2,8]{1,0:T(2,128)} %refs_3_.3) | copy-start | bytes 196
  0.6 3.9 %copy-start.3 = (f32[8]{0:T(128)S(1)}, f32[8]{0:T(128)}, u32[]{:S(2)}) copy-start(f32[8]{0:T(128)} %refs_1_.3) | copy-start | bytes 100
  0.7 3.9 %copy-start.2 = (f32[16]{0:T(128)S(1)}, f32[16]{0:T(128)}, u32[]{:S(2)}) copy-start(f32[16]{0:T(128)} %refs_0_.3) | copy-start | bytes 196
  0.7 3.9 %copy-start = (s32[8,3]{0,1:T(4,128)S(1)}, s32[8,3]{0,1:T(4,128)}, u32[]{:S(2)}) copy-start(s32[8,3]{0,1:T(4,128)} %param.12) | copy-start | bytes 292
  2.0 2.5 %collective-permute-start = (f32[52,32,128]{2,1,0:T(8,128)S(1)}, f32[52,32,128]{2,1,0:T(8,128)S(1)}, u32[]{:S(2)}, u32[]{:S(2)}) collective-permute-start(f32[52,32,128]{2,1,0:T(8,128)S(1)} %get-tuple-element.28.own_ref), channel_id=1, source_target_pairs={{0,1},{2,3},{4,5},{6,7},{8,9},{10,11},{12,13},{14,15},{1,0},{3,2},... | collective-permute-start | bytes 2555912 | tf_op jit(solution)/shard_map/ppermute | solution.py:636
  2.6 7.6 %collective-permute-start.3 = (f32[18,32,128]{2,1,0:T(8,128)S(1)}, f32[18,32,128]{2,1,0:T(8,128)S(1)}, u32[]{:S(2)}, u32[]{:S(2)}) collective-permute-start(f32[18,32,128]{2,1,0:T(8,128)S(1)} %get-tuple-element.27.edge_ref), channel_id=1, source_target_pairs={{1,2},{3,4},{5,6},{7,8},{9,10},{11,12},{13,14},{2,1},{4,3},{6,5},{... | collective-permute-start | bytes 884744 | tf_op jit(solution)/shard_map/ppermute | solution.py:633
  3.2 9.0 %collective-permute-start.2 = (f32[16,32,128]{2,1,0:T(8,128)S(1)}, f32[16,32,128]{2,1,0:T(8,128)S(1)}, u32[]{:S(2)}, u32[]{:S(2)}) collective-permute-start(f32[16,32,128]{2,1,0:T(8,128)S(1)} %get-tuple-element.34), channel_id=1, source_target_pairs={{1,2},{3,4},{5,6},{7,8},{9,10},{11,12},{13,14},{2,1},{4,3},{6,5},{... | collective-permute-start | bytes 786440 | tf_op jit(solution)/shard_map/ppermute | solution.py:634
  9.5 5.1 %collective-permute-start.1 = (f32[1,32,2,8,128]{4,3,2,1,0:T(8,128)S(1)}, f32[1,32,2,8,128]{4,3,2,1,0:T(8,128)S(1)}, u32[]{:S(2)}, u32[]{:S(2)}) collective-permute-start(f32[1,32,2,8,128]{4,3,2,1,0:T(8,128)S(1)} %get-tuple-element.33), channel_id=1, source_target_pairs={{1,2},{3,4},{5,6},{7,8},{9,10},{11,12},{13,14},{2,1},{4,3},{6,5},{... | collective-permute-start | bytes 786440 | tf_op jit(solution)/shard_map/ppermute | solution.py:673

commit v6 on v5

--- a/solution.py
+++ b/solution.py
@@ -7,7 +7,7 @@
 from jax.experimental.pallas import tpu as pltpu
 from jax.sharding import PartitionSpec as P
 
-SHIFT_BASE = 2.9
+SHIFT_BASE = 1.5
 BLOCKS = 3
 REACH = 3
 VMEM_BYTES = 24 * 1024 * 1024

time: 41.6 us -> 41.6 us (level)
  no operation moved by 1% of the time
where the time goes in v6:
time: 41.6 us; the launch traced here: 41.3 us
  blocking collectives  23.2 us (56%)
  Pallas kernels  14.2 us (34%)
  starting transfers between devices  2.54 us (6%)
  between operations  0.75 us (2%)
  waiting for transfers between devices  0.65 us (2%)
    all_to_all x1, blocking collectives, shards(): grams = lax.all_to_all(grams, 'gz', 0, 0)  23.2 us
    pallas_call x2, Pallas kernels, run_stage(): pl.pallas_call(functools.partial(stage_kernel, stage, depth_total, layers...  4.43 us
    pallas_call x1, Pallas kernels, shards(): pl.pallas_call(functools.partial(early_kernel, depth_total), out_shape=(p...  3.08 us
    pallas_call x1, Pallas kernels, shards(): pl.pallas_call(back_kernel, out_shape=(jax.ShapeDtypeStruct(initial_guess...  2.87 us
    pallas_call x1, Pallas kernels, shards(): pl.pallas_call(functools.partial(image_kernel, depth_total), out_shape=(p...  1.78 us
    pallas_call x1, Pallas kernels, shards(): pl.pallas_call(pack_kernel, out_shape=(float_shape(fields + 2, width, lan...  1.36 us
  transfers between devices with their start and end apart: 4, of which 1 were waited for; matrix products, arithmetic and copies ran while one was open for 0% of the time, Pallas kernels for 22%

profile of v6, /device:TPU:0, one launch (start us, length us, event | category | flops | bytes accessed | tf_op | source)
XLA Modules:
  0.0 41.3 jit_solution(14480659830717955536)
XLA Ops:
  0.6 0.0 copy-start.1
  0.6 0.0 copy-start.3
  0.7 0.0 copy-start.2
  0.7 0.0 copy-start
  0.7 1.4 %pack.1 = (f32[18,32,128]{2,1,0:T(8,128)S(1)}, f32[16,32,128]{2,1,0:T(8,128)S(1)}, f32[52,32,128]{2,1,0:T(8,128)S(1)}, f32[2,4,32,128]{3,2,1,0:T(8,128)S(1)}) custom-call(f32[4,2,8,32,128]{4,3,2,1,0:T(8,128)} %guess_ref.1, s32[4,32,128]{2,1,0:T(8,128)} %class_ref.1, s32[4,32,128]{2,1,0:T(8,128)} %layer_ref.1), custom_call_target="tpu_custom_call" | custom-call | tf_op jit(solution)/shard_map/pack/pallas_call | solution.py:611
  2.0 0.5 %collective-permute-start = (f32[52,32,128]{2,1,0:T(8,128)S(1)}, f32[52,32,128]{2,1,0:T(8,128)S(1)}, u32[]{:S(2)}, u32[]{:S(2)}) collective-permute-start(f32[52,32,128]{2,1,0:T(8,128)S(1)} %get-tuple-element.28.own_ref), channel_id=1, source_target_pairs={{0,1},{2,3},{4,5},{6,7},{8,9},{10,11},{12,13},{14,15},{1,0},{3,2},... | collective-permute-start | bytes 2555912 | tf_op jit(solution)/shard_map/ppermute | solution.py:636
  2.6 0.7 %collective-permute-start.3 = (f32[18,32,128]{2,1,0:T(8,128)S(1)}, f32[18,32,128]{2,1,0:T(8,128)S(1)}, u32[]{:S(2)}, u32[]{:S(2)}) collective-permute-start(f32[18,32,128]{2,1,0:T(8,128)S(1)} %get-tuple-element.27.edge_ref), channel_id=1, source_target_pairs={{1,2},{3,4},{5,6},{7,8},{9,10},{11,12},{13,14},{2,1},{4,3},{6,5},{... | collective-permute-start | bytes 884744 | tf_op jit(solution)/shard_map/ppermute | solution.py:633
  3.2 0.7 %collective-permute-start.2 = (f32[16,32,128]{2,1,0:T(8,128)S(1)}, f32[16,32,128]{2,1,0:T(8,128)S(1)}, u32[]{:S(2)}, u32[]{:S(2)}) collective-permute-start(f32[16,32,128]{2,1,0:T(8,128)S(1)} %get-tuple-element.34), channel_id=1, source_target_pairs={{1,2},{3,4},{5,6},{7,8},{9,10},{11,12},{13,14},{2,1},{4,3},{6,5},{... | collective-permute-start | bytes 786440 | tf_op jit(solution)/shard_map/ppermute | solution.py:634
  3.9 0.6 %collective-permute-done.near_ref = f32[52,32,128]{2,1,0:T(8,128)S(1)} collective-permute-done((f32[52,32,128]{2,1,0:T(8,128)S(1)}, f32[52,32,128]{2,1,0:T(8,128)S(1)}, u32[]{:S(2)}, u32[]{:S(2)}) %collective-permute-start) | collective-permute-done | bytes 852000 | tf_op jit(solution)/shard_map/ppermute | solution.py:636
  4.6 0.0 copy-done.1
  4.6 0.0 copy-done.3
  4.6 0.0 copy-done.2
  4.6 0.0 copy-done
  4.6 3.1 %early.1 = (f32[7,32,2,8,128]{4,3,2,1,0:T(8,128)S(1)}, f32[5,32,2,8,128]{4,3,2,1,0:T(8,128)S(1)}, f32[6,4,32,128]{3,2,1,0:T(8,128)S(1)}, f32[2,16,24]{2,1,0:T(8,128)S(1)}) custom-call(f32[16]{0:T(128)S(1)} %copy-done.2, f32[8]{0:T(128)S(1)} %copy-done.3, s32[3,8]{1,0:T(4,128)S(1)} %bitcast.2, f32[2,8]{1,0:T(2,128)S(1)} %copy-done.1, ...), custom_call_target="tpu_custom_call" | custom-call | flops 10000000 | bytes 16000000 | tf_op jit(solution)/shard_map/early/pallas_call | solution.py:654
  7.7 1.8 %images.1 = (f32[3,32,2,8,128]{4,3,2,1,0:T(8,128)S(1)}, bf16[144,4096]{1,0:T(8,128)(2,1)S(1)}, f32[144,144]{1,0:T(8,128)S(1)}, f32[1,32,2,8,128]{4,3,2,1,0:T(8,128)S(1)}) custom-call(f32[5,32,2,8,128]{4,3,2,1,0:T(8,128)S(1)} %get-tuple-element.31.start.refs_7_.refs_8_, f32[6,4,32,128]{3,2,1,0:T(8,128)S(1)} %get-tuple-element.32.tables.refs_11_), custom_call_target="tpu_custom_call" | custom-call | flops 10000000 | bytes 16000000 | tf_op jit(solution)/shard_map/images/pallas_call | solution.py:663
  9.4 0.7 %collective-permute-start.1 = (f32[1,32,2,8,128]{4,3,2,1,0:T(8,128)S(1)}, f32[1,32,2,8,128]{4,3,2,1,0:T(8,128)S(1)}, u32[]{:S(2)}, u32[]{:S(2)}) collective-permute-start(f32[1,32,2,8,128]{4,3,2,1,0:T(8,128)S(1)} %get-tuple-element.33), channel_id=1, source_target_pairs={{1,2},{3,4},{5,6},{7,8},{9,10},{11,12},{13,14},{2,1},{4,3},{6,5},{... | collective-permute-start | bytes 786440 | tf_op jit(solution)/shard_map/ppermute | solution.py:673
  10.1 0.0 collective-permute-done.3.refs_4_.refs_13_
  10.1 2.0 %stage_0.1 = (f32[1,32,2,8,128]{4,3,2,1,0:T(8,128)S(1)}, f32[1,32,2,8,128]{4,3,2,1,0:T(8,128)S(1)}, f32[1,32,2,8,128]{4,3,2,1,0:T(8,128)S(1)}, bf16[144,4096]{1,0:T(8,128)(2,1)S(1)}, f32[144,144]{1,0:T(8,128)S(1)}) custom-call(f32[16]{0:T(128)S(1)} %copy-done.2, f32[8]{0:T(128)S(1)} %copy-done.3, s32[3,8]{1,0:T(4,128)S(1)} %bitcast.3, f32[2,8]{1,0:T(2,128)S(1)} %copy-done.1, ...), custom_call_target="tpu_custom_call" | custom-call | flops 10000000 | bytes 16000000 | tf_op jit(solution)/shard_map/stage_0/pallas_call | solution.py:693
  12.2 0.0 collective-permute-done.2.refs_4_
  12.2 2.4 %stage_1.1 = (f32[1,32,2,8,128]{4,3,2,1,0:T(8,128)S(1)}, bf16[144,4096]{1,0:T(8,128)(2,1)S(1)}, f32[144,144]{1,0:T(8,128)S(1)}, bf16[144,4096]{1,0:T(8,128)(2,1)S(1)}) custom-call(f32[16]{0:T(128)S(1)} %copy-done.2, f32[8]{0:T(128)S(1)} %copy-done.3, s32[3,8]{1,0:T(4,128)S(1)} %bitcast.4, f32[2,8]{1,0:T(2,128)S(1)} %copy-done.1, ...), custom_call_target="tpu_custom_call" | custom-call | flops 10000000 | bytes 16000000 | tf_op jit(solution)/shard_map/stage_1/pallas_call | solution.py:693
  14.6 0.0 collective-permute-done.1.far_ref
  14.6 0.7 %last.1 = (bf16[144,4096]{1,0:T(8,128)(2,1)S(1)}, f32[16,8,128]{2,1,0:T(8,128)S(1)}) custom-call(f32[1,32,2,8,128]{4,3,2,1,0:T(8,128)S(1)} %collective-permute-done.1.far_ref, f32[1,32,2,8,128]{4,3,2,1,0:T(8,128)S(1)} %get-tuple-element.42.base_ref, f32[144,144]{1,0:T(8,128)S(1)} %get-tuple-element.43.products_ref, ...), custom_call_target="tpu_custom_call", output_to_operand_aliasing={{0}: (3, {})} | custom-call | tf_op jit(solution)/shard_map/last/pallas_call | solution.py:742
  15.3 23.2 %all_to_all.5.grams_ref = f32[16,8,128]{2,1,0:T(8,128)S(1)} all-to-all(f32[16,8,128]{2,1,0:T(8,128)S(1)} %get-tuple-element.45), channel_id=1, replica_groups=mesh['freq'=2,'gz'=16] {'gz'}, dimensions={0} | all-to-all | bytes 131072 | tf_op jit(solution)/shard_map/all_to_all | solution.py:751
  38.5 2.9 %back.1 = (f32[4,2,8,32,128]{4,3,2,1,0:T(8,128)}, f32[2,16,24]{2,1,0:T(8,128)}) custom-call(f32[2,16,24]{2,1,0:T(8,128)S(1)} %get-tuple-element.30.shift_ref, f32[16,8,128]{2,1,0:T(8,128)S(1)} %all_to_all.5.grams_ref, bf16[144,4096]{1,0:T(8,128)(2,1)S(1)} %get-tuple-element.46.rest_0_, bf16[144,4096]{1,0:T(8,128)(2,1)S(1)} %get-tuple-element.47.rest_1_, ...), custom_call_target="tpu_custom_call" | custom-call | tf_op jit(solution)/shard_map/back/pallas_call | solution.py:752
Async XLA Ops:
  0.6 3.9 %copy-start.1 = (f32[2,8]{1,0:T(2,128)S(1)}, f32[2,8]{1,0:T(2,128)}, u32[]{:S(2)}) copy-start(f32[2,8]{1,0:T(2,128)} %refs_3_.3) | copy-start | bytes 196
  0.6 3.9 %copy-start.3 = (f32[8]{0:T(128)S(1)}, f32[8]{0:T(128)}, u32[]{:S(2)}) copy-start(f32[8]{0:T(128)} %refs_1_.3) | copy-start | bytes 100
  0.7 3.9 %copy-start.2 = (f32[16]{0:T(128)S(1)}, f32[16]{0:T(128)}, u32[]{:S(2)}) copy-start(f32[16]{0:T(128)} %refs_0_.3) | copy-start | bytes 196
  0.7 3.9 %copy-start = (s32[8,3]{0,1:T(4,128)S(1)}, s32[8,3]{0,1:T(4,128)}, u32[]{:S(2)}) copy-start(s32[8,3]{0,1:T(4,128)} %param.12) | copy-start | bytes 292
  2.0 2.5 %collective-permute-start = (f32[52,32,128]{2,1,0:T(8,128)S(1)}, f32[52,32,128]{2,1,0:T(8,128)S(1)}, u32[]{:S(2)}, u32[]{:S(2)}) collective-permute-start(f32[52,32,128]{2,1,0:T(8,128)S(1)} %get-tuple-element.28.own_ref), channel_id=1, source_target_pairs={{0,1},{2,3},{4,5},{6,7},{8,9},{10,11},{12,13},{14,15},{1,0},{3,2},... | collective-permute-start | bytes 2555912 | tf_op jit(solution)/shard_map/ppermute | solution.py:636
  2.6 7.6 %collective-permute-start.3 = (f32[18,32,128]{2,1,0:T(8,128)S(1)}, f32[18,32,128]{2,1,0:T(8,128)S(1)}, u32[]{:S(2)}, u32[]{:S(2)}) collective-permute-start(f32[18,32,128]{2,1,0:T(8,128)S(1)} %get-tuple-element.27.edge_ref), channel_id=1, source_target_pairs={{1,2},{3,4},{5,6},{7,8},{9,10},{11,12},{13,14},{2,1},{4,3},{6,5},{... | collective-permute-start | bytes 884744 | tf_op jit(solution)/shard_map/ppermute | solution.py:633
  3.2 9.0 %collective-permute-start.2 = (f32[16,32,128]{2,1,0:T(8,128)S(1)}, f32[16,32,128]{2,1,0:T(8,128)S(1)}, u32[]{:S(2)}, u32[]{:S(2)}) collective-permute-start(f32[16,32,128]{2,1,0:T(8,128)S(1)} %get-tuple-element.34), channel_id=1, source_target_pairs={{1,2},{3,4},{5,6},{7,8},{9,10},{11,12},{13,14},{2,1},{4,3},{6,5},{... | collective-permute-start | bytes 786440 | tf_op jit(solution)/shard_map/ppermute | solution.py:634
  9.4 5.1 %collective-permute-start.1 = (f32[1,32,2,8,128]{4,3,2,1,0:T(8,128)S(1)}, f32[1,32,2,8,128]{4,3,2,1,0:T(8,128)S(1)}, u32[]{:S(2)}, u32[]{:S(2)}) collective-permute-start(f32[1,32,2,8,128]{4,3,2,1,0:T(8,128)S(1)} %get-tuple-element.33), channel_id=1, source_target_pairs={{1,2},{3,4},{5,6},{7,8},{9,10},{11,12},{13,14},{2,1},{4,3},{6,5},{... | collective-permute-start | bytes 786440 | tf_op jit(solution)/shard_map/ppermute | solution.py:673

commit v7 on v6

--- a/solution.py
+++ b/solution.py
@@ -529,7 +529,6 @@
     left = jnp.concatenate(pieces, axis=0)[:, 0:spread]
 
     odd = lax.rem(lax.axis_index("gz"), 2) == 1
-    out_rows = basis_ref.reshape(layers * fields * width, y)
     spots = [
         (ref, spot)
         for ref in rest[:-2]
@@ -545,10 +544,9 @@
                 left, source[:, offset : offset + group * y], preferred_element_type=jnp.float32
             )
             mixed = mixed[0:fields] + mixed[fields : 2 * fields] + mixed[2 * fields : 3 * fields]
-            for column in range(group):
-                out_rows[pl.ds(plane * (fields * width) + begin + column, fields, stride=width), :] = mixed[
-                    :, column * y : (column + 1) * y
-                ]
+            turned = mixed.reshape(fields, group, y)
+            for part in range(parts):
+                basis_ref[plane, part, :, begin : begin + group] = turned[part * shots : (part + 1) * shots]
 
     wide = 2 * tile
     full_real = jnp.concatenate(real, axis=0)

time: 41.6 us -> 41.4 us (level)
  transfers between devices with their start and end apart: 4 -> 4, of which waited for: 1 -> 1; matrix products, arithmetic and copies ran while one was open for 0% -> 0% of each run, Pallas kernels for 22% -> 23%
where the time goes in v7:
time: 41.4 us; the launch traced here: 41.2 us
  blocking collectives  23.2 us (56%)
  Pallas kernels  14.1 us (34%)
  starting transfers between devices  2.54 us (6%)
  between operations  0.75 us (2%)
  waiting for transfers between devices  0.65 us (2%)
    all_to_all x1, blocking collectives, shards(): grams = lax.all_to_all(grams, 'gz', 0, 0)  23.2 us
    pallas_call x2, Pallas kernels, run_stage(): pl.pallas_call(functools.partial(stage_kernel, stage, depth_total, layers...  4.43 us
    pallas_call x1, Pallas kernels, shards(): pl.pallas_call(functools.partial(early_kernel, depth_total), out_shape=(p...  3.08 us
    pallas_call x1, Pallas kernels, shards(): pl.pallas_call(back_kernel, out_shape=(jax.ShapeDtypeStruct(initial_guess...  2.74 us
    pallas_call x1, Pallas kernels, shards(): pl.pallas_call(functools.partial(image_kernel, depth_total), out_shape=(p...  1.78 us
    pallas_call x1, Pallas kernels, shards(): pl.pallas_call(pack_kernel, out_shape=(float_shape(fields + 2, width, lan...  1.36 us
  transfers between devices with their start and end apart: 4, of which 1 were waited for; matrix products, arithmetic and copies ran while one was open for 0% of the time, Pallas kernels for 23%

profile of v7, /device:TPU:0, one launch (start us, length us, event | category | flops | bytes accessed | tf_op | source)
XLA Modules:
  0.0 41.2 jit_solution(14336801001004673832)
XLA Ops:
  0.6 0.0 copy-start.1
  0.6 0.0 copy-start.3
  0.7 0.0 copy-start.2
  0.7 0.0 copy-start
  0.7 1.4 %pack.1 = (f32[18,32,128]{2,1,0:T(8,128)S(1)}, f32[16,32,128]{2,1,0:T(8,128)S(1)}, f32[52,32,128]{2,1,0:T(8,128)S(1)}, f32[2,4,32,128]{3,2,1,0:T(8,128)S(1)}) custom-call(f32[4,2,8,32,128]{4,3,2,1,0:T(8,128)} %guess_ref.1, s32[4,32,128]{2,1,0:T(8,128)} %class_ref.1, s32[4,32,128]{2,1,0:T(8,128)} %layer_ref.1), custom_call_target="tpu_custom_call" | custom-call | tf_op jit(solution)/shard_map/pack/pallas_call | solution.py:609
  2.0 0.5 %collective-permute-start = (f32[52,32,128]{2,1,0:T(8,128)S(1)}, f32[52,32,128]{2,1,0:T(8,128)S(1)}, u32[]{:S(2)}, u32[]{:S(2)}) collective-permute-start(f32[52,32,128]{2,1,0:T(8,128)S(1)} %get-tuple-element.28.own_ref), channel_id=1, source_target_pairs={{0,1},{2,3},{4,5},{6,7},{8,9},{10,11},{12,13},{14,15},{1,0},{3,2},... | collective-permute-start | bytes 2555912 | tf_op jit(solution)/shard_map/ppermute | solution.py:634
  2.6 0.7 %collective-permute-start.3 = (f32[18,32,128]{2,1,0:T(8,128)S(1)}, f32[18,32,128]{2,1,0:T(8,128)S(1)}, u32[]{:S(2)}, u32[]{:S(2)}) collective-permute-start(f32[18,32,128]{2,1,0:T(8,128)S(1)} %get-tuple-element.27.edge_ref), channel_id=1, source_target_pairs={{1,2},{3,4},{5,6},{7,8},{9,10},{11,12},{13,14},{2,1},{4,3},{6,5},{... | collective-permute-start | bytes 884744 | tf_op jit(solution)/shard_map/ppermute | solution.py:631
  3.2 0.7 %collective-permute-start.2 = (f32[16,32,128]{2,1,0:T(8,128)S(1)}, f32[16,32,128]{2,1,0:T(8,128)S(1)}, u32[]{:S(2)}, u32[]{:S(2)}) collective-permute-start(f32[16,32,128]{2,1,0:T(8,128)S(1)} %get-tuple-element.34), channel_id=1, source_target_pairs={{1,2},{3,4},{5,6},{7,8},{9,10},{11,12},{13,14},{2,1},{4,3},{6,5},{... | collective-permute-start | bytes 786440 | tf_op jit(solution)/shard_map/ppermute | solution.py:632
  3.9 0.6 %collective-permute-done.near_ref = f32[52,32,128]{2,1,0:T(8,128)S(1)} collective-permute-done((f32[52,32,128]{2,1,0:T(8,128)S(1)}, f32[52,32,128]{2,1,0:T(8,128)S(1)}, u32[]{:S(2)}, u32[]{:S(2)}) %collective-permute-start) | collective-permute-done | bytes 852000 | tf_op jit(solution)/shard_map/ppermute | solution.py:634
  4.6 0.0 copy-done.1
  4.6 0.0 copy-done.3
  4.6 0.0 copy-done.2
  4.6 0.0 copy-done
  4.6 3.1 %early.1 = (f32[7,32,2,8,128]{4,3,2,1,0:T(8,128)S(1)}, f32[5,32,2,8,128]{4,3,2,1,0:T(8,128)S(1)}, f32[6,4,32,128]{3,2,1,0:T(8,128)S(1)}, f32[2,16,24]{2,1,0:T(8,128)S(1)}) custom-call(f32[16]{0:T(128)S(1)} %copy-done.2, f32[8]{0:T(128)S(1)} %copy-done.3, s32[3,8]{1,0:T(4,128)S(1)} %bitcast.2, f32[2,8]{1,0:T(2,128)S(1)} %copy-done.1, ...), custom_call_target="tpu_custom_call" | custom-call | flops 10000000 | bytes 16000000 | tf_op jit(solution)/shard_map/early/pallas_call | solution.py:652
  7.7 1.8 %images.1 = (f32[3,32,2,8,128]{4,3,2,1,0:T(8,128)S(1)}, bf16[144,4096]{1,0:T(8,128)(2,1)S(1)}, f32[144,144]{1,0:T(8,128)S(1)}, f32[1,32,2,8,128]{4,3,2,1,0:T(8,128)S(1)}) custom-call(f32[5,32,2,8,128]{4,3,2,1,0:T(8,128)S(1)} %get-tuple-element.31.start.refs_7_.refs_8_, f32[6,4,32,128]{3,2,1,0:T(8,128)S(1)} %get-tuple-element.32.tables.refs_11_), custom_call_target="tpu_custom_call" | custom-call | flops 10000000 | bytes 16000000 | tf_op jit(solution)/shard_map/images/pallas_call | solution.py:661
  9.4 0.7 %collective-permute-start.1 = (f32[1,32,2,8,128]{4,3,2,1,0:T(8,128)S(1)}, f32[1,32,2,8,128]{4,3,2,1,0:T(8,128)S(1)}, u32[]{:S(2)}, u32[]{:S(2)}) collective-permute-start(f32[1,32,2,8,128]{4,3,2,1,0:T(8,128)S(1)} %get-tuple-element.33), channel_id=1, source_target_pairs={{1,2},{3,4},{5,6},{7,8},{9,10},{11,12},{13,14},{2,1},{4,3},{6,5},{... | collective-permute-start | bytes 786440 | tf_op jit(solution)/shard_map/ppermute | solution.py:671
  10.1 0.0 collective-permute-done.3.refs_4_.refs_13_
  10.1 2.0 %stage_0.1 = (f32[1,32,2,8,128]{4,3,2,1,0:T(8,128)S(1)}, f32[1,32,2,8,128]{4,3,2,1,0:T(8,128)S(1)}, f32[1,32,2,8,128]{4,3,2,1,0:T(8,128)S(1)}, bf16[144,4096]{1,0:T(8,128)(2,1)S(1)}, f32[144,144]{1,0:T(8,128)S(1)}) custom-call(f32[16]{0:T(128)S(1)} %copy-done.2, f32[8]{0:T(128)S(1)} %copy-done.3, s32[3,8]{1,0:T(4,128)S(1)} %bitcast.3, f32[2,8]{1,0:T(2,128)S(1)} %copy-done.1, ...), custom_call_target="tpu_custom_call" | custom-call | flops 10000000 | bytes 16000000 | tf_op jit(solution)/shard_map/stage_0/pallas_call | solution.py:691
  12.2 0.0 collective-permute-done.2.refs_4_
  12.2 2.4 %stage_1.1 = (f32[1,32,2,8,128]{4,3,2,1,0:T(8,128)S(1)}, bf16[144,4096]{1,0:T(8,128)(2,1)S(1)}, f32[144,144]{1,0:T(8,128)S(1)}, bf16[144,4096]{1,0:T(8,128)(2,1)S(1)}) custom-call(f32[16]{0:T(128)S(1)} %copy-done.2, f32[8]{0:T(128)S(1)} %copy-done.3, s32[3,8]{1,0:T(4,128)S(1)} %bitcast.4, f32[2,8]{1,0:T(2,128)S(1)} %copy-done.1, ...), custom_call_target="tpu_custom_call" | custom-call | flops 10000000 | bytes 16000000 | tf_op jit(solution)/shard_map/stage_1/pallas_call | solution.py:691
  14.6 0.0 collective-permute-done.1.far_ref
  14.6 0.7 %last.1 = (bf16[144,4096]{1,0:T(8,128)(2,1)S(1)}, f32[16,8,128]{2,1,0:T(8,128)S(1)}) custom-call(f32[1,32,2,8,128]{4,3,2,1,0:T(8,128)S(1)} %collective-permute-done.1.far_ref, f32[1,32,2,8,128]{4,3,2,1,0:T(8,128)S(1)} %get-tuple-element.42.base_ref, f32[144,144]{1,0:T(8,128)S(1)} %get-tuple-element.43.products_ref, ...), custom_call_target="tpu_custom_call", output_to_operand_aliasing={{0}: (3, {})} | custom-call | tf_op jit(solution)/shard_map/last/pallas_call | solution.py:740
  15.3 23.2 %all_to_all.5.grams_ref = f32[16,8,128]{2,1,0:T(8,128)S(1)} all-to-all(f32[16,8,128]{2,1,0:T(8,128)S(1)} %get-tuple-element.45), channel_id=1, replica_groups=mesh['freq'=2,'gz'=16] {'gz'}, dimensions={0} | all-to-all | bytes 131072 | tf_op jit(solution)/shard_map/all_to_all | solution.py:749
  38.5 2.7 %back.1 = (f32[4,2,8,32,128]{4,3,2,1,0:T(8,128)}, f32[2,16,24]{2,1,0:T(8,128)}) custom-call(f32[2,16,24]{2,1,0:T(8,128)S(1)} %get-tuple-element.30.shift_ref, f32[16,8,128]{2,1,0:T(8,128)S(1)} %all_to_all.5.grams_ref, bf16[144,4096]{1,0:T(8,128)(2,1)S(1)} %get-tuple-element.46.rest_0_, bf16[144,4096]{1,0:T(8,128)(2,1)S(1)} %get-tuple-element.47.rest_1_, ...), custom_call_target="tpu_custom_call" | custom-call | tf_op jit(solution)/shard_map/back/pallas_call | solution.py:750
Async XLA Ops:
  0.6 3.9 %copy-start.1 = (f32[2,8]{1,0:T(2,128)S(1)}, f32[2,8]{1,0:T(2,128)}, u32[]{:S(2)}) copy-start(f32[2,8]{1,0:T(2,128)} %refs_3_.3) | copy-start | bytes 196
  0.6 3.9 %copy-start.3 = (f32[8]{0:T(128)S(1)}, f32[8]{0:T(128)}, u32[]{:S(2)}) copy-start(f32[8]{0:T(128)} %refs_1_.3) | copy-start | bytes 100
  0.7 3.9 %copy-start.2 = (f32[16]{0:T(128)S(1)}, f32[16]{0:T(128)}, u32[]{:S(2)}) copy-start(f32[16]{0:T(128)} %refs_0_.3) | copy-start | bytes 196
  0.7 3.9 %copy-start = (s32[8,3]{0,1:T(4,128)S(1)}, s32[8,3]{0,1:T(4,128)}, u32[]{:S(2)}) copy-start(s32[8,3]{0,1:T(4,128)} %param.12) | copy-start | bytes 292
  2.0 2.5 %collective-permute-start = (f32[52,32,128]{2,1,0:T(8,128)S(1)}, f32[52,32,128]{2,1,0:T(8,128)S(1)}, u32[]{:S(2)}, u32[]{:S(2)}) collective-permute-start(f32[52,32,128]{2,1,0:T(8,128)S(1)} %get-tuple-element.28.own_ref), channel_id=1, source_target_pairs={{0,1},{2,3},{4,5},{6,7},{8,9},{10,11},{12,13},{14,15},{1,0},{3,2},... | collective-permute-start | bytes 2555912 | tf_op jit(solution)/shard_map/ppermute | solution.py:634
  2.6 7.6 %collective-permute-start.3 = (f32[18,32,128]{2,1,0:T(8,128)S(1)}, f32[18,32,128]{2,1,0:T(8,128)S(1)}, u32[]{:S(2)}, u32[]{:S(2)}) collective-permute-start(f32[18,32,128]{2,1,0:T(8,128)S(1)} %get-tuple-element.27.edge_ref), channel_id=1, source_target_pairs={{1,2},{3,4},{5,6},{7,8},{9,10},{11,12},{13,14},{2,1},{4,3},{6,5},{... | collective-permute-start | bytes 884744 | tf_op jit(solution)/shard_map/ppermute | solution.py:631
  3.2 9.0 %collective-permute-start.2 = (f32[16,32,128]{2,1,0:T(8,128)S(1)}, f32[16,32,128]{2,1,0:T(8,128)S(1)}, u32[]{:S(2)}, u32[]{:S(2)}) collective-permute-start(f32[16,32,128]{2,1,0:T(8,128)S(1)} %get-tuple-element.34), channel_id=1, source_target_pairs={{1,2},{3,4},{5,6},{7,8},{9,10},{11,12},{13,14},{2,1},{4,3},{6,5},{... | collective-permute-start | bytes 786440 | tf_op jit(solution)/shard_map/ppermute | solution.py:632
  9.4 5.1 %collective-permute-start.1 = (f32[1,32,2,8,128]{4,3,2,1,0:T(8,128)S(1)}, f32[1,32,2,8,128]{4,3,2,1,0:T(8,128)S(1)}, u32[]{:S(2)}, u32[]{:S(2)}) collective-permute-start(f32[1,32,2,8,128]{4,3,2,1,0:T(8,128)S(1)} %get-tuple-element.33), channel_id=1, source_target_pairs={{1,2},{3,4},{5,6},{7,8},{9,10},{11,12},{13,14},{2,1},{4,3},{6,5},{... | collective-permute-start | bytes 786440 | tf_op jit(solution)/shard_map/ppermute | solution.py:671
